TPU v7x, 512 devices: a whole 4x8x8 slice. The times are simulated.
512 devices in a mesh: shard: 32 (over z, x), group: 16 (over y, core).
Axes of the slice: x: 4, y: 8, z: 8, core: 2. Of those that a mesh axis runs over, the one named last changes fastest.
Arguments:
- embeddings: bfloat16 [262144, 1024], P(('shard', 'group')), may hold values from -0.1875 to 0.1875
- cluster_key: int32 [262144, 1], P(('shard', 'group')), may hold values from 0 to 511; in each aligned block of 512 rows (0 to 511, 512 to 1023, ...) at most 2 rows name the same one
- child_first: int32 [262144], P(('shard', 'group')), may hold values from 0 to 511
- child_second: int32 [262144], P(('shard', 'group')), may hold values from 0 to 511
- coarse_centroids: bfloat16 [32, 512, 1024], P('shard'), may hold values from -0.1875 to 0.1875
- fine_centroids: bfloat16 [16, 512, 1024], P('group'), may hold values from -0.1875 to 0.1875
Outputs:
- coarse_new: bfloat16 [32, 512, 1024], P('shard')
- fine_new: bfloat16 [16, 512, 1024], P('group')
- coarse_cost: float32 [32, 512], P('shard')
- fine_cost: float32 [16, 512], P('group')
Inputs may be any that keep to these rules, and one draw needn't show every extreme that they name: `cluster_key`: in every aligned block of 512 documents (the documents of one device) no key appears more than 2 times.
All inputs are finite; a program needn't handle non-finite values.
Results may differ from a plain program's by a relative error of at most 0.022.
Values may be sent and summed in bfloat16 or wider, within the bound.
No kernel may reach another device: no remote copies, remote signals or barrier semaphores. Data moves between devices by JAX's collectives and lax.ppermute only.
A program may use at most 128 MiB of HBM per device.

v0:
```python
import jax
import jax.numpy as jnp
from jax import lax
from jax.sharding import PartitionSpec as P


def split_codes(codes, children):
    live = codes > 0
    first = jnp.where(live, (codes - 1) // children, -1)
    second = jnp.where(live, (codes - 1) % children, -1)
    return (live, first, second)


def level_terms(rows, assign, live, centroids):
    products = lax.dot_general(
        rows, centroids, (((1,), (1,)), ((), ())), preferred_element_type=jnp.float32
    )
    cent_f = centroids.astype(jnp.float32)
    squares = jnp.sum(cent_f * cent_f, axis=1)
    scores = squares[None, :] - 2.0 * products
    labels = lax.broadcasted_iota(jnp.int32, scores.shape, 1)
    picked = assign[:, None] == labels
    assigned = jnp.sum(jnp.where(picked, scores, 0.0), axis=1)
    margin = jnp.where(live, assigned - jnp.min(scores, axis=1), 0.0)
    member = picked.astype(jnp.bfloat16)
    sums = lax.dot_general(
        member, rows, (((0,), (0,)), ((), ())), preferred_element_type=jnp.float32
    )
    counts = jnp.sum(picked.astype(jnp.float32), axis=0)
    costs = jnp.sum(jnp.where(picked, margin[:, None], 0.0), axis=0)
    return (sums, counts, costs)


def residual_of(rows, first, live, centers):
    picked = centers[jnp.maximum(first, 0)]
    return jnp.where(live[:, None], rows.astype(jnp.float32) - picked, 0.0).astype(jnp.bfloat16)


def local(embeddings, cluster_key, child_first, child_second, coarse_centroids, fine_centroids):
    n_shard = lax.axis_size("shard")
    n_group = lax.axis_size("group")
    count_rows = embeddings.shape[0]
    width = embeddings.shape[1]
    children = coarse_centroids.shape[1]
    slots = max(2, 2 * count_rows // (n_shard * n_group))
    total_slots = n_shard * n_group * slots
    keys = cluster_key[:, 0]
    order = jnp.argsort(keys, stable=True)
    sorted_keys = keys[order]
    begins = jnp.searchsorted(sorted_keys, sorted_keys, side="left")
    sorted_rank = jnp.arange(count_rows, dtype=jnp.int32) - begins
    rank = jnp.zeros((count_rows,), jnp.int32).at[order].set(sorted_rank)
    place = keys * slots + rank
    codes = child_first * children + child_second + 1
    layout = jnp.zeros((total_slots, width), jnp.bfloat16).at[place].set(embeddings)
    code_layout = jnp.zeros((total_slots,), jnp.int32).at[place].set(codes)
    layout = layout.reshape(n_shard, n_group * slots, width)
    code_layout = code_layout.reshape(n_shard, n_group * slots)
    arrived, arrived_codes = (
        lax.all_to_all(layout, "shard", split_axis=0, concat_axis=0, tiled=True),
        lax.all_to_all(code_layout, "shard", split_axis=0, concat_axis=0, tiled=True),
    )
    code_grid = arrived_codes.reshape(n_shard, n_group, slots)
    flat_rows = arrived.reshape(-1, width)
    live_one, first_one, second_one = split_codes(arrived_codes.reshape(-1), children)
    sums_one, counts_one, costs_one = level_terms(
        flat_rows, first_one, live_one, coarse_centroids[0]
    )
    old_one = coarse_centroids[0].astype(jnp.float32)
    tot_sums, tot_counts, tot_costs = (
        lax.psum(sums_one.astype(jnp.bfloat16), "group").astype(jnp.float32),
        lax.psum(counts_one.astype(jnp.bfloat16), "group").astype(jnp.float32),
        lax.psum(costs_one.astype(jnp.bfloat16), "group").astype(jnp.float32),
    )
    coarse_f = (tot_sums + old_one) / (tot_counts[:, None] + 1.0)
    residual = residual_of(flat_rows, first_one, live_one, coarse_f).reshape(
        n_shard, n_group, slots, width
    )
    moved_res, moved_codes = (
        lax.all_to_all(residual, "group", split_axis=1, concat_axis=1, tiled=True),
        lax.all_to_all(code_grid, "group", split_axis=1, concat_axis=1, tiled=True),
    )
    live_two, first_two, second_two = split_codes(moved_codes.reshape(-1), children)
    fine_rows = moved_res.reshape(-1, width)
    sums_two, counts_two, costs_two = level_terms(
        fine_rows, second_two, live_two, fine_centroids[0]
    )
    old_two = fine_centroids[0].astype(jnp.float32)
    all_sums, all_counts, all_costs = (
        lax.psum(sums_two.astype(jnp.bfloat16), "shard").astype(jnp.float32),
        lax.psum(counts_two.astype(jnp.bfloat16), "shard").astype(jnp.float32),
        lax.psum(costs_two.astype(jnp.bfloat16), "shard").astype(jnp.float32),
    )
    fine_f = (all_sums + old_two) / (all_counts[:, None] + 1.0)
    return (
        coarse_f.astype(jnp.bfloat16)[None],
        fine_f.astype(jnp.bfloat16)[None],
        tot_costs[None],
        all_costs[None],
    )


def solution(mesh):
    placed = (
        P(("shard", "group"), None),
        P(("shard", "group"), None),
        P(("shard", "group")),
        P(("shard", "group")),
        P("shard", None, None),
        P("group", None, None),
    )
    return jax.shard_map(
        local,
        mesh=mesh,
        in_specs=placed,
        out_specs=(
            P("shard", None, None),
            P("group", None, None),
            P("shard", None),
            P("group", None),
        ),
        check_vma=False,
    )
```

profile of v0, /device:TPU:56, one launch (start us, length us, event | category | flops | bytes accessed | tf_op | source)
XLA Modules:
  0.0 517.2 jit_solution(979569741164195802)
XLA Ops:
  7.2 4.4 sort.17
  11.7 3.6 gather_fusion.1
  15.3 35.9 %while.25 = (s32[]{:T(128)}, u32[512]{0:T(512)S(1)}, u32[512]{0:T(512)S(1)}, s32[512]{0:T(512)S(1)}, s32[]{:T(128)}, /*index=5*/s32[]{:T(128)}, s32[]{}) while((s32[]{:T(128)}, u32[512]{0:T(512)S(1)}, u32[512]{0:T(512)S(1)}, s32[512]{0:T(512)S(1)}, s32[]{:T(128)}, /*index=5*/s32[]{:T(128)}, s32[]{}) %tuple.47), condition=%wide.region_2.3_spmd.clone, body=%wide.region_1.2_spmd.clone.sunk | while | flops 10244 | bytes 40037 | solution.py:50
  15.3 3.5 gather_fusion
  18.9 3.5 gather_fusion
  22.5 3.5 gather_fusion
  26.1 3.5 gather_fusion
  29.7 3.5 gather_fusion
  33.3 3.5 gather_fusion
  36.9 3.5 gather_fusion
  40.5 3.5 gather_fusion
  44.0 3.5 gather_fusion
  47.6 3.5 gather_fusion
  56.8 13.2 %all-to-all-start = ((s32[32,1,32]{2,1,0:T(1,128)}), s32[32,1,32]{2,1,0:T(1,128)S(1)}, u32[]{:S(2)}, u32[]{:S(2)}) async-start(s32[32,1,32]{2,1,0:T(1,128)} %bitcast.1), calls=%async_computation | async-start | bytes 32768 | tf_op jit(solution)/shard_map/all_to_all | solution.py:61
  70.0 4.8 scatter_custom_fusion.2
  74.8 4.8 all-to-all-done
  79.7 5.1 all-to-all-start.1
  86.9 47.4 %all-to-all-done.1 = bf16[32,32,1024]{2,1,0:T(8,128)(2,1)S(1)} async-done(((bf16[32,32,1024]{2,1,0:T(8,128)(2,1)}), bf16[32,32,1024]{2,1,0:T(8,128)(2,1)S(1)}, u32[]{:S(2)}, u32[]{:S(2)}) %all-to-all-start.1) | async-done | bytes 2097184 | tf_op jit(solution)/shard_map/all_to_all | solution.py:60
  134.3 6.9 %all-to-all-start.2 = ((s32[32,16,2]{0,2,1:T(2,128)}), s32[32,16,2]{0,2,1:T(2,128)S(1)}, u32[]{:S(2)}, u32[]{:S(2)}) async-start(s32[32,16,2]{0,2,1:T(2,128)} %bitcast.6), calls=%async_computation.2 | async-start | bytes 32768 | tf_op jit(solution)/shard_map/all_to_all | solution.py:81
  145.7 3.1 copy.55
  148.9 22.2 %all-reduce.1 = (bf16[512]{0:T(512)(128)(2,1)S(1)}, bf16[1,512]{1,0:T(2,128)(2,1)S(1)}) all-reduce(bf16[512]{0:T(512)(128)(2,1)S(1)} %get-tuple-element.93, bf16[1,512]{1,0:T(2,128)(2,1)S(1)} %broadcast_in_dim.111), channel_id=1, replica_groups=mesh['shard'=32,'group'=16] {'group'}, use_global_device_ids=true, to_apply=%region_8.9 | all-reduce | flops 1024 | bytes 4096 | tf_op jit(solution)/shard_map/psum | solution.py:72
  171.1 86.3 %all-reduce.5.cloned.1.call-done = bf16[512,1024]{1,0:T(8,128)(2,1)} async-done(((bf16[512,1024]{1,0:T(8,128)(2,1)}), bf16[512,1024]{1,0:T(8,128)(2,1)}) %all-reduce.5.cloned.1.call-update) | async-done | bytes 1048592 | tf_op jit(solution)/shard_map/psum | solution.py:71
  260.2 5.5 %gather_fusion.2 = f32[1024,1024]{1,0:T(8,128)} fusion(f32[512,1024]{1,0:T(8,128)S(1)} %get-tuple-element.110, s32[1024]{0:T(1024)S(1)} %broadcast_clamp_fusion), kind=kCustom, calls=%fused_computation.2 | custom fusion | bytes 8392704 | tf_op jit(solution)/shard_map/gather | solution.py:35
  265.6 5.8 %gather.17 = f32[32,16,2,1024]{3,2,1,0:T(2,128)} reshape(f32[1024,1024]{1,0:T(8,128)} %gather_fusion.2) | data formatting | bytes 8388608 | tf_op jit(solution)/shard_map/gather | solution.py:35
  271.5 6.4 %fusion.1 = bf16[32,16,2,1024]{3,0,2,1:T(8,128)(2,1)S(1)} fusion(f32[32,16,2,1024]{3,0,2,1:T(8,128)} %bitcast.39, f32[32,16,2,1024]{3,2,1,0:T(2,128)} %gather.17, pred[32,16,2]{0,2,1:T(4,128)(4,1)S(1)} %broadcast_compare_fusion), kind=kLoop, calls=%fused_computation.12 | loop fusion | flops 3145728 | bytes 10486784 | tf_op jit(solution)/shard_map/convert_element_type | solution.py:36
  277.8 3.5 copy.57
  281.3 8.5 %all-to-all-start.3 = ((bf16[32,16,2,1024]{3,2,0,1:T(2,128)(2,1)}), bf16[32,16,2,1024]{3,2,0,1:T(2,128)(2,1)S(1)}, u32[]{:S(2)}, u32[]{:S(2)}) async-start(bf16[32,16,2,1024]{3,2,0,1:T(2,128)(2,1)} %copy.57), calls=%async_computation.3 | async-start | bytes 4194304 | tf_op jit(solution)/shard_map/all_to_all | solution.py:80
  291.0 46.5 %all-to-all-done.3 = bf16[32,16,2,1024]{3,2,0,1:T(2,128)(2,1)S(1)} async-done(((bf16[32,16,2,1024]{3,2,0,1:T(2,128)(2,1)}), bf16[32,16,2,1024]{3,2,0,1:T(2,128)(2,1)S(1)}, u32[]{:S(2)}, u32[]{:S(2)}) %all-to-all-start.3) | async-done | bytes 2097184 | tf_op jit(solution)/shard_map/all_to_all | solution.py:80
  337.5 3.6 copy.58
  341.0 2.7 reshape.179
  349.0 75.9 %all-reduce = (bf16[512]{0:T(512)(128)(2,1)S(1)}, bf16[1,512]{1,0:T(2,128)(2,1)S(1)}) all-reduce(bf16[512]{0:T(512)(128)(2,1)S(1)} %get-tuple-element.94, bf16[1,512]{1,0:T(2,128)(2,1)S(1)} %broadcast_in_dim.114), channel_id=1, replica_groups=mesh['shard'=32,'group'=16] {'shard'}, use_global_device_ids=true, to_apply=%region_11.12 | all-reduce | flops 1024 | bytes 4096 | tf_op jit(solution)/shard_map/psum | solution.py:91
  425.4 82.2 %all-reduce.7.cloned.1.call-done = bf16[512,1024]{1,0:T(8,128)(2,1)} async-done(((bf16[512,1024]{1,0:T(8,128)(2,1)}), bf16[512,1024]{1,0:T(8,128)(2,1)}) %all-reduce.7.cloned.1.call-update) | async-done | bytes 1048592 | tf_op jit(solution)/shard_map/psum | solution.py:90
  (111 shorter events, 24.9 us)
Async XLA Ops:
  15.3 38.4 %copy-start = (s32[512,1]{0,1:T(1,128)S(1)}, s32[512,1]{0,1:T(1,128)}, u32[]{:S(2)}) copy-start(s32[512,1]{0,1:T(1,128)} %param.9) | copy-start | bytes 6148
  15.3 38.4 %copy-start.3 = (s32[512]{0:T(512)S(1)}, s32[512]{0:T(512)}, u32[]{:S(2)}) copy-start(s32[512]{0:T(512)} %param.11) | copy-start | bytes 6148
  15.3 38.4 %copy-start.4 = (s32[512]{0:T(512)S(1)}, s32[512]{0:T(512)}, u32[]{:S(2)}) copy-start(s32[512]{0:T(512)} %param.10) | copy-start | bytes 6148
  56.8 22.8 %all-to-all-start = ((s32[32,1,32]{2,1,0:T(1,128)}), s32[32,1,32]{2,1,0:T(1,128)S(1)}, u32[]{:S(2)}, u32[]{:S(2)}) async-start(s32[32,1,32]{2,1,0:T(1,128)} %bitcast.1), calls=%async_computation | async-start | bytes 32768 | tf_op jit(solution)/shard_map/all_to_all | solution.py:61
  79.7 5.1 copy-start.1
  79.7 54.7 %all-to-all-start.1 = ((bf16[32,32,1024]{2,1,0:T(8,128)(2,1)}), bf16[32,32,1024]{2,1,0:T(8,128)(2,1)S(1)}, u32[]{:S(2)}, u32[]{:S(2)}) async-start(bf16[32,32,1024]{2,1,0:T(8,128)(2,1)} %bitcast.42), calls=%async_computation.1 | async-start | bytes 4194304 | tf_op jit(solution)/shard_map/all_to_all | solution.py:60
  134.3 147.0 %all-to-all-start.2 = ((s32[32,16,2]{0,2,1:T(2,128)}), s32[32,16,2]{0,2,1:T(2,128)S(1)}, u32[]{:S(2)}, u32[]{:S(2)}) async-start(s32[32,16,2]{0,2,1:T(2,128)} %bitcast.6), calls=%async_computation.2 | async-start | bytes 32768 | tf_op jit(solution)/shard_map/all_to_all | solution.py:81
  141.2 116.2 %all-reduce.5.cloned.1.call-start = ((), (), s32[]{:S(2)}) async-start(), calls=%async_computation.4 | async-start | bytes 2097152 | tf_op jit(solution)/shard_map/psum | solution.py:71
  281.3 56.1 %all-to-all-start.3 = ((bf16[32,16,2,1024]{3,2,0,1:T(2,128)(2,1)}), bf16[32,16,2,1024]{3,2,0,1:T(2,128)(2,1)S(1)}, u32[]{:S(2)}, u32[]{:S(2)}) async-start(bf16[32,16,2,1024]{3,2,0,1:T(2,128)(2,1)} %copy.57), calls=%async_computation.3 | async-start | bytes 4194304 | tf_op jit(solution)/shard_map/all_to_all | solution.py:80
  289.9 217.8 %all-reduce.7.cloned.1.call-start = ((), (), s32[]{:S(2)}) async-start(), calls=%async_computation.5 | async-start | bytes 2097152 | tf_op jit(solution)/shard_map/psum | solution.py:90
  343.8 2.3 copy-start.2
Sparse Core Ops, SparseCore 0:
  145.5 111.8 all-reduce.4
  346.2 161.4 all-reduce.6
where the time goes:
time: 518 us; the launch traced here: 517 us
  waiting for transfers between devices  267 us (52%)
  blocking collectives  98.1 us (19%)
  local copies, waits for them, and re-layouts  75 us (14%)
  starting transfers between devices  34.1 us (7%)
  other arithmetic  19.9 us (4%)
  between operations  14.3 us (3%)
  matrix products  7.89 us (2%)
    psum x1, waiting for transfers between devices, local(): lax.psum(sums_one.astype(jnp.bfloat16), 'group').astype(jnp.float32)  86.3 us
    psum x1, waiting for transfers between devices, local(): lax.psum(sums_two.astype(jnp.bfloat16), 'shard').astype(jnp.float32)  82.2 us
    psum x1, blocking collectives, local(): lax.psum(counts_two.astype(jnp.bfloat16), 'shard').astype(jnp.float32)  75.9 us
    all_to_all x1, waiting for transfers between devices, local(): lax.all_to_all(layout, 'shard', split_axis=0, concat_axis=0, tiled=True)  47.4 us
    all_to_all x1, waiting for transfers between devices, local(): lax.all_to_all(residual, 'group', split_axis=1, concat_axis=1, tiled=True)  46.5 us
    gather x10, local copies, waits for them, and re-layouts, local(): begins = jnp.searchsorted(sorted_keys, sorted_keys, side='left')  34.9 us
    psum x1, blocking collectives, local(): lax.psum(counts_one.astype(jnp.bfloat16), 'group').astype(jnp.float32)  22.2 us
    all_to_all x1, starting transfers between devices, local(): lax.all_to_all(code_layout, 'shard', split_axis=0, concat_axis=0, tiled=T...  13.2 us
  transfers between devices with their start and end apart: 6, of which 5 were waited for; matrix products, arithmetic and copies ran while one was open for 8% of the time, Pallas kernels for 0%

commit v1 on v0

v1 whole, which is shorter than its diff:
```python
import jax
import jax.numpy as jnp
from jax import lax
from jax.sharding import Mesh
from jax.sharding import PartitionSpec as P

SHARD = ("z", "x")
GROUP = ("y", "core")
ALL = SHARD + GROUP
SLOTS = 2
EXTRA = 128


def exchange(blocks, axes):
    return lax.all_to_all(blocks, axes, split_axis=0, concat_axis=0, tiled=True)


def columns(values, rows):
    lanes = lax.broadcasted_iota(jnp.int32, (rows, EXTRA), 1)
    out = jnp.zeros((rows, EXTRA), jnp.bfloat16)
    for lane, value in enumerate(values):
        out = jnp.where(lanes == lane, value.astype(jnp.bfloat16)[:, None], out)
    return out


def halves(value):
    high = value.astype(jnp.bfloat16)
    return high, (value - high.astype(jnp.float32)).astype(jnp.bfloat16)


def level_sums(rows, member, live, centroids):
    products = lax.dot_general(
        rows, centroids, (((1,), (1,)), ((), ())), preferred_element_type=jnp.float32
    )
    cent_f = centroids.astype(jnp.float32)
    squares = jnp.sum(cent_f * cent_f, axis=1)
    scores = squares[None, :] - 2.0 * products
    assigned = jnp.sum(jnp.where(member, scores, 0.0), axis=1)
    margin = jnp.where(live, assigned - jnp.min(scores, axis=1), 0.0)
    extra = columns((live,) + halves(margin), rows.shape[0])
    return lax.dot_general(
        member.astype(jnp.bfloat16),
        jnp.concatenate([rows, extra], axis=1),
        (((0,), (0,)), ((), ())),
        preferred_element_type=jnp.float32,
    ).astype(jnp.bfloat16)


def merged(partial, axes, parts, mine, centroids):
    children, wide = partial.shape
    each = children // parts
    width = wide - EXTRA
    arrived = exchange(partial.reshape(parts, each, wide), axes)
    total = jnp.sum(arrived.astype(jnp.float32), axis=0)
    old = lax.dynamic_slice_in_dim(centroids, mine * each, each, 0).astype(jnp.float32)
    fresh = (total[:, :width] + old) / (total[:, width : width + 1] + 1.0)
    cost = total[:, width + 1] + total[:, width + 2]
    return jnp.concatenate([fresh.astype(jnp.bfloat16), columns(halves(cost), each)], axis=1)


def spread(block, axes, parts):
    return exchange(jnp.broadcast_to(block[None], (parts,) + block.shape), axes)


def cost_of(full, width):
    tail = full[:, width : width + 2].astype(jnp.float32)
    return tail[:, 0] + tail[:, 1]


def local(embeddings, cluster_key, child_first, child_second, coarse_centroids, fine_centroids):
    n_shard = lax.axis_size(SHARD)
    n_group = lax.axis_size(GROUP)
    rows_dev, width = embeddings.shape
    children = coarse_centroids.shape[1]
    devices = n_shard * n_group
    slots = devices * SLOTS
    coarse, fine = coarse_centroids[0], fine_centroids[0]

    keys = cluster_key[:, 0]
    rows_i = lax.broadcasted_iota(jnp.int32, (rows_dev, rows_dev), 0)
    cols_i = lax.broadcasted_iota(jnp.int32, (rows_dev, rows_dev), 1)
    same = (keys[:, None] == keys[None, :]) & (rows_i < cols_i)
    place = keys * SLOTS + jnp.sum(same.astype(jnp.int32), axis=0)
    move = lax.broadcasted_iota(jnp.int32, (slots, rows_dev), 0) == place[None, :]
    codes = columns(
        (
            jnp.ones((rows_dev,), jnp.int32),
            child_first // 16,
            child_first % 16,
            child_second // 16,
            child_second % 16,
        ),
        rows_dev,
    )
    layout = lax.dot_general(
        move.astype(jnp.bfloat16),
        jnp.concatenate([embeddings, codes], axis=1),
        (((1,), (0,)), ((), ())),
        preferred_element_type=jnp.float32,
    ).astype(jnp.bfloat16)
    arrived = exchange(layout.reshape(devices, SLOTS, width + EXTRA), ALL)
    arrived = arrived.reshape(slots, width + EXTRA)
    rows = arrived[:, :width]
    tail = arrived[:, width : width + 5].astype(jnp.int32)
    live = tail[:, 0] > 0
    labels = lax.broadcasted_iota(jnp.int32, (slots, children), 1)
    member_one = ((tail[:, 1] * 16 + tail[:, 2])[:, None] == labels) & live[:, None]
    member_two = ((tail[:, 3] * 16 + tail[:, 4])[:, None] == labels) & live[:, None]

    partial_one = level_sums(rows, member_one, live, coarse)
    block_one = merged(partial_one, GROUP, n_group, lax.axis_index(GROUP), coarse)
    n_y = lax.axis_size("y")
    own = spread(block_one, "y", n_y)
    other = lax.ppermute(own, "core", [(0, 1), (1, 0)])
    even = lax.axis_index("core") == 0
    full_one = jnp.stack(
        [jnp.where(even, own, other), jnp.where(even, other, own)], axis=1
    ).reshape(children, width + EXTRA)
    coarse_new = full_one[:, :width]

    center = lax.dot_general(
        member_one.astype(jnp.bfloat16),
        coarse_new,
        (((1,), (0,)), ((), ())),
        preferred_element_type=jnp.float32,
    )
    residual = (rows.astype(jnp.float32) - center).astype(jnp.bfloat16)
    partial_two = level_sums(residual, member_two, live, fine)
    block_two = merged(partial_two, SHARD, n_shard, lax.axis_index(SHARD), fine)
    full_two = spread(block_two, SHARD, n_shard).reshape(children, width + EXTRA)
    return (
        coarse_new[None],
        full_two[:, :width][None],
        cost_of(full_one, width)[None],
        cost_of(full_two, width)[None],
    )


def solution(mesh):
    torus = Mesh(mesh.devices.reshape(-1, 4, mesh.shape["group"] // 2, 2), ALL)
    placed = (
        P(ALL, None),
        P(ALL, None),
        P(ALL),
        P(ALL),
        P(SHARD, None, None),
        P(GROUP, None, None),
    )
    return jax.shard_map(
        local,
        mesh=torus,
        in_specs=placed,
        out_specs=(
            P(SHARD, None, None),
            P(GROUP, None, None),
            P(SHARD, None),
            P(GROUP, None),
        ),
        check_vma=False,
    )
```

time: 518 us -> 257 us (0.50)
  waiting for transfers between devices: 267 us -> 142 us
  blocking collectives: 98.1 us -> 22.1 us
  local copies, waits for them, and re-layouts: 75 us -> 16.7 us
  between operations: 14.3 us -> 0.98 us
  other arithmetic: 19.9 us -> 10.6 us
  starting transfers between devices: 34.1 us -> 43.3 us
  matrix products: 7.89 us -> 16.7 us
    psum x2 -> x0, waiting for transfers between devices: 169 us -> none  [the longest x1 86.3 us: local(): lax.psum(sums_one.astype(jnp.bfloat16), 'group').astype(jnp.float32)]
    psum x2 -> x0, blocking collectives: 98.1 us -> none  [the longest x1 75.9 us: local(): lax.psum(counts_two.astype(jnp.bfloat16), 'shard').astype(jnp.float32)]
    gather x13 -> x0, local copies, waits for them, and re-layouts: 49.8 us -> none  [the longest x10 34.9 us: local(): begins = jnp.searchsorted(sorted_keys, sorted_keys, side='left')]
    all_to_all x4, waiting for transfers between devices: 98.7 us -> 140 us  [exchange(): return lax.all_to_all(blocks, axes, split_axis=0, concat_axis=0, tiled=True)]
    all_to_all x0 -> x1, blocking collectives: none -> 22.1 us  [exchange(): return lax.all_to_all(blocks, axes, split_axis=0, concat_axis=0, tiled=True)]
    scatter x3 -> x0, local copies, waits for them, and re-layouts: 9.71 us -> none  [the longest x1 4.82 us: local(): jnp.zeros((total_slots, width), jnp.bfloat16).at[place].set(embeddings)]
    dot_general x4 -> x6, matrix products: 7.89 us -> 16.7 us  [the longest x2 8.65 us: level_sums(): lax.dot_general(member.astype(jnp.bfloat16), jnp.concatenate([rows, extra...]
    all_to_all x4, starting transfers between devices: 33.7 us -> 41.4 us  [exchange(): return lax.all_to_all(blocks, axes, split_axis=0, concat_axis=0, tiled=True)]
  transfers between devices with their start and end apart: 6 -> 5, of which waited for: 5 -> 5; matrix products, arithmetic and copies ran while one was open for 8% -> 1% of each run, Pallas kernels for 0% -> 0%
where the time goes in v1:
time: 257 us; the launch traced here: 252 us
  waiting for transfers between devices  142 us (55%)
  starting transfers between devices  43.3 us (17%)
  blocking collectives  22.1 us (9%)
  matrix products  16.7 us (6%)
  local copies, waits for them, and re-layouts  16.7 us (6%)
  other arithmetic  10.6 us (4%)
    all_to_all x4, waiting for transfers between devices, exchange(): return lax.all_to_all(blocks, axes, split_axis=0, concat_axis=0, tiled=True)  140 us
    all_to_all x4, starting transfers between devices, exchange(): return lax.all_to_all(blocks, axes, split_axis=0, concat_axis=0, tiled=True)  41.4 us
    all_to_all x1, blocking collectives, exchange(): return lax.all_to_all(blocks, axes, split_axis=0, concat_axis=0, tiled=True)  22.1 us
    dot_general x2, matrix products, level_sums(): lax.dot_general(member.astype(jnp.bfloat16), jnp.concatenate([rows, extra...  8.65 us
    unnamed x18, local copies, waits for them, and re-layouts  5.58 us
  transfers between devices with their start and end apart: 5, of which 5 were waited for; matrix products, arithmetic and copies ran while one was open for 1% of the time, Pallas kernels for 0%

profile of v1, /device:TPU:56, one launch (start us, length us, event | category | flops | bytes accessed | tf_op | source)
XLA Modules:
  0.0 252.4 jit_solution(17680961666295654464)
XLA Ops:
  0.7 0.9 convert_reduce_fusion.2
  1.6 0.7 multiply_add_fusion
  2.3 0.7 fusion.49
  3.3 2.8 %convolution_convert_fusion = bf16[1024,1152]{1,0:T(8,128)(2,1)S(1)} fusion(bf16[512,128]{1,0:T(8,128)(2,1)S(1)} %select_select_fusion.2, bf16[512,1024]{1,0:T(8,128)(2,1)} %param.6, s32[512]{0:T(512)S(1)} %multiply_add_fusion), kind=kOutput, calls=%fused_computation.1 | convolution fusion | flops 1212022784 | bytes 3540992 | tf_op jit(solution)/shard_map/dot_general | solution.py:95
  6.2 2.3 reshape.113
  8.5 22.6 %all-to-all-start = ((bf16[512,2,1152]{2,1,0:T(2,128)(2,1)}), bf16[512,2,1152]{2,1,0:T(2,128)(2,1)}, u32[]{:S(2)}, u32[]{:S(2)}) async-start(bf16[512,2,1152]{2,1,0:T(2,128)(2,1)} %reshape.113), calls=%async_computation | async-start | bytes 4718592 | tf_op jit(solution)/shard_map/all_to_all | solution.py:15
  31.1 0.9 multiply_reduce_fusion.1
  32.0 53.7 %all-to-all-done = bf16[512,2,1152]{2,1,0:T(2,128)(2,1)} async-done(((bf16[512,2,1152]{2,1,0:T(2,128)(2,1)}), bf16[512,2,1152]{2,1,0:T(2,128)(2,1)}, u32[]{:S(2)}, u32[]{:S(2)}) %all-to-all-start) | async-done | bytes 2359328 | tf_op jit(solution)/shard_map/all_to_all | solution.py:15
  85.7 5.0 %reshape.114 = bf16[1024,1152]{1,0:T(8,128)(2,1)S(1)} reshape(bf16[512,2,1152]{2,1,0:T(2,128)(2,1)} %all-to-all-done) | data formatting | bytes 4718592 | tf_op jit(solution)/shard_map/reshape | solution.py:102
  90.8 1.6 fusion.29
  92.6 1.6 slice.96
  94.2 4.0 %copy.22 = bf16[1024,1024]{0,1:T(8,128)(2,1)} copy(bf16[1024,1024]{1,0:T(8,128)(2,1)} %slice.96) | data formatting | bytes 4194304
  98.1 2.3 fusion.11
  101.1 4.3 %convolution_convert_fusion.2 = bf16[512,1152]{1,0:T(8,128)(2,1)} fusion(bf16[1024,128]{0,1:T(8,128)(2,1)S(1)} %fusion.33, bf16[1024,1024]{0,1:T(8,128)(2,1)} %copy.22, s32[1024]{0:T(1024)} %get-tuple-element.13, pred[1024]{0:T(1024)(128)(4,1)} %copy-done.5), kind=kOutput, calls=%fused_computation.3 | convolution fusion | flops 1214316544 | bytes 3544064 | tf_op jit(solution)/shard_map/dot_general | solution.py:41
  105.5 8.4 %all-to-all-start.1 = ((bf16[16,32,1152]{2,1,0:T(8,128)(2,1)}), bf16[16,32,1152]{2,1,0:T(8,128)(2,1)S(1)}, u32[]{:S(2)}, u32[]{:S(2)}) async-start(bf16[16,32,1152]{2,1,0:T(8,128)(2,1)} %bitcast.3), calls=%async_computation.1 | async-start | bytes 2359296 | tf_op jit(solution)/shard_map/all_to_all | solution.py:15
  113.9 27.7 %all-to-all-done.1 = bf16[16,32,1152]{2,1,0:T(8,128)(2,1)S(1)} async-done(((bf16[16,32,1152]{2,1,0:T(8,128)(2,1)}), bf16[16,32,1152]{2,1,0:T(8,128)(2,1)S(1)}, u32[]{:S(2)}, u32[]{:S(2)}) %all-to-all-start.1) | async-done | bytes 1179680 | tf_op jit(solution)/shard_map/all_to_all | solution.py:15
  142.4 22.1 %all_to_all.25 = bf16[8,32,1152]{2,1,0:T(8,128)(2,1)S(1)} all-to-all(bf16[8,32,1152]{2,1,0:T(8,128)(2,1)S(1)} %broadcast_in_dim.184), channel_id=1, replica_groups=mesh['z'=8,'x'=4,'y'=8,'core'=2] {'y'}, dimensions={0} | all-to-all | bytes 1179648 | tf_op jit(solution)/shard_map/all_to_all | solution.py:15
  164.4 1.9 collective-permute-start
  166.7 1.6 collective-permute-done
  168.6 1.4 subtract_convert_fusion
  170.0 1.6 fusion.12
  172.3 4.3 %convolution_convert_fusion.1 = bf16[512,1152]{1,0:T(8,128)(2,1)} fusion(bf16[1024,128]{0,1:T(8,128)(2,1)S(1)} %fusion.34, bf16[1024,1024]{0,1:T(8,128)(2,1)} %copy-done.7, s32[1024]{0:T(1024)S(1)} %copy-done.3, pred[1024]{0:T(1024)(128)(4,1)S(1)} %copy-done.6), kind=kOutput, calls=%fused_computation.2 | convolution fusion | flops 1214316544 | bytes 3544064 | tf_op jit(solution)/shard_map/dot_general | solution.py:41
  176.6 4.8 %all-to-all-start.3 = ((bf16[32,16,1152]{2,1,0:T(8,128)(2,1)}), bf16[32,16,1152]{2,1,0:T(8,128)(2,1)S(1)}, u32[]{:S(2)}, u32[]{:S(2)}) async-start(bf16[32,16,1152]{2,1,0:T(8,128)(2,1)} %bitcast.12), calls=%async_computation.3 | async-start | bytes 2359296 | tf_op jit(solution)/shard_map/all_to_all | solution.py:15
  181.4 31.1 %all-to-all-done.3 = bf16[32,16,1152]{2,1,0:T(8,128)(2,1)S(1)} async-done(((bf16[32,16,1152]{2,1,0:T(8,128)(2,1)}), bf16[32,16,1152]{2,1,0:T(8,128)(2,1)S(1)}, u32[]{:S(2)}, u32[]{:S(2)}) %all-to-all-start.3) | async-done | bytes 1179680 | tf_op jit(solution)/shard_map/all_to_all | solution.py:15
  213.0 0.8 fusion.42
  213.9 1.1 broadcast_in_dim.195
  215.0 5.6 %all-to-all-start.4 = ((bf16[32,16,1152]{2,1,0:T(8,128)(2,1)}), bf16[32,16,1152]{2,1,0:T(8,128)(2,1)S(1)}, u32[]{:S(2)}, u32[]{:S(2)}) async-start(bf16[32,16,1152]{2,1,0:T(8,128)(2,1)} %broadcast_in_dim.195), calls=%async_computation.4 | async-start | bytes 2359296 | tf_op jit(solution)/shard_map/all_to_all | solution.py:15
  220.7 0.8 fusion.38
  221.5 1.1 slice_bitcast_fusion.1
  222.6 27.8 %all-to-all-done.4 = bf16[32,16,1152]{2,1,0:T(8,128)(2,1)S(1)} async-done(((bf16[32,16,1152]{2,1,0:T(8,128)(2,1)}), bf16[32,16,1152]{2,1,0:T(8,128)(2,1)S(1)}, u32[]{:S(2)}, u32[]{:S(2)}) %all-to-all-start.4) | async-done | bytes 1179680 | tf_op jit(solution)/shard_map/all_to_all | solution.py:15
  250.5 1.1 slice_bitcast_fusion
  251.6 0.8 fusion.37
  (49 shorter events, 3.9 us)
Async XLA Ops:
  8.5 22.6 %copy-start.1 = (bf16[1,512,1024]{2,1,0:T(8,128)(2,1)S(1)}, bf16[1,512,1024]{2,1,0:T(8,128)(2,1)}, u32[]{:S(2)}) copy-start(bf16[1,512,1024]{2,1,0:T(8,128)(2,1)} %param.10) | copy-start | bytes 3145732
  8.5 77.2 %all-to-all-start = ((bf16[512,2,1152]{2,1,0:T(2,128)(2,1)}), bf16[512,2,1152]{2,1,0:T(2,128)(2,1)}, u32[]{:S(2)}, u32[]{:S(2)}) async-start(bf16[512,2,1152]{2,1,0:T(2,128)(2,1)} %reshape.113), calls=%async_computation | async-start | bytes 4718592 | tf_op jit(solution)/shard_map/all_to_all | solution.py:15
  92.5 1.6 copy-start.5
  105.5 36.1 %all-to-all-start.1 = ((bf16[16,32,1152]{2,1,0:T(8,128)(2,1)}), bf16[16,32,1152]{2,1,0:T(8,128)(2,1)S(1)}, u32[]{:S(2)}, u32[]{:S(2)}) async-start(bf16[16,32,1152]{2,1,0:T(8,128)(2,1)} %bitcast.3), calls=%async_computation.1 | async-start | bytes 2359296 | tf_op jit(solution)/shard_map/all_to_all | solution.py:15
  113.9 52.4 %copy-start.2 = (bf16[1,512,1024]{2,1,0:T(8,128)(2,1)S(1)}, bf16[1,512,1024]{2,1,0:T(8,128)(2,1)}, u32[]{:S(2)}) copy-start(bf16[1,512,1024]{2,1,0:T(8,128)(2,1)} %param.11) | copy-start | bytes 3145732
  164.4 3.9 %collective-permute-start = (bf16[8,32,1152]{2,1,0:T(8,128)(2,1)S(1)}, bf16[8,32,1152]{2,1,0:T(8,128)(2,1)S(1)}, u32[]{:S(2)}, u32[]{:S(2)}) collective-permute-start(bf16[8,32,1152]{2,1,0:T(8,128)(2,1)S(1)} %all_to_all.25), channel_id=1, source_target_pairs={{0,1},{1,0},{2,3},{3,2},{4,5},{5,4},{6,7},{7,6},{8,9},{9,8},{10,11... | collective-permute-start | bytes 1769480 | tf_op jit(solution)/shard_map/ppermute | solution.py:114
  166.6 1.9 copy-start
  166.6 1.9 copy-start.4
  166.6 1.9 copy-start.6
  168.6 1.4 copy-start.3
  169.9 1.6 copy-start.7
  176.6 35.9 %all-to-all-start.3 = ((bf16[32,16,1152]{2,1,0:T(8,128)(2,1)}), bf16[32,16,1152]{2,1,0:T(8,128)(2,1)S(1)}, u32[]{:S(2)}, u32[]{:S(2)}) async-start(bf16[32,16,1152]{2,1,0:T(8,128)(2,1)} %bitcast.12), calls=%async_computation.3 | async-start | bytes 2359296 | tf_op jit(solution)/shard_map/all_to_all | solution.py:15
  215.0 35.4 %all-to-all-start.4 = ((bf16[32,16,1152]{2,1,0:T(8,128)(2,1)}), bf16[32,16,1152]{2,1,0:T(8,128)(2,1)S(1)}, u32[]{:S(2)}, u32[]{:S(2)}) async-start(bf16[32,16,1152]{2,1,0:T(8,128)(2,1)} %broadcast_in_dim.195), calls=%async_computation.4 | async-start | bytes 2359296 | tf_op jit(solution)/shard_map/all_to_all | solution.py:15

commit v2 on v1

v2 whole, which is shorter than its diff:
```python
import functools

import jax
import jax.numpy as jnp
from jax import lax
from jax.experimental import pallas as pl
from jax.experimental.pallas import tpu as pltpu
from jax.sharding import Mesh
from jax.sharding import PartitionSpec as P

SHARD = ("z", "x")
GROUP = ("y", "core")
ALL = SHARD + GROUP
SLOTS = 2
LANES = 128
EXTRA = 16
DIGIT = 16
F32 = jnp.float32
BF16 = jnp.bfloat16


def exchange(blocks, axes):
    return lax.all_to_all(blocks, axes, split_axis=0, concat_axis=0, tiled=True)


def iota(shape, dim):
    return lax.broadcasted_iota(jnp.int32, shape, dim)


def matmul(a, b, dims):
    return lax.dot_general(a, b, (dims, ((), ())), preferred_element_type=F32)


def kernel_call(body, name, flops, moved, **rest):
    return pl.pallas_call(
        body,
        name=name,
        cost_estimate=pl.CostEstimate(flops=flops, bytes_accessed=moved, transcendentals=0),
        compiler_params=pltpu.CompilerParams(vmem_limit_bytes=48 * 2**20),
        **rest,
    )


def whole(shape):
    return pl.BlockSpec(shape, lambda *_: (0,) * len(shape))


def place_body(info_ref, emb_ref, out_ref, wide_ref, place_ref):
    count, width = emb_ref.shape
    devices, slots, wide = out_ref.shape
    step = pl.program_id(0)

    @pl.when(step == 0)
    def _():
        info = info_ref[...]
        turned = jnp.transpose(info.astype(F32)).astype(jnp.int32)
        keys_row, keys_col = info[0:1, :], turned[:, 0:1]
        earlier = (keys_col == keys_row) & (iota((count, count), 0) < iota((count, count), 1))
        rank = jnp.sum(earlier.astype(jnp.int32), axis=0, keepdims=True)
        place_ref[...] = jnp.broadcast_to(keys_row * slots + rank, place_ref.shape)
        one, two = turned[:, 1:2], turned[:, 2:3]
        lane = iota((count, LANES), 1)
        codes = jnp.where(lane == 0, 1, 0)
        for index, value in enumerate((one // DIGIT, one % DIGIT, two // DIGIT, two % DIGIT)):
            codes = jnp.where(lane == index + 1, value, codes)
        wide_ref[:, :width] = emb_ref[...]
        wide_ref[:, width:] = codes.astype(F32).astype(BF16)

    block = devices * slots
    target = iota((block, count), 0) + step * block
    move = (target == place_ref[0:1, :]).astype(F32).astype(BF16)
    moved = matmul(move, wide_ref[...], ((1,), (0,))).astype(BF16)
    out_ref[...] = moved.reshape(devices, slots, wide)


def place(info, embeddings, devices, steps):
    count, width = embeddings.shape
    wide = width + LANES
    each = devices // steps
    return kernel_call(
        place_body,
        "place",
        2 * devices * SLOTS * count * wide,
        2 * (count * width + devices * SLOTS * wide),
        grid=(steps,),
        in_specs=[whole(info.shape), whole(embeddings.shape)],
        out_specs=pl.BlockSpec((each, SLOTS, wide), lambda i: (i, 0, 0)),
        out_shape=jax.ShapeDtypeStruct((devices, SLOTS, wide), BF16),
        scratch_shapes=[pltpu.VMEM((count, wide), BF16), pltpu.VMEM((8, count), jnp.int32)],
    )(info, embeddings)


def label_row(tail, first):
    turned = jnp.transpose(tail.astype(F32))
    label = turned[first : first + 1, :] * DIGIT + turned[first + 1 : first + 2, :]
    return jnp.where(turned[0:1, :] > 0, label, -1.0).astype(jnp.int32)


def label_col(tail, first):
    tail = tail.astype(F32)
    label = tail[:, first : first + 1] * DIGIT + tail[:, first + 1 : first + 2]
    return jnp.where(tail[:, 0:1] > 0, label, -1.0).astype(jnp.int32)


def add_sums(step, rows, label, sums_ref, counts_ref):
    children, count = sums_ref.shape[0], rows.shape[0]
    member = (iota((children, count), 0) == label).astype(F32).astype(BF16)
    sums = matmul(member, rows, ((1,), (0,)))
    counts = matmul(jnp.ones((EXTRA, count), BF16), member, ((1,), (1,)))

    @pl.when(step == 0)
    def _():
        sums_ref[...] = sums
        counts_ref[...] = counts

    @pl.when(step > 0)
    def _():
        sums_ref[...] += sums
        counts_ref[...] += counts


def write_blocks(out_ref, sums_ref, counts_ref):
    parts, tall, _ = out_ref.shape
    children, width = sums_ref.shape
    each = children // parts
    for j in range(width // LANES):
        piece = sums_ref[:, j * LANES : (j + 1) * LANES].astype(BF16)
        out_ref[:, j * each : (j + 1) * each, :] = piece.reshape(parts, each, LANES)
    counts = counts_ref[...].astype(BF16)
    for h in range(parts):
        chunk = h * each // LANES * LANES
        out_ref[h, tall - EXTRA :, :] = counts[:, chunk : chunk + LANES]


def first_body(arrived_ref, rows_ref, out_ref, sums_ref, counts_ref):
    count, wide = rows_ref.shape
    step = pl.program_id(0)
    rows = arrived_ref[...].reshape(count, wide)
    rows_ref[...] = rows
    width = wide - LANES
    add_sums(step, rows[:, :width], label_row(rows[:, width:], 1), sums_ref, counts_ref)

    @pl.when(step == pl.num_programs(0) - 1)
    def _():
        write_blocks(out_ref, sums_ref, counts_ref)


def first_sums(arrived, children, parts, steps):
    devices, slots, wide = arrived.shape
    width = wide - LANES
    total = devices * slots
    tall = children // parts * (width // LANES) + EXTRA
    return kernel_call(
        first_body,
        "first_sums",
        2 * total * children * width,
        4 * total * wide + 2 * children * width,
        grid=(steps,),
        in_specs=[pl.BlockSpec((devices // steps, slots, wide), lambda i: (i, 0, 0))],
        out_specs=[
            pl.BlockSpec((total // steps, wide), lambda i: (i, 0)),
            whole((parts, tall, LANES)),
        ],
        out_shape=[
            jax.ShapeDtypeStruct((total, wide), BF16),
            jax.ShapeDtypeStruct((parts, tall, LANES), BF16),
        ],
        scratch_shapes=[pltpu.VMEM((children, width), F32), pltpu.VMEM((EXTRA, children), F32)],
    )(arrived)


def margin_body(first, rows_ref, tail_ref, cents_ref, squares_ref, out_ref, costs_ref):
    step = pl.program_id(0)
    products = matmul(rows_ref[...], cents_ref[...], ((1,), (1,)))
    scores = squares_ref[...] - 2.0 * products
    member = iota(scores.shape, 1) == label_col(tail_ref[...], first)
    assigned = jnp.sum(jnp.where(member, scores, 0.0), axis=1, keepdims=True)
    margin = assigned - jnp.min(scores, axis=1, keepdims=True)
    costs = jnp.sum(jnp.where(member, margin, 0.0), axis=0, keepdims=True)

    @pl.when(step == 0)
    def _():
        costs_ref[...] = jnp.broadcast_to(costs, costs_ref.shape)

    @pl.when(step > 0)
    def _():
        costs_ref[...] += jnp.broadcast_to(costs, costs_ref.shape)

    @pl.when(step == pl.num_programs(0) - 1)
    def _():
        costs = costs_ref[0:1, :]
        high = costs.astype(BF16).astype(F32)
        chunks = costs.shape[1] // LANES
        index = iota(out_ref.shape, 0)
        out = jnp.zeros(out_ref.shape, F32)
        for q in range(chunks):
            lanes = slice(q * LANES, (q + 1) * LANES)
            out = jnp.where(index == q, high[:, lanes], out)
            out = jnp.where(index == q + chunks, (costs - high)[:, lanes], out)
        out_ref[...] = out.astype(BF16)


def margins(rows, codes, centroids, squares, first, steps):
    total = rows.shape[0]
    children, width = centroids.shape
    tail_at = codes.shape[1] // LANES - 1
    return kernel_call(
        functools.partial(margin_body, first),
        "margins",
        2 * total * children * width,
        2 * (total + children) * width,
        grid=(steps,),
        in_specs=[
            pl.BlockSpec((total // steps, width), lambda i: (i, 0)),
            pl.BlockSpec((total // steps, LANES), lambda i: (i, tail_at)),
            whole(centroids.shape),
            whole(squares.shape),
        ],
        out_specs=whole((EXTRA, LANES)),
        out_shape=jax.ShapeDtypeStruct((EXTRA, LANES), BF16),
        scratch_shapes=[pltpu.VMEM((8, children), F32)],
    )(rows, codes, centroids, squares)


def merge_body(mine_ref, arrived_ref, old_ref, costs_ref, out_ref):
    copies, tall, _ = out_ref.shape
    each, width = old_ref.shape
    total = jnp.sum(arrived_ref[...].astype(F32), axis=0)
    counts = total[tall - EXTRA : tall - EXTRA + 1, :]
    start = lax.rem(mine_ref[0] * each, LANES)
    mask = iota((each, LANES), 1) == iota((each, LANES), 0) + start
    count = jnp.sum(jnp.where(mask, counts, 0.0), axis=1, keepdims=True)
    for j in range(width // LANES):
        old = old_ref[:, j * LANES : (j + 1) * LANES].astype(F32)
        fresh = (total[j * each : (j + 1) * each, :] + old) / (count + 1.0)
        out_ref[:, j * each : (j + 1) * each, :] = jnp.broadcast_to(
            fresh.astype(BF16)[None], (copies, each, LANES)
        )
    out_ref[:, tall - EXTRA :, :] = jnp.broadcast_to(costs_ref[...][None], (copies, EXTRA, LANES))


def merge(mine, arrived, centroids, costs, copies):
    parts, tall, _ = arrived.shape
    children, width = centroids.shape
    each = children // parts
    return kernel_call(
        merge_body,
        "merge",
        arrived.size,
        2 * (arrived.size + each * width + copies * tall * LANES),
        grid_spec=pltpu.PrefetchScalarGridSpec(
            num_scalar_prefetch=1,
            grid=(1,),
            in_specs=[
                pl.BlockSpec(arrived.shape, lambda i, mine: (0, 0, 0)),
                pl.BlockSpec((each, width), lambda i, mine: (mine[0], 0)),
                pl.BlockSpec(costs.shape, lambda i, mine: (0, 0)),
            ],
            out_specs=pl.BlockSpec((copies, tall, LANES), lambda i, mine: (0, 0, 0)),
        ),
        out_shape=jax.ShapeDtypeStruct((copies, tall, LANES), BF16),
    )(mine, arrived, centroids, costs)


def cost_sum(costs, chunks):
    total = jnp.sum(costs.astype(F32), axis=0)
    return total[0:chunks, :] + total[chunks : 2 * chunks, :]


def second_body(
    core_ref, rows_ref, own_ref, other_ref, new_ref, cost_ref, residual_ref, out_ref, sums_ref, counts_ref
):
    step = pl.program_id(0)
    parts, tall, _ = own_ref.shape
    children, width = new_ref.shape
    each = children // (2 * parts)

    @pl.when(step == 0)
    def _():
        core = core_ref[0]
        for ref, side in ((own_ref, core), (other_ref, 1 - core)):
            for y in range(parts):
                at = pl.ds(pl.multiple_of((2 * y + side) * each, each), each)
                for j in range(width // LANES):
                    new_ref[at, j * LANES : (j + 1) * LANES] = ref[y, j * each : (j + 1) * each, :]
        chunks = children // LANES
        cost_ref[...] = cost_sum(own_ref[:, tall - EXTRA :, :], chunks) + cost_sum(
            other_ref[:, tall - EXTRA :, :], chunks
        )

    rows = rows_ref[:, :width]
    tail = rows_ref[:, width:]
    count = rows.shape[0]
    picked = (iota((count, children), 1) == label_col(tail, 1)).astype(F32).astype(BF16)
    center = matmul(picked, new_ref[...], ((1,), (0,)))
    residual = (rows.astype(F32) - center).astype(BF16)
    residual_ref[...] = residual
    add_sums(step, residual, label_row(tail, 3), sums_ref, counts_ref)

    @pl.when(step == pl.num_programs(0) - 1)
    def _():
        write_blocks(out_ref, sums_ref, counts_ref)


def second_sums(core, rows, own, other, children, parts, steps):
    total, wide = rows.shape
    width = wide - LANES
    tall = children // parts * (width // LANES) + EXTRA
    chunks = children // LANES
    fixed = lambda shape: pl.BlockSpec(shape, lambda i, core: (0,) * len(shape))
    return kernel_call(
        second_body,
        "second_sums",
        4 * total * children * width,
        4 * total * wide + 6 * children * width,
        grid_spec=pltpu.PrefetchScalarGridSpec(
            num_scalar_prefetch=1,
            grid=(steps,),
            in_specs=[
                pl.BlockSpec((total // steps, wide), lambda i, core: (i, 0)),
                fixed(own.shape),
                fixed(other.shape),
            ],
            out_specs=[
                fixed((children, width)),
                fixed((chunks, LANES)),
                pl.BlockSpec((total // steps, width), lambda i, core: (i, 0)),
                fixed((parts, tall, LANES)),
            ],
            scratch_shapes=[
                pltpu.VMEM((children, width), F32),
                pltpu.VMEM((EXTRA, children), F32),
            ],
        ),
        out_shape=[
            jax.ShapeDtypeStruct((children, width), BF16),
            jax.ShapeDtypeStruct((chunks, LANES), F32),
            jax.ShapeDtypeStruct((total, width), BF16),
            jax.ShapeDtypeStruct((parts, tall, LANES), BF16),
        ],
    )(core, rows, own, other)


def last_body(full_ref, new_ref, cost_ref):
    parts, tall, _ = full_ref.shape
    children, width = new_ref.shape
    each = children // parts
    for j in range(width // LANES):
        piece = full_ref[:, j * each : (j + 1) * each, :]
        new_ref[:, j * LANES : (j + 1) * LANES] = piece.reshape(children, LANES)
    cost_ref[...] = cost_sum(full_ref[:, tall - EXTRA :, :], children // LANES)


def last(full, children, width):
    return kernel_call(
        last_body,
        "last",
        full.size,
        4 * full.size,
        out_shape=[
            jax.ShapeDtypeStruct((children, width), BF16),
            jax.ShapeDtypeStruct((children // LANES, LANES), F32),
        ],
    )(full)


def squares_of(centroids):
    cent_f = centroids.astype(F32)
    return jnp.sum(cent_f * cent_f, axis=1)[None, :]


def local(embeddings, cluster_key, child_first, child_second, coarse_centroids, fine_centroids):
    n_shard = lax.axis_size(SHARD)
    n_group = lax.axis_size(GROUP)
    rows_dev = embeddings.shape[0]
    children = coarse_centroids.shape[1]
    width = embeddings.shape[1]
    devices = n_shard * n_group
    steps = max(1, devices // 128)
    coarse, fine = coarse_centroids[0], fine_centroids[0]
    core = lax.axis_index("core").astype(jnp.int32)[None]
    group = lax.axis_index(GROUP).astype(jnp.int32)[None]
    shard = lax.axis_index(SHARD).astype(jnp.int32)[None]

    info = jnp.stack(
        [cluster_key[:, 0], child_first, child_second] + [jnp.zeros((rows_dev,), jnp.int32)] * 5
    )
    layout = place(info, embeddings, devices, steps)
    arrived = exchange(layout, ALL)

    rows, partial_one = first_sums(arrived, children, n_group, steps)
    parts_one = exchange(partial_one, GROUP)
    costs_one = margins(rows, rows, coarse, squares_of(coarse), 1, steps)
    copies_one = merge(group, parts_one, coarse, costs_one, lax.axis_size("y"))
    own = exchange(copies_one, "y")
    other = lax.ppermute(own, "core", [(0, 1), (1, 0)])

    coarse_new, coarse_cost, residual, partial_two = second_sums(
        core, rows, own, other, children, n_shard, steps
    )
    parts_two = exchange(partial_two, SHARD)
    costs_two = margins(residual, rows, fine, squares_of(fine), 3, steps)
    copies_two = merge(shard, parts_two, fine, costs_two, n_shard)
    fine_new, fine_cost = last(exchange(copies_two, SHARD), children, width)
    return (
        coarse_new[None],
        fine_new[None],
        coarse_cost.reshape(1, children),
        fine_cost.reshape(1, children),
    )


def solution(mesh):
    torus = Mesh(mesh.devices.reshape(-1, 4, mesh.shape["group"] // 2, 2), ALL)
    placed = (
        P(ALL, None),
        P(ALL, None),
        P(ALL),
        P(ALL),
        P(SHARD, None, None),
        P(GROUP, None, None),
    )
    return jax.shard_map(
        local,
        mesh=torus,
        in_specs=placed,
        out_specs=(
            P(SHARD, None, None),
            P(GROUP, None, None),
            P(SHARD, None),
            P(GROUP, None),
        ),
        check_vma=False,
    )
```

time: 257 us -> 238 us (0.926)
  blocking collectives: 22.1 us -> 136 us
  waiting for transfers between devices: 142 us -> 52.3 us
  starting transfers between devices: 43.3 us -> 16.2 us
  Pallas kernels: 0 us -> 22.9 us
  matrix products: 16.7 us -> 0 us
  other arithmetic: 10.6 us -> 0.56 us
  local copies, waits for them, and re-layouts: 16.7 us -> 6.91 us
    all_to_all x1 -> x3, blocking collectives: 22.1 us -> 136 us  [exchange(): return lax.all_to_all(blocks, axes, split_axis=0, concat_axis=0, tiled=True)]
    all_to_all x4 -> x2, waiting for transfers between devices: 140 us -> 50.4 us  [exchange(): return lax.all_to_all(blocks, axes, split_axis=0, concat_axis=0, tiled=True)]
    all_to_all x4 -> x2, starting transfers between devices: 41.4 us -> 14.3 us  [exchange(): return lax.all_to_all(blocks, axes, split_axis=0, concat_axis=0, tiled=True)]
    pallas_call x0 -> x8, Pallas kernels: none -> 22.9 us  [the longest x1 7.06 us: second_sums(): kernel_call(second_body, 'second_sums', 4 * total * children * width, 4 *...]
    dot_general x6 -> x0, matrix products: 16.7 us -> none  [the longest x2 8.65 us: level_sums(): lax.dot_general(member.astype(jnp.bfloat16), jnp.concatenate([rows, extra...]
    reshape x2 -> x0, local copies, waits for them, and re-layouts: 7.34 us -> none  [the longest x1 5.01 us: local(): arrived = arrived.reshape(slots, width + EXTRA)]
    add x6 -> x0, other arithmetic: 4.12 us -> none  [the longest x2 1.63 us: cost_of(): return tail[:, 0] + tail[:, 1]]
    broadcast_in_dim x4 -> x0, local copies, waits for them, and re-layouts: 3.37 us -> none  [the longest x2 1.14 us: spread(): return exchange(jnp.broadcast_to(block[None], (parts,) + block.shape), axes)]
  transfers between devices with their start and end apart: 5 -> 3, of which waited for: 5 -> 3; matrix products, arithmetic and copies ran while one was open for 1% -> 0% of each run, Pallas kernels for 0% -> 2%
where the time goes in v2:
time: 238 us; the launch traced here: 236 us
  blocking collectives  136 us (57%)
  waiting for transfers between devices  52.3 us (22%)
  Pallas kernels  22.9 us (10%)
  starting transfers between devices  16.2 us (7%)
  local copies, waits for them, and re-layouts  6.91 us (3%)
    all_to_all x3, blocking collectives, exchange(): return lax.all_to_all(blocks, axes, split_axis=0, concat_axis=0, tiled=True)  136 us
    all_to_all x2, waiting for transfers between devices, exchange(): return lax.all_to_all(blocks, axes, split_axis=0, concat_axis=0, tiled=True)  50.4 us
    all_to_all x2, starting transfers between devices, exchange(): return lax.all_to_all(blocks, axes, split_axis=0, concat_axis=0, tiled=True)  14.3 us
    pallas_call x1, Pallas kernels, second_sums(): kernel_call(second_body, 'second_sums', 4 * total * children * width, 4 *...  7.06 us
    unnamed x18, local copies, waits for them, and re-layouts  6.16 us
    pallas_call x2, Pallas kernels, margins(): kernel_call(functools.partial(margin_body, first), 'margins', 2 * total *...  5.41 us
  transfers between devices with their start and end apart: 3, of which 3 were waited for; matrix products, arithmetic and copies ran while one was open for 0% of the time, Pallas kernels for 2%

profile of v2, /device:TPU:56, one launch (start us, length us, event | category | flops | bytes accessed | tf_op | source)
XLA Modules:
  0.0 235.6 jit_solution(13751265510918407606)
XLA Ops:
  0.7 0.7 stack.15.info_ref
  1.4 0.0 copy-start.8
  1.4 1.2 copy-done.8
  2.6 2.8 %place.1 = bf16[512,2,1152]{2,1,0:T(2,128)(2,1)S(1)} custom-call(s32[8,512]{1,0:T(8,128)S(1)} %stack.15.info_ref, bf16[512,1024]{1,0:T(8,128)(2,1)S(1)} %copy-done.8), custom_call_target="tpu_custom_call" | custom-call | flops 1207959552 | bytes 3407872 | tf_op jit(solution)/shard_map/place/pallas_call | solution.py:80
  5.4 76.9 %all_to_all.25.arrived_ref = bf16[512,2,1152]{2,1,0:T(2,128)(2,1)S(1)} all-to-all(bf16[512,2,1152]{2,1,0:T(2,128)(2,1)S(1)} %place.1), channel_id=1, replica_groups=mesh['z'=8,'x'=4,'y'=8,'core'=2] {'z','x','y','core'}, dimensions={0} | all-to-all | bytes 4718592 | tf_op jit(solution)/shard_map/all_to_all | solution.py:23
  82.3 3.3 %first_sums.1 = (bf16[1024,1152]{1,0:T(8,128)(2,1)S(1)}, bf16[16,272,128]{2,1,0:T(8,128)(2,1)S(1)}) custom-call(bf16[512,2,1152]{2,1,0:T(2,128)(2,1)S(1)} %all_to_all.25.arrived_ref), custom_call_target="tpu_custom_call" | custom-call | flops 1073741824 | bytes 5767168 | tf_op jit(solution)/shard_map/first_sums/pallas_call | solution.py:153
  85.6 0.0 copy-start.7
  85.6 1.0 copy-done.7
  86.6 9.3 %all-to-all-start.1 = ((bf16[16,272,128]{2,1,0:T(8,128)(2,1)}), bf16[16,272,128]{2,1,0:T(8,128)(2,1)}, u32[]{:S(2)}, u32[]{:S(2)}) async-start(bf16[16,272,128]{2,1,0:T(8,128)(2,1)} %copy-done.7), calls=%async_computation.1 | async-start | bytes 2228224 | tf_op jit(solution)/shard_map/all_to_all | solution.py:23
  96.0 0.0 copy-done.3
  96.0 0.3 multiply_reduce_fusion.1
  96.2 2.8 %margins.2.costs_ref = bf16[16,128]{1,0:T(8,128)(2,1)S(1)} custom-call(bf16[1024,1152]{1,0:T(8,128)(2,1)S(1)} %get-tuple-element.12.rows_ref.tail_ref, bf16[1024,1152]{1,0:T(8,128)(2,1)S(1)} %get-tuple-element.12.rows_ref.tail_ref, bf16[512,1024]{1,0:T(8,128)(2,1)S(1)} %bitcast.18, f32[1,512]{1,0:T(1,128)S(1)} %bitcast.21), custom_call_target="tpu_custom_call" | custom-call | flops 1073741824 | bytes 3145728 | tf_op jit(solution)/shard_map/margins/pallas_call | solution.py:207
  99.0 0.0 copy-done
  99.0 23.4 %all-to-all-done.1.arrived_ref = bf16[16,272,128]{2,1,0:T(8,128)(2,1)} async-done(((bf16[16,272,128]{2,1,0:T(8,128)(2,1)}), bf16[16,272,128]{2,1,0:T(8,128)(2,1)}, u32[]{:S(2)}, u32[]{:S(2)}) %all-to-all-start.1) | async-done | bytes 1114144 | tf_op jit(solution)/shard_map/all_to_all | solution.py:23
  122.4 1.5 merge.2
  123.9 21.8 %all_to_all.26.own_ref = bf16[8,272,128]{2,1,0:T(8,128)(2,1)S(1)} all-to-all(bf16[8,272,128]{2,1,0:T(8,128)(2,1)S(1)} %merge.2), channel_id=1, replica_groups=mesh['z'=8,'x'=4,'y'=8,'core'=2] {'y'}, dimensions={0} | all-to-all | bytes 1114112 | tf_op jit(solution)/shard_map/all_to_all | solution.py:23
  145.7 1.9 collective-permute-start
  147.6 1.9 collective-permute-done.other_ref
  149.6 7.1 %second_sums.1 = (bf16[512,1024]{1,0:T(8,128)(2,1)}, f32[4,128]{1,0:T(4,128)}, bf16[1024,1024]{1,0:T(8,128)(2,1)S(1)}, bf16[32,144,128]{2,1,0:T(8,128)(2,1)S(1)}) custom-call(s32[1]{0:T(128)} %bitcast.core_ref, bf16[1024,1152]{1,0:T(8,128)(2,1)} %copy-done, bf16[8,272,128]{2,1,0:T(8,128)(2,1)S(1)} %all_to_all.26.own_ref, ...), custom_call_target="tpu_custom_call" | custom-call | flops 2147483648 | bytes 7864320 | tf_op jit(solution)/shard_map/second_sums/pallas_call | solution.py:311
  156.6 1.3 copy-done.4
  157.9 1.0 copy-done.6
  158.9 5.0 %all-to-all-start.3 = ((bf16[32,144,128]{2,1,0:T(8,128)(2,1)}), bf16[32,144,128]{2,1,0:T(8,128)(2,1)}, u32[]{:S(2)}, u32[]{:S(2)}) async-start(bf16[32,144,128]{2,1,0:T(8,128)(2,1)} %copy-done.6), calls=%async_computation.3 | async-start | bytes 2359296 | tf_op jit(solution)/shard_map/all_to_all | solution.py:23
  163.9 0.0 copy-done.2
  164.0 0.3 multiply_reduce_fusion
  164.2 0.0 copy-done.1
  164.2 0.0 copy-start.5
  164.3 1.6 copy-done.5
  165.8 2.6 %margins.3.costs_ref = bf16[16,128]{1,0:T(8,128)(2,1)S(1)} custom-call(bf16[1024,1024]{1,0:T(8,128)(2,1)S(1)} %copy-done.5, bf16[1024,1152]{1,0:T(8,128)(2,1)S(1)} %copy-done.1, bf16[512,1024]{1,0:T(8,128)(2,1)S(1)} %bitcast.16, f32[1,512]{1,0:T(1,128)S(1)} %bitcast.20), custom_call_target="tpu_custom_call" | custom-call | flops 1073741824 | bytes 3145728 | tf_op jit(solution)/shard_map/margins/pallas_call | solution.py:207
  168.5 27.0 %all-to-all-done.3.arrived_ref = bf16[32,144,128]{2,1,0:T(8,128)(2,1)} async-done(((bf16[32,144,128]{2,1,0:T(8,128)(2,1)}), bf16[32,144,128]{2,1,0:T(8,128)(2,1)}, u32[]{:S(2)}, u32[]{:S(2)}) %all-to-all-start.3) | async-done | bytes 1179680 | tf_op jit(solution)/shard_map/all_to_all | solution.py:23
  195.5 1.5 merge.3
  197.0 37.3 %all_to_all.27.full_ref = bf16[32,144,128]{2,1,0:T(8,128)(2,1)S(1)} all-to-all(bf16[32,144,128]{2,1,0:T(8,128)(2,1)S(1)} %merge.3), channel_id=1, replica_groups=mesh['z'=8,'x'=4,'y'=8,'core'=2] {'z','x'}, dimensions={0} | all-to-all | bytes 2359296 | tf_op jit(solution)/shard_map/all_to_all | solution.py:23
  234.3 1.3 last.1
  (8 shorter events, 0.0 us)
Async XLA Ops:
  1.4 1.2 copy-start.8
  85.6 1.0 copy-start.7
  86.6 12.4 %copy-start = (bf16[1024,1152]{1,0:T(8,128)(2,1)}, bf16[1024,1152]{1,0:T(8,128)(2,1)S(1)}, u32[]{:S(2)}) copy-start(bf16[1024,1152]{1,0:T(8,128)(2,1)S(1)} %get-tuple-element.12.rows_ref.tail_ref) | copy-start | bytes 7077892
  86.6 9.3 %copy-start.3 = (bf16[1,512,1024]{2,1,0:T(8,128)(2,1)S(1)}, bf16[1,512,1024]{2,1,0:T(8,128)(2,1)}, u32[]{:S(2)}) copy-start(bf16[1,512,1024]{2,1,0:T(8,128)(2,1)} %param.10) | copy-start | bytes 3145732
  86.6 35.8 %all-to-all-start.1 = ((bf16[16,272,128]{2,1,0:T(8,128)(2,1)}), bf16[16,272,128]{2,1,0:T(8,128)(2,1)}, u32[]{:S(2)}, u32[]{:S(2)}) async-start(bf16[16,272,128]{2,1,0:T(8,128)(2,1)} %copy-done.7), calls=%async_computation.1 | async-start | bytes 2228224 | tf_op jit(solution)/shard_map/all_to_all | solution.py:23
  145.7 3.8 %collective-permute-start = (bf16[8,272,128]{2,1,0:T(8,128)(2,1)S(1)}, bf16[8,272,128]{2,1,0:T(8,128)(2,1)S(1)}, u32[]{:S(2)}, u32[]{:S(2)}) collective-permute-start(bf16[8,272,128]{2,1,0:T(8,128)(2,1)S(1)} %all_to_all.26.own_ref), channel_id=1, source_target_pairs={{0,1},{1,0},{2,3},{3,2},{4,5},{5,4},{6,7},{7,6},{8,9},{9,8},{10,11... | collective-permute-start | bytes 1671176 | tf_op jit(solution)/shard_map/ppermute | solution.py:396
  149.5 14.4 %copy-start.2 = (bf16[1,512,1024]{2,1,0:T(8,128)(2,1)S(1)}, bf16[1,512,1024]{2,1,0:T(8,128)(2,1)}, u32[]{:S(2)}) copy-start(bf16[1,512,1024]{2,1,0:T(8,128)(2,1)} %param.11) | copy-start | bytes 3145732
  156.6 1.3 copy-start.4
  157.9 1.0 copy-start.6
  158.9 5.3 %copy-start.1 = (bf16[1024,1152]{1,0:T(8,128)(2,1)S(1)}, bf16[1024,1152]{1,0:T(8,128)(2,1)}, u32[]{:S(2)}) copy-start(bf16[1024,1152]{1,0:T(8,128)(2,1)} %copy-done) | copy-start | bytes 7077892
  158.9 36.5 %all-to-all-start.3 = ((bf16[32,144,128]{2,1,0:T(8,128)(2,1)}), bf16[32,144,128]{2,1,0:T(8,128)(2,1)}, u32[]{:S(2)}, u32[]{:S(2)}) async-start(bf16[32,144,128]{2,1,0:T(8,128)(2,1)} %copy-done.6), calls=%async_computation.3 | async-start | bytes 2359296 | tf_op jit(solution)/shard_map/all_to_all | solution.py:23
  164.2 1.6 copy-start.5

commit v3 on v2

--- a/solution.py
+++ b/solution.py
@@ -11,6 +11,7 @@
 SHARD = ("z", "x")
 GROUP = ("y", "core")
 ALL = SHARD + GROUP
+SWAP = [(0, 1), (1, 0)]
 SLOTS = 2
 LANES = 128
 EXTRA = 16
@@ -36,7 +37,7 @@
         body,
         name=name,
         cost_estimate=pl.CostEstimate(flops=flops, bytes_accessed=moved, transcendentals=0),
-        compiler_params=pltpu.CompilerParams(vmem_limit_bytes=48 * 2**20),
+        compiler_params=pltpu.CompilerParams(vmem_limit_bytes=24 * 2**20),
         **rest,
     )
 
@@ -132,7 +133,24 @@
         out_ref[h, tall - EXTRA :, :] = counts[:, chunk : chunk + LANES]
 
 
-def first_body(arrived_ref, rows_ref, out_ref, sums_ref, counts_ref):
+def write_halves(core, keep_ref, send_ref, sums_ref, counts_ref):
+    parts, tall, _ = keep_ref.shape
+    children, width = sums_ref.shape
+    each = children // (2 * parts)
+    even = core == 0
+    for j in range(width // LANES):
+        rows = slice(j * each, (j + 1) * each)
+        piece = sums_ref[:, j * LANES : (j + 1) * LANES].reshape(parts, 2, each, LANES)
+        keep_ref[:, rows, :] = jnp.where(even, piece[:, 0], piece[:, 1]).astype(BF16)
+        send_ref[:, rows, :] = jnp.where(even, piece[:, 1], piece[:, 0]).astype(BF16)
+    for y in range(parts):
+        chunks = [(2 * y + side) * each // LANES * LANES for side in range(2)]
+        zero, one = [counts_ref[:, chunk : chunk + LANES] for chunk in chunks]
+        keep_ref[y, tall - EXTRA :, :] = jnp.where(even, zero, one).astype(BF16)
+        send_ref[y, tall - EXTRA :, :] = jnp.where(even, one, zero).astype(BF16)
+
+
+def first_body(core_ref, arrived_ref, rows_ref, keep_ref, send_ref, sums_ref, counts_ref):
     count, wide = rows_ref.shape
     step = pl.program_id(0)
     rows = arrived_ref[...].reshape(count, wide)
@@ -142,31 +160,39 @@
 
     @pl.when(step == pl.num_programs(0) - 1)
     def _():
-        write_blocks(out_ref, sums_ref, counts_ref)
-
-
-def first_sums(arrived, children, parts, steps):
+        write_halves(core_ref[0], keep_ref, send_ref, sums_ref, counts_ref)
+
+
+def first_sums(core, arrived, children, parts, steps):
     devices, slots, wide = arrived.shape
     width = wide - LANES
     total = devices * slots
-    tall = children // parts * (width // LANES) + EXTRA
+    half = (parts // 2, children // parts * (width // LANES) + EXTRA, LANES)
     return kernel_call(
         first_body,
         "first_sums",
         2 * total * children * width,
         4 * total * wide + 2 * children * width,
-        grid=(steps,),
-        in_specs=[pl.BlockSpec((devices // steps, slots, wide), lambda i: (i, 0, 0))],
-        out_specs=[
-            pl.BlockSpec((total // steps, wide), lambda i: (i, 0)),
-            whole((parts, tall, LANES)),
-        ],
+        grid_spec=pltpu.PrefetchScalarGridSpec(
+            num_scalar_prefetch=1,
+            grid=(steps,),
+            in_specs=[pl.BlockSpec((devices // steps, slots, wide), lambda i, core: (i, 0, 0))],
+            out_specs=[
+                pl.BlockSpec((total // steps, wide), lambda i, core: (i, 0)),
+                whole(half),
+                whole(half),
+            ],
+            scratch_shapes=[
+                pltpu.VMEM((children, width), F32),
+                pltpu.VMEM((EXTRA, children), F32),
+            ],
+        ),
         out_shape=[
             jax.ShapeDtypeStruct((total, wide), BF16),
-            jax.ShapeDtypeStruct((parts, tall, LANES), BF16),
+            jax.ShapeDtypeStruct(half, BF16),
+            jax.ShapeDtypeStruct(half, BF16),
         ],
-        scratch_shapes=[pltpu.VMEM((children, width), F32), pltpu.VMEM((EXTRA, children), F32)],
-    )(arrived)
+    )(core, arrived)
 
 
 def margin_body(first, rows_ref, tail_ref, cents_ref, squares_ref, out_ref, costs_ref):
@@ -240,9 +266,9 @@
 
 
 def merge(mine, arrived, centroids, costs, copies):
-    parts, tall, _ = arrived.shape
-    children, width = centroids.shape
-    each = children // parts
+    tall = arrived.shape[1]
+    width = centroids.shape[1]
+    each = (tall - EXTRA) // (width // LANES)
     return kernel_call(
         merge_body,
         "merge",
@@ -307,7 +333,6 @@
     width = wide - LANES
     tall = children // parts * (width // LANES) + EXTRA
     chunks = children // LANES
-    fixed = lambda shape: pl.BlockSpec(shape, lambda i, core: (0,) * len(shape))
     return kernel_call(
         second_body,
         "second_sums",
@@ -318,14 +343,14 @@
             grid=(steps,),
             in_specs=[
                 pl.BlockSpec((total // steps, wide), lambda i, core: (i, 0)),
-                fixed(own.shape),
-                fixed(other.shape),
+                whole(own.shape),
+                whole(other.shape),
             ],
             out_specs=[
-                fixed((children, width)),
-                fixed((chunks, LANES)),
+                whole((children, width)),
+                whole((chunks, LANES)),
                 pl.BlockSpec((total // steps, width), lambda i, core: (i, 0)),
-                fixed((parts, tall, LANES)),
+                whole((parts, tall, LANES)),
             ],
             scratch_shapes=[
                 pltpu.VMEM((children, width), F32),
@@ -388,12 +413,13 @@
     layout = place(info, embeddings, devices, steps)
     arrived = exchange(layout, ALL)
 
-    rows, partial_one = first_sums(arrived, children, n_group, steps)
-    parts_one = exchange(partial_one, GROUP)
+    rows, keep, send = first_sums(core, arrived, children, n_group, steps)
+    taken = lax.ppermute(send, "core", SWAP)
+    parts_one = exchange((keep.astype(F32) + taken.astype(F32)).astype(BF16), "y")
     costs_one = margins(rows, rows, coarse, squares_of(coarse), 1, steps)
     copies_one = merge(group, parts_one, coarse, costs_one, lax.axis_size("y"))
     own = exchange(copies_one, "y")
-    other = lax.ppermute(own, "core", [(0, 1), (1, 0)])
+    other = lax.ppermute(own, "core", SWAP)
 
     coarse_new, coarse_cost, residual, partial_two = second_sums(
         core, rows, own, other, children, n_shard, steps

time: 238 us -> 234 us (0.983)
  blocking collectives: 136 us -> 60.3 us
  waiting for transfers between devices: 52.3 us -> 97.4 us
  starting transfers between devices: 16.2 us -> 39.6 us
  local copies, waits for them, and re-layouts: 6.91 us -> 10.4 us
    all_to_all x3 -> x2, blocking collectives: 136 us -> 60.3 us  [exchange(): return lax.all_to_all(blocks, axes, split_axis=0, concat_axis=0, tiled=True)]
    all_to_all x2 -> x3, waiting for transfers between devices: 50.4 us -> 93.9 us  [exchange(): return lax.all_to_all(blocks, axes, split_axis=0, concat_axis=0, tiled=True)]
    all_to_all x2 -> x3, starting transfers between devices: 14.3 us -> 33.8 us  [exchange(): return lax.all_to_all(blocks, axes, split_axis=0, concat_axis=0, tiled=True)]
    ppermute x1 -> x2, starting transfers between devices: 1.91 us -> 5.82 us  [the longest x1 3.91 us: local(): taken = lax.ppermute(send, 'core', SWAP)]
    unnamed x18, local copies, waits for them, and re-layouts: 6.16 us -> 9.68 us
  transfers between devices with their start and end apart: 3 -> 5, of which waited for: 3 -> 5; matrix products, arithmetic and copies ran while one was open for 0% -> 0% of each run, Pallas kernels for 2% -> 2%
where the time goes in v3:
time: 234 us; the launch traced here: 232 us
  waiting for transfers between devices  97.4 us (42%)
  blocking collectives  60.3 us (26%)
  starting transfers between devices  39.6 us (17%)
  Pallas kernels  21.5 us (9%)
  local copies, waits for them, and re-layouts  10.4 us (4%)
    all_to_all x3, waiting for transfers between devices, exchange(): return lax.all_to_all(blocks, axes, split_axis=0, concat_axis=0, tiled=True)  93.9 us
    all_to_all x2, blocking collectives, exchange(): return lax.all_to_all(blocks, axes, split_axis=0, concat_axis=0, tiled=True)  60.3 us
    all_to_all x3, starting transfers between devices, exchange(): return lax.all_to_all(blocks, axes, split_axis=0, concat_axis=0, tiled=True)  33.8 us
    unnamed x18, local copies, waits for them, and re-layouts  9.68 us
    pallas_call x1, Pallas kernels, second_sums(): kernel_call(second_body, 'second_sums', 4 * total * children * width, 4 *...  5.86 us
    pallas_call x2, Pallas kernels, margins(): kernel_call(functools.partial(margin_body, first), 'margins', 2 * total *...  5.45 us
  transfers between devices with their start and end apart: 5, of which 5 were waited for; matrix products, arithmetic and copies ran while one was open for 0% of the time, Pallas kernels for 2%

profile of v3, /device:TPU:56, one launch (start us, length us, event | category | flops | bytes accessed | tf_op | source)
XLA Modules:
  0.0 231.5 jit_solution(3806427787675567672)
XLA Ops:
  0.7 0.7 stack.15.info_ref
  1.4 1.2 copy-done.8
  2.6 2.8 %place.1 = bf16[512,2,1152]{2,1,0:T(2,128)(2,1)S(1)} custom-call(s32[8,512]{1,0:T(8,128)S(1)} %stack.15.info_ref, bf16[512,1024]{1,0:T(8,128)(2,1)S(1)} %copy-done.8), custom_call_target="tpu_custom_call" | custom-call | flops 1207959552 | bytes 3407872 | tf_op jit(solution)/shard_map/place/pallas_call | solution.py:81
  5.4 1.4 copy-done.4
  6.8 20.7 %all-to-all-start = ((bf16[512,2,1152]{2,1,0:T(2,128)(2,1)}), bf16[512,2,1152]{2,1,0:T(2,128)(2,1)S(1)}, u32[]{:S(2)}, u32[]{:S(2)}) async-start(bf16[512,2,1152]{2,1,0:T(2,128)(2,1)} %copy-done.4), calls=%async_computation | async-start | bytes 4718592 | tf_op jit(solution)/shard_map/all_to_all | solution.py:24
  27.6 56.3 %all-to-all-done.arrived_ref = bf16[512,2,1152]{2,1,0:T(2,128)(2,1)S(1)} async-done(((bf16[512,2,1152]{2,1,0:T(2,128)(2,1)}), bf16[512,2,1152]{2,1,0:T(2,128)(2,1)S(1)}, u32[]{:S(2)}, u32[]{:S(2)}) %all-to-all-start) | async-done | bytes 2359328 | tf_op jit(solution)/shard_map/all_to_all | solution.py:24
  84.0 1.4 copy-done.2
  85.4 1.7 copy-done.3
  87.1 3.4 %first_sums.1 = (bf16[1024,1152]{1,0:T(8,128)(2,1)S(1)}, bf16[8,272,128]{2,1,0:T(8,128)(2,1)S(1)}, bf16[8,272,128]{2,1,0:T(8,128)(2,1)S(1)}) custom-call(s32[1]{0:T(128)} %bitcast.core_ref, bf16[512,2,1152]{2,1,0:T(2,128)(2,1)S(1)} %copy-done.3), custom_call_target="tpu_custom_call" | custom-call | flops 1073741824 | bytes 5767168 | tf_op jit(solution)/shard_map/first_sums/pallas_call | solution.py:171
  90.5 0.0 copy-start.1
  90.5 3.9 %collective-permute-start = (bf16[8,272,128]{2,1,0:T(8,128)(2,1)S(1)}, bf16[8,272,128]{2,1,0:T(8,128)(2,1)S(1)}, u32[]{:S(2)}, u32[]{:S(2)}) collective-permute-start(bf16[8,272,128]{2,1,0:T(8,128)(2,1)S(1)} %get-tuple-element.15), channel_id=1, source_target_pairs={{0,1},{1,0},{2,3},{3,2},{4,5},{5,4},{6,7},{7,6},{8,9},{9,8},{10,11... | collective-permute-start | bytes 1671176 | tf_op jit(solution)/shard_map/ppermute | solution.py:417
  94.4 1.6 collective-permute-done
  96.0 0.9 add_convert_fusion
  96.9 7.4 %all-to-all-start.1 = ((bf16[8,272,128]{2,1,0:T(8,128)(2,1)}), bf16[8,272,128]{2,1,0:T(8,128)(2,1)}, u32[]{:S(2)}, u32[]{:S(2)}) async-start(bf16[8,272,128]{2,1,0:T(8,128)(2,1)} %add_convert_fusion), calls=%async_computation.1 | async-start | bytes 1114112 | tf_op jit(solution)/shard_map/all_to_all | solution.py:24
  104.4 0.3 multiply_reduce_fusion.1
  104.7 2.8 %margins.2.costs_ref = bf16[16,128]{1,0:T(8,128)(2,1)S(1)} custom-call(bf16[1024,1152]{1,0:T(8,128)(2,1)S(1)} %get-tuple-element.13.rows_ref.tail_ref, bf16[1024,1152]{1,0:T(8,128)(2,1)S(1)} %get-tuple-element.13.rows_ref.tail_ref, bf16[512,1024]{1,0:T(8,128)(2,1)S(1)} %bitcast.18, f32[1,512]{1,0:T(1,128)S(1)} %bitcast.21), custom_call_target="tpu_custom_call" | custom-call | flops 1073741824 | bytes 3145728 | tf_op jit(solution)/shard_map/margins/pallas_call | solution.py:233
  107.5 11.1 %all-to-all-done.1.arrived_ref = bf16[8,272,128]{2,1,0:T(8,128)(2,1)} async-done(((bf16[8,272,128]{2,1,0:T(8,128)(2,1)}), bf16[8,272,128]{2,1,0:T(8,128)(2,1)}, u32[]{:S(2)}, u32[]{:S(2)}) %all-to-all-start.1) | async-done | bytes 557088 | tf_op jit(solution)/shard_map/all_to_all | solution.py:24
  118.5 1.2 merge.2
  119.7 22.9 %all_to_all.25.own_ref = bf16[8,272,128]{2,1,0:T(8,128)(2,1)S(1)} all-to-all(bf16[8,272,128]{2,1,0:T(8,128)(2,1)S(1)} %merge.2), channel_id=1, replica_groups=mesh['z'=8,'x'=4,'y'=8,'core'=2] {'y'}, dimensions={0} | all-to-all | bytes 1114112 | tf_op jit(solution)/shard_map/all_to_all | solution.py:24
  142.6 1.9 collective-permute-start.1
  144.6 1.9 collective-permute-done.1.other_ref
  146.5 5.9 %second_sums.1 = (bf16[512,1024]{1,0:T(8,128)(2,1)}, f32[4,128]{1,0:T(4,128)}, bf16[1024,1024]{1,0:T(8,128)(2,1)S(1)}, bf16[32,144,128]{2,1,0:T(8,128)(2,1)S(1)}) custom-call(s32[1]{0:T(128)} %bitcast.core_ref, bf16[1024,1152]{1,0:T(8,128)(2,1)S(1)} %get-tuple-element.13.rows_ref.tail_ref, bf16[8,272,128]{2,1,0:T(8,128)(2,1)S(1)} %all_to_all.25.own_ref, ...), custom_call_target="tpu_custom_call" | custom-call | flops 2147483648 | bytes 7864320 | tf_op jit(solution)/shard_map/second_sums/pallas_call | solution.py:336
  152.3 1.3 copy-done.5
  153.7 1.0 copy-done.7
  154.7 5.6 %all-to-all-start.3 = ((bf16[32,144,128]{2,1,0:T(8,128)(2,1)}), bf16[32,144,128]{2,1,0:T(8,128)(2,1)}, u32[]{:S(2)}, u32[]{:S(2)}) async-start(bf16[32,144,128]{2,1,0:T(8,128)(2,1)} %copy-done.7), calls=%async_computation.3 | async-start | bytes 2359296 | tf_op jit(solution)/shard_map/all_to_all | solution.py:24
  160.3 0.3 multiply_reduce_fusion
  160.6 1.6 copy-done.6
  162.2 2.7 %margins.3.costs_ref = bf16[16,128]{1,0:T(8,128)(2,1)S(1)} custom-call(bf16[1024,1024]{1,0:T(8,128)(2,1)S(1)} %copy-done.6, bf16[1024,1152]{1,0:T(8,128)(2,1)S(1)} %get-tuple-element.13.rows_ref.tail_ref, bf16[512,1024]{1,0:T(8,128)(2,1)S(1)} %bitcast.16, f32[1,512]{1,0:T(1,128)S(1)} %bitcast.20), custom_call_target="tpu_custom_call" | custom-call | flops 1073741824 | bytes 3145728 | tf_op jit(solution)/shard_map/margins/pallas_call | solution.py:233
  164.9 26.5 %all-to-all-done.3.arrived_ref = bf16[32,144,128]{2,1,0:T(8,128)(2,1)} async-done(((bf16[32,144,128]{2,1,0:T(8,128)(2,1)}), bf16[32,144,128]{2,1,0:T(8,128)(2,1)}, u32[]{:S(2)}, u32[]{:S(2)}) %all-to-all-start.3) | async-done | bytes 1179680 | tf_op jit(solution)/shard_map/all_to_all | solution.py:24
  191.4 1.5 merge.3
  192.9 37.4 %all_to_all.26.full_ref = bf16[32,144,128]{2,1,0:T(8,128)(2,1)S(1)} all-to-all(bf16[32,144,128]{2,1,0:T(8,128)(2,1)S(1)} %merge.3), channel_id=1, replica_groups=mesh['z'=8,'x'=4,'y'=8,'core'=2] {'z','x'}, dimensions={0} | all-to-all | bytes 2359296 | tf_op jit(solution)/shard_map/all_to_all | solution.py:24
  230.3 1.3 last.1
  (12 shorter events, 0.0 us)
Async XLA Ops:
  1.4 1.2 copy-start.8
  5.4 1.4 copy-start.4
  6.8 77.1 %all-to-all-start = ((bf16[512,2,1152]{2,1,0:T(2,128)(2,1)}), bf16[512,2,1152]{2,1,0:T(2,128)(2,1)S(1)}, u32[]{:S(2)}, u32[]{:S(2)}) async-start(bf16[512,2,1152]{2,1,0:T(2,128)(2,1)} %copy-done.4), calls=%async_computation | async-start | bytes 4718592 | tf_op jit(solution)/shard_map/all_to_all | solution.py:24
  84.0 1.4 copy-start.2
  85.4 1.7 copy-start.3
  90.5 13.9 %copy-start.1 = (bf16[1,512,1024]{2,1,0:T(8,128)(2,1)S(1)}, bf16[1,512,1024]{2,1,0:T(8,128)(2,1)}, u32[]{:S(2)}) copy-start(bf16[1,512,1024]{2,1,0:T(8,128)(2,1)} %param.10) | copy-start | bytes 3145732
  90.5 5.5 %collective-permute-start = (bf16[8,272,128]{2,1,0:T(8,128)(2,1)S(1)}, bf16[8,272,128]{2,1,0:T(8,128)(2,1)S(1)}, u32[]{:S(2)}, u32[]{:S(2)}) collective-permute-start(bf16[8,272,128]{2,1,0:T(8,128)(2,1)S(1)} %get-tuple-element.15), channel_id=1, source_target_pairs={{0,1},{1,0},{2,3},{3,2},{4,5},{5,4},{6,7},{7,6},{8,9},{9,8},{10,11... | collective-permute-start | bytes 1671176 | tf_op jit(solution)/shard_map/ppermute | solution.py:417
  96.9 21.6 %all-to-all-start.1 = ((bf16[8,272,128]{2,1,0:T(8,128)(2,1)}), bf16[8,272,128]{2,1,0:T(8,128)(2,1)}, u32[]{:S(2)}, u32[]{:S(2)}) async-start(bf16[8,272,128]{2,1,0:T(8,128)(2,1)} %add_convert_fusion), calls=%async_computation.1 | async-start | bytes 1114112 | tf_op jit(solution)/shard_map/all_to_all | solution.py:24
  142.6 3.8 %collective-permute-start.1 = (bf16[8,272,128]{2,1,0:T(8,128)(2,1)S(1)}, bf16[8,272,128]{2,1,0:T(8,128)(2,1)S(1)}, u32[]{:S(2)}, u32[]{:S(2)}) collective-permute-start(bf16[8,272,128]{2,1,0:T(8,128)(2,1)S(1)} %all_to_all.25.own_ref), channel_id=1, source_target_pairs={{0,1},{1,0},{2,3},{3,2},{4,5},{5,4},{6,7},{7,6},{8,9},{9,8},{10,11... | collective-permute-start | bytes 1671176 | tf_op jit(solution)/shard_map/ppermute | solution.py:422
  152.3 1.3 copy-start.5
  153.7 1.0 copy-start.7
  154.7 5.6 %copy-start = (bf16[1,512,1024]{2,1,0:T(8,128)(2,1)S(1)}, bf16[1,512,1024]{2,1,0:T(8,128)(2,1)}, u32[]{:S(2)}) copy-start(bf16[1,512,1024]{2,1,0:T(8,128)(2,1)} %param.11) | copy-start | bytes 3145732
  154.7 36.7 %all-to-all-start.3 = ((bf16[32,144,128]{2,1,0:T(8,128)(2,1)}), bf16[32,144,128]{2,1,0:T(8,128)(2,1)}, u32[]{:S(2)}, u32[]{:S(2)}) async-start(bf16[32,144,128]{2,1,0:T(8,128)(2,1)} %copy-done.7), calls=%async_computation.3 | async-start | bytes 2359296 | tf_op jit(solution)/shard_map/all_to_all | solution.py:24
  160.6 1.6 copy-start.6

commit v4 on v1

v4 whole, which is shorter than its diff:
```python
import jax
import jax.numpy as jnp
from jax import lax
from jax.experimental import pallas as pl
from jax.experimental.pallas import tpu as pltpu
from jax.sharding import Mesh
from jax.sharding import PartitionSpec as P

SHARD = ("z", "x")
GROUP = ("y", "core")
ALL = SHARD + GROUP
SWAP = [(0, 1), (1, 0)]
SLOTS = 2
LANES = 128
EXTRA = 8
PIECES = 2
VMEM_BYTES = 32 * 2**20
DIGIT = 16
F32 = jnp.float32
BF16 = jnp.bfloat16


def exchange(blocks, axes):
    return lax.all_to_all(blocks, axes, split_axis=0, concat_axis=0, tiled=True)


def iota(shape, dim):
    return lax.broadcasted_iota(jnp.int32, shape, dim)


def matmul(a, b, dims):
    return lax.dot_general(a, b, (dims, ((), ())), preferred_element_type=F32)


def kernel_call(body, name, flops, outs, args, scalars=0, scratch=()):
    moved = sum(x.size * x.dtype.itemsize for x in list(outs) + list(args))
    specs = [pl.BlockSpec(memory_space=pltpu.SMEM)] * scalars
    specs += [pl.BlockSpec(memory_space=pltpu.VMEM)] * (len(args) - scalars)
    return pl.pallas_call(
        body,
        name=name,
        in_specs=specs,
        out_specs=[pl.BlockSpec(memory_space=pltpu.VMEM)] * len(outs),
        out_shape=list(outs),
        scratch_shapes=list(scratch),
        cost_estimate=pl.CostEstimate(flops=flops, bytes_accessed=moved, transcendentals=0),
        compiler_params=pltpu.CompilerParams(vmem_limit_bytes=VMEM_BYTES),
    )(*args)


def shaped(shape, dtype=BF16):
    return jax.ShapeDtypeStruct(shape, dtype)


def one_hot(mask):
    return mask.astype(F32).astype(BF16)


def place_body(info_ref, emb_ref, out_ref, wide_ref):
    count, width = emb_ref.shape
    devices, slots, wide = out_ref.shape
    info = info_ref[...]
    turned = jnp.transpose(info.astype(F32)).astype(jnp.int32)
    keys_row, keys_col = info[0:1, :], turned[:, 0:1]
    earlier = (keys_col == keys_row) & (iota((count, count), 0) < iota((count, count), 1))
    rank = jnp.sum(earlier.astype(jnp.int32), axis=0, keepdims=True)
    target = keys_row * slots + rank
    one, two = turned[:, 1:2], turned[:, 2:3]
    lane = iota((count, LANES), 1)
    codes = jnp.where(lane == 0, 1, 0)
    for index, value in enumerate((one // DIGIT, one % DIGIT, two // DIGIT, two % DIGIT)):
        codes = jnp.where(lane == index + 1, value, codes)
    wide_ref[:, :width] = emb_ref[...]
    wide_ref[:, width:] = codes.astype(F32).astype(BF16)
    block = devices // PIECES
    for piece in range(PIECES):
        at = iota((block * slots, count), 0) + piece * block * slots
        moved = matmul(one_hot(at == target), wide_ref[...], ((1,), (0,))).astype(BF16)
        out_ref[piece * block : (piece + 1) * block] = moved.reshape(block, slots, wide)


def place(info, embeddings, devices):
    count, width = embeddings.shape
    wide = width + LANES
    return kernel_call(
        place_body,
        "place",
        2 * devices * SLOTS * count * wide,
        [shaped((devices, SLOTS, wide))],
        [info, embeddings],
        scratch=[pltpu.VMEM((count, wide), BF16)],
    )[0]


def label_row(tail, first):
    turned = jnp.transpose(tail.astype(F32))
    label = turned[first : first + 1, :] * DIGIT + turned[first + 1 : first + 2, :]
    return jnp.where(turned[0:1, :] > 0, label, -1.0).astype(jnp.int32)


def label_col(tail, first):
    tail = tail.astype(F32)
    label = tail[:, first : first + 1] * DIGIT + tail[:, first + 1 : first + 2]
    return jnp.where(tail[:, 0:1] > 0, label, -1.0).astype(jnp.int32)


def sums_of(rows, label, children):
    count = rows.shape[0]
    member = one_hot(iota((children, count), 0) == label)
    sums = matmul(member, rows, ((1,), (0,)))
    return sums, matmul(jnp.ones((EXTRA, count), BF16), member, ((1,), (1,)))


def first_body(core_ref, arrived_ref, rows_ref, keep_ref, send_ref):
    total, wide = rows_ref.shape
    width = wide - LANES
    parts, tall, _ = keep_ref.shape
    each = (tall - EXTRA) // (width // LANES)
    children = 2 * parts * each
    rows = arrived_ref[...].reshape(total, wide)
    rows_ref[...] = rows
    sums, counts = sums_of(rows[:, :width], label_row(rows[:, width:], 1), children)
    even = core_ref[0] == 0
    for j in range(width // LANES):
        at = slice(j * each, (j + 1) * each)
        piece = sums[:, j * LANES : (j + 1) * LANES].reshape(parts, 2, each, LANES)
        keep_ref[:, at, :] = jnp.where(even, piece[:, 0], piece[:, 1]).astype(BF16)
        send_ref[:, at, :] = jnp.where(even, piece[:, 1], piece[:, 0]).astype(BF16)
    for y in range(parts):
        chunks = [(2 * y + side) * each // LANES * LANES for side in range(2)]
        zero, one = [counts[:, chunk : chunk + LANES] for chunk in chunks]
        keep_ref[y, tall - EXTRA :, :] = jnp.where(even, zero, one).astype(BF16)
        send_ref[y, tall - EXTRA :, :] = jnp.where(even, one, zero).astype(BF16)


def first_sums(core, arrived, children, parts):
    devices, slots, wide = arrived.shape
    width = wide - LANES
    total = devices * slots
    half = (parts // 2, children // parts * (width // LANES) + EXTRA, LANES)
    return kernel_call(
        first_body,
        "first_sums",
        2 * total * children * width,
        [shaped((total, wide)), shaped(half), shaped(half)],
        [core, arrived],
        scalars=1,
    )


def residual_of(rows_ref, centers_ref):
    children, width = centers_ref.shape
    rows, tail = rows_ref[:, :width], rows_ref[:, width:]
    picked = one_hot(iota((rows.shape[0], children), 1) == label_col(tail, 1))
    center = matmul(picked, centers_ref[...], ((1,), (0,)))
    return (rows.astype(F32) - center).astype(BF16)


def write_margins(rows, label, cents_ref, squares_ref, out_ref):
    scores = squares_ref[...] - 2.0 * matmul(rows, cents_ref[...], ((1,), (1,)))
    member = iota(scores.shape, 1) == label
    assigned = jnp.sum(jnp.where(member, scores, 0.0), axis=1, keepdims=True)
    margin = assigned - jnp.min(scores, axis=1, keepdims=True)
    costs = jnp.sum(jnp.where(member, margin, 0.0), axis=0, keepdims=True)
    high = costs.astype(BF16).astype(F32)
    chunks = costs.shape[1] // LANES
    index = iota(out_ref.shape, 0)
    out = jnp.zeros(out_ref.shape, F32)
    for q in range(chunks):
        lanes = slice(q * LANES, (q + 1) * LANES)
        out = jnp.where(index == q, high[:, lanes], out)
        out = jnp.where(index == q + chunks, (costs - high)[:, lanes], out)
    out_ref[...] = out.astype(BF16)


def margins_one_body(rows_ref, cents_ref, squares_ref, out_ref):
    width = cents_ref.shape[1]
    label = label_col(rows_ref[:, width:], 1)
    write_margins(rows_ref[:, :width], label, cents_ref, squares_ref, out_ref)


def margins_two_body(rows_ref, centers_ref, cents_ref, squares_ref, out_ref):
    width = cents_ref.shape[1]
    label = label_col(rows_ref[:, width:], 3)
    write_margins(residual_of(rows_ref, centers_ref), label, cents_ref, squares_ref, out_ref)


def margins(body, rows, *others):
    children, width = others[0].shape
    return kernel_call(
        body,
        "margins",
        2 * (len(others) - 1) * rows.shape[0] * children * width,
        [shaped((EXTRA, LANES))],
        [rows, *others],
    )[0]


def merge_body(mine_ref, arrived_ref, old_ref, costs_ref, out_ref):
    copies, tall, _ = out_ref.shape
    width = old_ref.shape[1]
    each = (tall - EXTRA) // (width // LANES)
    total = jnp.sum(arrived_ref[...].astype(F32), axis=0)
    counts = total[tall - EXTRA : tall - EXTRA + 1, :]
    first = mine_ref[0] * each
    mask = iota((each, LANES), 1) == iota((each, LANES), 0) + lax.rem(first, LANES)
    count = jnp.sum(jnp.where(mask, counts, 0.0), axis=1, keepdims=True)
    old_all = old_ref[pl.ds(pl.multiple_of(first, each), each), :].astype(F32)
    for j in range(width // LANES):
        old = old_all[:, j * LANES : (j + 1) * LANES]
        fresh = (total[j * each : (j + 1) * each, :] + old) / (count + 1.0)
        out_ref[:, j * each : (j + 1) * each, :] = jnp.broadcast_to(
            fresh.astype(BF16)[None], (copies, each, LANES)
        )
    out_ref[:, tall - EXTRA :, :] = jnp.broadcast_to(costs_ref[...][None], (copies, EXTRA, LANES))


def merge(mine, arrived, centroids, costs, copies):
    return kernel_call(
        merge_body,
        "merge",
        arrived.size,
        [shaped((copies,) + arrived.shape[1:])],
        [mine, arrived, centroids, costs],
        scalars=1,
    )[0]


def cost_sum(costs, chunks):
    total = jnp.sum(costs.astype(F32), axis=0)
    return total[0:chunks, :] + total[chunks : 2 * chunks, :]


def second_body(core_ref, rows_ref, own_ref, other_ref, new_ref, cost_ref, out_ref):
    parts, tall, _ = own_ref.shape
    children, width = new_ref.shape
    each = children // (2 * parts)
    core = core_ref[0]
    for ref, side in ((own_ref, core), (other_ref, 1 - core)):
        for y in range(parts):
            at = pl.ds(pl.multiple_of((2 * y + side) * each, each), each)
            for j in range(width // LANES):
                new_ref[at, j * LANES : (j + 1) * LANES] = ref[y, j * each : (j + 1) * each, :]
    chunks = children // LANES
    cost_ref[...] = cost_sum(own_ref[:, tall - EXTRA :, :], chunks) + cost_sum(
        other_ref[:, tall - EXTRA :, :], chunks
    )
    label = label_row(rows_ref[:, width:], 3)
    sums, counts = sums_of(residual_of(rows_ref, new_ref), label, children)
    parts, tall, _ = out_ref.shape
    each = children // parts
    for j in range(width // LANES):
        piece = sums[:, j * LANES : (j + 1) * LANES].astype(BF16)
        out_ref[:, j * each : (j + 1) * each, :] = piece.reshape(parts, each, LANES)
    for h in range(parts):
        chunk = h * each // LANES * LANES
        out_ref[h, tall - EXTRA :, :] = counts[:, chunk : chunk + LANES].astype(BF16)


def second_sums(core, rows, own, other, children, parts):
    total, wide = rows.shape
    width = wide - LANES
    tall = children // parts * (width // LANES) + EXTRA
    return kernel_call(
        second_body,
        "second_sums",
        4 * total * children * width,
        [
            shaped((children, width)),
            shaped((children // LANES, LANES), F32),
            shaped((parts, tall, LANES)),
        ],
        [core, rows, own, other],
        scalars=1,
    )


def last_body(full_ref, new_ref, cost_ref):
    parts, tall, _ = full_ref.shape
    children, width = new_ref.shape
    each = children // parts
    for j in range(width // LANES):
        piece = full_ref[:, j * each : (j + 1) * each, :]
        new_ref[:, j * LANES : (j + 1) * LANES] = piece.reshape(children, LANES)
    cost_ref[...] = cost_sum(full_ref[:, tall - EXTRA :, :], children // LANES)


def last(full, children, width):
    return kernel_call(
        last_body,
        "last",
        full.size,
        [shaped((children, width)), shaped((children // LANES, LANES), F32)],
        [full],
    )


def squares_of(centroids):
    cent_f = centroids.astype(F32)
    return jnp.sum(cent_f * cent_f, axis=1)[None, :]


def local(embeddings, cluster_key, child_first, child_second, coarse_centroids, fine_centroids):
    n_shard = lax.axis_size(SHARD)
    n_group = lax.axis_size(GROUP)
    rows_dev = embeddings.shape[0]
    children = coarse_centroids.shape[1]
    width = embeddings.shape[1]
    devices = n_shard * n_group
    coarse, fine = coarse_centroids[0], fine_centroids[0]
    core = lax.axis_index("core").astype(jnp.int32)[None]
    group = lax.axis_index(GROUP).astype(jnp.int32)[None]
    shard = lax.axis_index(SHARD).astype(jnp.int32)[None]

    info = jnp.stack(
        [cluster_key[:, 0], child_first, child_second] + [jnp.zeros((rows_dev,), jnp.int32)] * 5
    )
    layout = place(info, embeddings, devices)
    layout, core, group, shard = lax.optimization_barrier((layout, core, group, shard))
    arrived = exchange(layout, ALL)

    rows, keep, send = first_sums(core, arrived, children, n_group)
    taken = lax.ppermute(send, "core", SWAP)
    parts_one = exchange((keep.astype(F32) + taken.astype(F32)).astype(BF16), "y")
    costs_one = margins(margins_one_body, rows, coarse, squares_of(coarse))
    copies_one = merge(group, parts_one, coarse, costs_one, lax.axis_size("y"))
    own = exchange(copies_one, "y")
    other = lax.ppermute(own, "core", SWAP)

    coarse_new, coarse_cost, partial_two = second_sums(core, rows, own, other, children, n_shard)
    parts_two = exchange(partial_two, SHARD)
    costs_two = margins(margins_two_body, rows, coarse_new, fine, squares_of(fine))
    copies_two = merge(shard, parts_two, fine, costs_two, n_shard)
    fine_new, fine_cost = last(exchange(copies_two, SHARD), children, width)
    return (
        coarse_new[None],
        fine_new[None],
        coarse_cost.reshape(1, children),
        fine_cost.reshape(1, children),
    )


def solution(mesh):
    torus = Mesh(mesh.devices.reshape(-1, 4, mesh.shape["group"] // 2, 2), ALL)
    placed = (
        P(ALL, None),
        P(ALL, None),
        P(ALL),
        P(ALL),
        P(SHARD, None, None),
        P(GROUP, None, None),
    )
    return jax.shard_map(
        local,
        mesh=torus,
        in_specs=placed,
        out_specs=(
            P(SHARD, None, None),
            P(GROUP, None, None),
            P(SHARD, None),
            P(GROUP, None),
        ),
        check_vma=False,
    )
```

time: 257 us -> 218 us (0.85)
  blocking collectives: 22.1 us -> 136 us
  waiting for transfers between devices: 142 us -> 37.1 us
  starting transfers between devices: 43.3 us -> 18.3 us
  matrix products: 16.7 us -> 0 us
  Pallas kernels: 0 us -> 14.7 us
  local copies, waits for them, and re-layouts: 16.7 us -> 6.73 us
  other arithmetic: 10.6 us -> 1.5 us
    all_to_all x1 -> x3, blocking collectives: 22.1 us -> 136 us  [exchange(): return lax.all_to_all(blocks, axes, split_axis=0, concat_axis=0, tiled=True)]
    all_to_all x4 -> x2, waiting for transfers between devices: 140 us -> 33.7 us  [exchange(): return lax.all_to_all(blocks, axes, split_axis=0, concat_axis=0, tiled=True)]
    all_to_all x4 -> x2, starting transfers between devices: 41.4 us -> 12.5 us  [exchange(): return lax.all_to_all(blocks, axes, split_axis=0, concat_axis=0, tiled=True)]
    dot_general x6 -> x0, matrix products: 16.7 us -> none  [the longest x2 8.65 us: level_sums(): lax.dot_general(member.astype(jnp.bfloat16), jnp.concatenate([rows, extra...]
    pallas_call x0 -> x8, Pallas kernels: none -> 14.7 us  [kernel_call(): pl.pallas_call(body, name=name, in_specs=specs, out_specs=[pl.BlockSpec(m...]
    reshape x2 -> x0, local copies, waits for them, and re-layouts: 7.34 us -> none  [the longest x1 5.01 us: local(): arrived = arrived.reshape(slots, width + EXTRA)]
    add x6 -> x0, other arithmetic: 4.12 us -> none  [the longest x2 1.63 us: cost_of(): return tail[:, 0] + tail[:, 1]]
    ppermute x1 -> x2, starting transfers between devices: 1.91 us -> 5.82 us  [the longest x1 3.91 us: local(): taken = lax.ppermute(send, 'core', SWAP)]
  transfers between devices with their start and end apart: 5 -> 4, of which waited for: 5 -> 4; matrix products, arithmetic and copies ran while one was open for 1% -> 0% of each run, Pallas kernels for 0% -> 2%
where the time goes in v4:
time: 218 us; the launch traced here: 216 us
  blocking collectives  136 us (62%)
  waiting for transfers between devices  37.1 us (17%)
  starting transfers between devices  18.3 us (8%)
  Pallas kernels  14.7 us (7%)
  local copies, waits for them, and re-layouts  6.73 us (3%)
    all_to_all x3, blocking collectives, exchange(): return lax.all_to_all(blocks, axes, split_axis=0, concat_axis=0, tiled=True)  136 us
    all_to_all x2, waiting for transfers between devices, exchange(): return lax.all_to_all(blocks, axes, split_axis=0, concat_axis=0, tiled=True)  33.7 us
    pallas_call x8, Pallas kernels, kernel_call(): pl.pallas_call(body, name=name, in_specs=specs, out_specs=[pl.BlockSpec(m...  14.7 us
    all_to_all x2, starting transfers between devices, exchange(): return lax.all_to_all(blocks, axes, split_axis=0, concat_axis=0, tiled=True)  12.5 us
    unnamed x16, local copies, waits for them, and re-layouts  5.98 us
  transfers between devices with their start and end apart: 4, of which 4 were waited for; matrix products, arithmetic and copies ran while one was open for 0% of the time, Pallas kernels for 2%

profile of v4, /device:TPU:56, one launch (start us, length us, event | category | flops | bytes accessed | tf_op | source)
XLA Modules:
  0.0 215.5 jit_solution(8298830690225080587)
XLA Ops:
  0.7 0.7 stack.15.info_ref
  1.4 0.0 copy-start.2
  1.4 1.2 copy-done.2
  2.6 2.0 place.1
  4.7 76.9 %all_to_all.25.arrived_ref = bf16[512,2,1152]{2,1,0:T(2,128)(2,1)S(1)} all-to-all(bf16[512,2,1152]{2,1,0:T(2,128)(2,1)S(1)} %place.1), channel_id=1, replica_groups=mesh['z'=8,'x'=4,'y'=8,'core'=2] {'z','x','y','core'}, dimensions={0} | all-to-all | bytes 4718592 | tf_op jit(solution)/shard_map/all_to_all | solution.py:24
  81.6 1.9 first_sums.1
  83.4 1.4 copy-done.4
  84.9 3.9 %collective-permute-start = (bf16[8,264,128]{2,1,0:T(8,128)(2,1)S(1)}, bf16[8,264,128]{2,1,0:T(8,128)(2,1)S(1)}, u32[]{:S(2)}, u32[]{:S(2)}) collective-permute-start(bf16[8,264,128]{2,1,0:T(8,128)(2,1)S(1)} %get-tuple-element.21), channel_id=1, source_target_pairs={{0,1},{1,0},{2,3},{3,2},{4,5},{5,4},{6,7},{7,6},{8,9},{9,8},{10,11... | collective-permute-start | bytes 1622024 | tf_op jit(solution)/shard_map/ppermute | solution.py:323
  88.8 1.5 collective-permute-done
  90.3 0.9 add_convert_fusion
  91.3 6.8 %all-to-all-start.1 = ((bf16[8,264,128]{2,1,0:T(8,128)(2,1)}), bf16[8,264,128]{2,1,0:T(8,128)(2,1)S(1)}, u32[]{:S(2)}, u32[]{:S(2)}) async-start(bf16[8,264,128]{2,1,0:T(8,128)(2,1)} %add_convert_fusion), calls=%async_computation.1 | async-start | bytes 1081344 | tf_op jit(solution)/shard_map/all_to_all | solution.py:24
  98.1 0.0 copy-done.1
  98.1 0.3 multiply_reduce_fusion.1
  98.4 1.7 copy-done.5
  100.0 1.8 margins.2.costs_ref
  101.8 9.4 %all-to-all-done.1.arrived_ref = bf16[8,264,128]{2,1,0:T(8,128)(2,1)S(1)} async-done(((bf16[8,264,128]{2,1,0:T(8,128)(2,1)}), bf16[8,264,128]{2,1,0:T(8,128)(2,1)S(1)}, u32[]{:S(2)}, u32[]{:S(2)}) %all-to-all-start.1) | async-done | bytes 540704 | tf_op jit(solution)/shard_map/all_to_all | solution.py:24
  111.2 0.1 merge.2
  111.3 23.4 %all_to_all.26.own_ref = bf16[8,264,128]{2,1,0:T(8,128)(2,1)S(1)} all-to-all(bf16[8,264,128]{2,1,0:T(8,128)(2,1)S(1)} %merge.2), channel_id=1, replica_groups=mesh['z'=8,'x'=4,'y'=8,'core'=2] {'y'}, dimensions={0} | all-to-all | bytes 1081344 | tf_op jit(solution)/shard_map/all_to_all | solution.py:24
  134.8 1.9 collective-permute-start.1
  136.7 1.9 collective-permute-done.1.other_ref
  138.6 0.0 copy-done.6
  138.6 4.0 %second_sums.1 = (bf16[512,1024]{1,0:T(8,128)(2,1)}, f32[4,128]{1,0:T(4,128)}, bf16[32,136,128]{2,1,0:T(8,128)(2,1)}) custom-call(s32[1]{0:T(128)} %bitcast.3.core_ref, bf16[1024,1152]{1,0:T(8,128)(2,1)S(1)} %copy-done.6, bf16[8,264,128]{2,1,0:T(8,128)(2,1)S(1)} %all_to_all.26.own_ref, bf16[8,264,128]{2,1,0:T(8,128)(2,1)S(1)} %collective-permute-done.1.other_ref), custom_call_target="tpu_custom_call" | custom-call | flops 2147483648 | bytes 5605380 | tf_op jit(solution)/shard_map/second_sums/pallas_call | solution.py:39
  142.6 5.7 %all-to-all-start.3 = ((bf16[32,136,128]{2,1,0:T(8,128)(2,1)}), bf16[32,136,128]{2,1,0:T(8,128)(2,1)S(1)}, u32[]{:S(2)}, u32[]{:S(2)}) async-start(bf16[32,136,128]{2,1,0:T(8,128)(2,1)} %get-tuple-element.24), calls=%async_computation.3 | async-start | bytes 2228224 | tf_op jit(solution)/shard_map/all_to_all | solution.py:24
  148.3 0.0 copy-done
  148.3 0.3 multiply_reduce_fusion
  148.6 0.0 copy-done.3
  148.6 1.7 copy-done.7
  150.3 3.3 %margins.3.costs_ref = bf16[8,128]{1,0:T(8,128)(2,1)S(1)} custom-call(bf16[1024,1152]{1,0:T(8,128)(2,1)S(1)} %copy-done.7, bf16[512,1024]{1,0:T(8,128)(2,1)S(1)} %copy-done.3, bf16[512,1024]{1,0:T(8,128)(2,1)S(1)} %bitcast.16, f32[1,512]{1,0:T(1,128)S(1)} %bitcast.21), custom_call_target="tpu_custom_call" | custom-call | flops 2147483648 | bytes 4460544 | tf_op jit(solution)/shard_map/margins/pallas_call | solution.py:39
  153.5 24.3 %all-to-all-done.3.arrived_ref = bf16[32,136,128]{2,1,0:T(8,128)(2,1)S(1)} async-done(((bf16[32,136,128]{2,1,0:T(8,128)(2,1)}), bf16[32,136,128]{2,1,0:T(8,128)(2,1)S(1)}, u32[]{:S(2)}, u32[]{:S(2)}) %all-to-all-start.3) | async-done | bytes 1114144 | tf_op jit(solution)/shard_map/all_to_all | solution.py:24
  177.8 0.3 merge.3
  178.1 36.1 %all_to_all.27.full_ref = bf16[32,136,128]{2,1,0:T(8,128)(2,1)S(1)} all-to-all(bf16[32,136,128]{2,1,0:T(8,128)(2,1)S(1)} %merge.3), channel_id=1, replica_groups=mesh['z'=8,'x'=4,'y'=8,'core'=2] {'z','x'}, dimensions={0} | all-to-all | bytes 2228224 | tf_op jit(solution)/shard_map/all_to_all | solution.py:24
  214.3 1.3 last.1
  (9 shorter events, 0.0 us)
Async XLA Ops:
  1.4 1.2 copy-start.2
  83.4 1.4 copy-start.4
  84.9 13.2 %copy-start.1 = (bf16[1,512,1024]{2,1,0:T(8,128)(2,1)S(1)}, bf16[1,512,1024]{2,1,0:T(8,128)(2,1)}, u32[]{:S(2)}) copy-start(bf16[1,512,1024]{2,1,0:T(8,128)(2,1)} %param.10) | copy-start | bytes 3145732
  84.9 5.5 %collective-permute-start = (bf16[8,264,128]{2,1,0:T(8,128)(2,1)S(1)}, bf16[8,264,128]{2,1,0:T(8,128)(2,1)S(1)}, u32[]{:S(2)}, u32[]{:S(2)}) collective-permute-start(bf16[8,264,128]{2,1,0:T(8,128)(2,1)S(1)} %get-tuple-element.21), channel_id=1, source_target_pairs={{0,1},{1,0},{2,3},{3,2},{4,5},{5,4},{6,7},{7,6},{8,9},{9,8},{10,11... | collective-permute-start | bytes 1622024 | tf_op jit(solution)/shard_map/ppermute | solution.py:323
  91.3 19.9 %all-to-all-start.1 = ((bf16[8,264,128]{2,1,0:T(8,128)(2,1)}), bf16[8,264,128]{2,1,0:T(8,128)(2,1)S(1)}, u32[]{:S(2)}, u32[]{:S(2)}) async-start(bf16[8,264,128]{2,1,0:T(8,128)(2,1)} %add_convert_fusion), calls=%async_computation.1 | async-start | bytes 1081344 | tf_op jit(solution)/shard_map/all_to_all | solution.py:24
  98.4 1.7 copy-start.5
  111.2 27.4 %copy-start.6 = (bf16[1024,1152]{1,0:T(8,128)(2,1)S(1)}, bf16[1024,1152]{1,0:T(8,128)(2,1)}, u32[]{:S(2)}) copy-start(bf16[1024,1152]{1,0:T(8,128)(2,1)} %copy-done.4) | copy-start | bytes 7077892
  134.8 3.8 %collective-permute-start.1 = (bf16[8,264,128]{2,1,0:T(8,128)(2,1)S(1)}, bf16[8,264,128]{2,1,0:T(8,128)(2,1)S(1)}, u32[]{:S(2)}, u32[]{:S(2)}) collective-permute-start(bf16[8,264,128]{2,1,0:T(8,128)(2,1)S(1)} %all_to_all.26.own_ref), channel_id=1, source_target_pairs={{0,1},{1,0},{2,3},{3,2},{4,5},{5,4},{6,7},{7,6},{8,9},{9,8},{10,11... | collective-permute-start | bytes 1622024 | tf_op jit(solution)/shard_map/ppermute | solution.py:328
  142.6 5.7 %copy-start = (bf16[1,512,1024]{2,1,0:T(8,128)(2,1)S(1)}, bf16[1,512,1024]{2,1,0:T(8,128)(2,1)}, u32[]{:S(2)}) copy-start(bf16[1,512,1024]{2,1,0:T(8,128)(2,1)} %param.11) | copy-start | bytes 3145732
  142.6 6.0 %copy-start.3 = (bf16[512,1024]{1,0:T(8,128)(2,1)S(1)}, bf16[512,1024]{1,0:T(8,128)(2,1)}, u32[]{:S(2)}) copy-start(bf16[512,1024]{1,0:T(8,128)(2,1)} %get-tuple-element.22.centers_ref) | copy-start | bytes 3145732
  142.6 35.2 %all-to-all-start.3 = ((bf16[32,136,128]{2,1,0:T(8,128)(2,1)}), bf16[32,136,128]{2,1,0:T(8,128)(2,1)S(1)}, u32[]{:S(2)}, u32[]{:S(2)}) async-start(bf16[32,136,128]{2,1,0:T(8,128)(2,1)} %get-tuple-element.24), calls=%async_computation.3 | async-start | bytes 2228224 | tf_op jit(solution)/shard_map/all_to_all | solution.py:24
  148.6 1.7 copy-start.7

commit v5 on v4

--- a/solution.py
+++ b/solution.py
@@ -247,20 +247,22 @@
     )
     label = label_row(rows_ref[:, width:], 3)
     sums, counts = sums_of(residual_of(rows_ref, new_ref), label, children)
-    parts, tall, _ = out_ref.shape
-    each = children // parts
+    nx, nz, tall, _ = out_ref.shape
+    each = children // (nx * nz)
     for j in range(width // LANES):
-        piece = sums[:, j * LANES : (j + 1) * LANES].astype(BF16)
-        out_ref[:, j * each : (j + 1) * each, :] = piece.reshape(parts, each, LANES)
-    for h in range(parts):
-        chunk = h * each // LANES * LANES
-        out_ref[h, tall - EXTRA :, :] = counts[:, chunk : chunk + LANES].astype(BF16)
-
-
-def second_sums(core, rows, own, other, children, parts):
+        piece = sums[:, j * LANES : (j + 1) * LANES].astype(BF16).reshape(nz, nx, each, LANES)
+        for x in range(nx):
+            out_ref[x, :, j * each : (j + 1) * each, :] = piece[:, x]
+    for z in range(nz):
+        for x in range(nx):
+            chunk = (z * nx + x) * each // LANES * LANES
+            out_ref[x, z, tall - EXTRA :, :] = counts[:, chunk : chunk + LANES].astype(BF16)
+
+
+def second_sums(core, rows, own, other, children, nx, nz):
     total, wide = rows.shape
     width = wide - LANES
-    tall = children // parts * (width // LANES) + EXTRA
+    tall = children // (nx * nz) * (width // LANES) + EXTRA
     return kernel_call(
         second_body,
         "second_sums",
@@ -268,7 +270,7 @@
         [
             shaped((children, width)),
             shaped((children // LANES, LANES), F32),
-            shaped((parts, tall, LANES)),
+            shaped((nx, nz, tall, LANES)),
         ],
         [core, rows, own, other],
         scalars=1,
@@ -276,13 +278,14 @@
 
 
 def last_body(full_ref, new_ref, cost_ref):
-    parts, tall, _ = full_ref.shape
+    nx, nz, tall, _ = full_ref.shape
     children, width = new_ref.shape
-    each = children // parts
+    each = children // (nx * nz)
     for j in range(width // LANES):
-        piece = full_ref[:, j * each : (j + 1) * each, :]
-        new_ref[:, j * LANES : (j + 1) * LANES] = piece.reshape(children, LANES)
-    cost_ref[...] = cost_sum(full_ref[:, tall - EXTRA :, :], children // LANES)
+        piece = [full_ref[x, :, j * each : (j + 1) * each, :] for x in range(nx)]
+        new_ref[:, j * LANES : (j + 1) * LANES] = jnp.stack(piece, axis=1).reshape(children, LANES)
+    chunks = children // LANES
+    cost_ref[...] = sum(cost_sum(full_ref[x, :, tall - EXTRA :, :], chunks) for x in range(nx))
 
 
 def last(full, children, width):
@@ -327,11 +330,14 @@
     own = exchange(copies_one, "y")
     other = lax.ppermute(own, "core", SWAP)
 
-    coarse_new, coarse_cost, partial_two = second_sums(core, rows, own, other, children, n_shard)
-    parts_two = exchange(partial_two, SHARD)
+    nx, nz = lax.axis_size("x"), lax.axis_size("z")
+    coarse_new, coarse_cost, partial_two = second_sums(core, rows, own, other, children, nx, nz)
+    parts_two = jnp.sum(exchange(partial_two, "x").astype(F32), axis=0).astype(BF16)
+    parts_two = exchange(parts_two, "z")
     costs_two = margins(margins_two_body, rows, coarse_new, fine, squares_of(fine))
-    copies_two = merge(shard, parts_two, fine, costs_two, n_shard)
-    fine_new, fine_cost = last(exchange(copies_two, SHARD), children, width)
+    copies_two = exchange(merge(shard, parts_two, fine, costs_two, nz), "z")
+    full_two = exchange(jnp.broadcast_to(copies_two[None], (nx,) + copies_two.shape), "x")
+    fine_new, fine_cost = last(full_two, children, width)
     return (
         coarse_new[None],
         fine_new[None],

time: 218 us -> 210 us (0.963)
  waiting for transfers between devices: 37.1 us -> 18.9 us
  blocking collectives: 136 us -> 148 us
    all_to_all x2, waiting for transfers between devices: 33.7 us -> 15.5 us  [exchange(): return lax.all_to_all(blocks, axes, split_axis=0, concat_axis=0, tiled=True)]
    all_to_all x3 -> x5, blocking collectives: 136 us -> 148 us  [exchange(): return lax.all_to_all(blocks, axes, split_axis=0, concat_axis=0, tiled=True)]
where the time goes in v5:
time: 210 us; the launch traced here: 208 us
  blocking collectives  148 us (70%)
  waiting for transfers between devices  18.9 us (9%)
  starting transfers between devices  16.2 us (8%)
  Pallas kernels  14 us (7%)
  local copies, waits for them, and re-layouts  6.88 us (3%)
  other arithmetic  2.42 us (1%)
    all_to_all x5, blocking collectives, exchange(): return lax.all_to_all(blocks, axes, split_axis=0, concat_axis=0, tiled=True)  148 us
    all_to_all x2, waiting for transfers between devices, exchange(): return lax.all_to_all(blocks, axes, split_axis=0, concat_axis=0, tiled=True)  15.5 us
    pallas_call x8, Pallas kernels, kernel_call(): pl.pallas_call(body, name=name, in_specs=specs, out_specs=[pl.BlockSpec(m...  14 us
    all_to_all x2, starting transfers between devices, exchange(): return lax.all_to_all(blocks, axes, split_axis=0, concat_axis=0, tiled=True)  10.4 us
    unnamed x16, local copies, waits for them, and re-layouts  5.99 us
  transfers between devices with their start and end apart: 4, of which 4 were waited for; matrix products, arithmetic and copies ran while one was open for 0% of the time, Pallas kernels for 2%

profile of v5, /device:TPU:56, one launch (start us, length us, event | category | flops | bytes accessed | tf_op | source)
XLA Modules:
  0.0 207.7 jit_solution(6540627065406689636)
XLA Ops:
  0.7 0.7 stack.15.info_ref
  1.4 0.0 copy-start.2
  1.4 1.2 copy-done.2
  2.6 2.0 place.1
  4.7 76.9 %all_to_all.35.arrived_ref = bf16[512,2,1152]{2,1,0:T(2,128)(2,1)S(1)} all-to-all(bf16[512,2,1152]{2,1,0:T(2,128)(2,1)S(1)} %place.1), channel_id=1, replica_groups=mesh['z'=8,'x'=4,'y'=8,'core'=2] {'z','x','y','core'}, dimensions={0} | all-to-all | bytes 4718592 | tf_op jit(solution)/shard_map/all_to_all | solution.py:24
  81.6 1.9 first_sums.1
  83.4 1.4 copy-done.4
  84.9 3.9 %collective-permute-start = (bf16[8,264,128]{2,1,0:T(8,128)(2,1)S(1)}, bf16[8,264,128]{2,1,0:T(8,128)(2,1)S(1)}, u32[]{:S(2)}, u32[]{:S(2)}) collective-permute-start(bf16[8,264,128]{2,1,0:T(8,128)(2,1)S(1)} %get-tuple-element.21), channel_id=1, source_target_pairs={{0,1},{1,0},{2,3},{3,2},{4,5},{5,4},{6,7},{7,6},{8,9},{9,8},{10,11... | collective-permute-start | bytes 1622024 | tf_op jit(solution)/shard_map/ppermute | solution.py:326
  88.8 1.5 collective-permute-done
  90.3 0.9 add_convert_fusion
  91.3 6.8 %all-to-all-start.1 = ((bf16[8,264,128]{2,1,0:T(8,128)(2,1)}), bf16[8,264,128]{2,1,0:T(8,128)(2,1)S(1)}, u32[]{:S(2)}, u32[]{:S(2)}) async-start(bf16[8,264,128]{2,1,0:T(8,128)(2,1)} %add_convert_fusion), calls=%async_computation.1 | async-start | bytes 1081344 | tf_op jit(solution)/shard_map/all_to_all | solution.py:24
  98.1 0.3 multiply_reduce_fusion.1
  98.4 1.7 copy-done.5
  100.0 1.8 margins.2.costs_ref
  101.8 9.4 %all-to-all-done.1.arrived_ref = bf16[8,264,128]{2,1,0:T(8,128)(2,1)S(1)} async-done(((bf16[8,264,128]{2,1,0:T(8,128)(2,1)}), bf16[8,264,128]{2,1,0:T(8,128)(2,1)S(1)}, u32[]{:S(2)}, u32[]{:S(2)}) %all-to-all-start.1) | async-done | bytes 540704 | tf_op jit(solution)/shard_map/all_to_all | solution.py:24
  111.2 0.1 merge.2
  111.3 23.4 %all_to_all.36.own_ref = bf16[8,264,128]{2,1,0:T(8,128)(2,1)S(1)} all-to-all(bf16[8,264,128]{2,1,0:T(8,128)(2,1)S(1)} %merge.2), channel_id=1, replica_groups=mesh['z'=8,'x'=4,'y'=8,'core'=2] {'y'}, dimensions={0} | all-to-all | bytes 1081344 | tf_op jit(solution)/shard_map/all_to_all | solution.py:24
  134.8 1.9 collective-permute-start.1
  136.7 1.9 collective-permute-done.1.other_ref
  138.6 3.5 %second_sums.1 = (bf16[512,1024]{1,0:T(8,128)(2,1)}, f32[4,128]{1,0:T(4,128)}, bf16[4,8,136,128]{3,2,1,0:T(8,128)(2,1)S(1)}) custom-call(s32[1]{0:T(128)} %bitcast.3.core_ref, bf16[1024,1152]{1,0:T(8,128)(2,1)S(1)} %copy-done.6, bf16[8,264,128]{2,1,0:T(8,128)(2,1)S(1)} %all_to_all.36.own_ref, bf16[8,264,128]{2,1,0:T(8,128)(2,1)S(1)} %collective-permute-done.1.other_ref), custom_call_target="tpu_custom_call" | custom-call | flops 2147483648 | bytes 5605380 | tf_op jit(solution)/shard_map/second_sums/pallas_call | solution.py:39
  142.1 19.4 %all_to_all.37 = bf16[4,8,136,128]{3,2,1,0:T(8,128)(2,1)S(1)} all-to-all(bf16[4,8,136,128]{3,2,1,0:T(8,128)(2,1)S(1)} %get-tuple-element.24), channel_id=1, replica_groups=mesh['z'=8,'x'=4,'y'=8,'core'=2] {'x'}, dimensions={0} | all-to-all | bytes 2228224 | tf_op jit(solution)/shard_map/all_to_all | solution.py:24
  161.4 0.9 reduce_sum.31
  162.3 3.6 %all-to-all-start.4 = ((bf16[8,136,128]{2,1,0:T(8,128)(2,1)}), bf16[8,136,128]{2,1,0:T(8,128)(2,1)S(1)}, u32[]{:S(2)}, u32[]{:S(2)}) async-start(bf16[8,136,128]{2,1,0:T(8,128)(2,1)} %reduce_sum.31), calls=%async_computation.4 | async-start | bytes 557056 | tf_op jit(solution)/shard_map/all_to_all | solution.py:24
  166.0 0.3 multiply_reduce_fusion
  166.2 1.7 copy-done.7
  167.9 3.3 %margins.3.costs_ref = bf16[8,128]{1,0:T(8,128)(2,1)S(1)} custom-call(bf16[1024,1152]{1,0:T(8,128)(2,1)S(1)} %copy-done.7, bf16[512,1024]{1,0:T(8,128)(2,1)S(1)} %copy-done.3, bf16[512,1024]{1,0:T(8,128)(2,1)S(1)} %bitcast.18, f32[1,512]{1,0:T(1,128)S(1)} %bitcast.21), custom_call_target="tpu_custom_call" | custom-call | flops 2147483648 | bytes 4460544 | tf_op jit(solution)/shard_map/margins/pallas_call | solution.py:39
  171.2 6.1 %all-to-all-done.4.arrived_ref = bf16[8,136,128]{2,1,0:T(8,128)(2,1)S(1)} async-done(((bf16[8,136,128]{2,1,0:T(8,128)(2,1)}), bf16[8,136,128]{2,1,0:T(8,128)(2,1)S(1)}, u32[]{:S(2)}, u32[]{:S(2)}) %all-to-all-start.4) | async-done | bytes 278560 | tf_op jit(solution)/shard_map/all_to_all | solution.py:24
  177.3 0.1 merge.3
  177.5 13.3 %all_to_all.38 = bf16[8,136,128]{2,1,0:T(8,128)(2,1)S(1)} all-to-all(bf16[8,136,128]{2,1,0:T(8,128)(2,1)S(1)} %merge.3), channel_id=1, replica_groups=mesh['z'=8,'x'=4,'y'=8,'core'=2] {'z'}, dimensions={0} | all-to-all | bytes 557056 | tf_op jit(solution)/shard_map/all_to_all | solution.py:24
  190.7 0.1 broadcast_in_dim.33
  190.9 15.5 %all_to_all.39.full_ref = bf16[4,8,136,128]{3,2,1,0:T(8,128)(2,1)S(1)} all-to-all(bf16[4,8,136,128]{3,2,1,0:T(8,128)(2,1)S(1)} %broadcast_in_dim.33), channel_id=1, replica_groups=mesh['z'=8,'x'=4,'y'=8,'core'=2] {'x'}, dimensions={0} | all-to-all | bytes 2228224 | tf_op jit(solution)/shard_map/all_to_all | solution.py:24
  206.4 1.3 last.1
  (13 shorter events, 0.0 us)
Async XLA Ops:
  1.4 1.2 copy-start.2
  83.4 1.4 copy-start.4
  84.9 13.2 %copy-start = (bf16[1,512,1024]{2,1,0:T(8,128)(2,1)S(1)}, bf16[1,512,1024]{2,1,0:T(8,128)(2,1)}, u32[]{:S(2)}) copy-start(bf16[1,512,1024]{2,1,0:T(8,128)(2,1)} %param.10) | copy-start | bytes 3145732
  84.9 5.5 %collective-permute-start = (bf16[8,264,128]{2,1,0:T(8,128)(2,1)S(1)}, bf16[8,264,128]{2,1,0:T(8,128)(2,1)S(1)}, u32[]{:S(2)}, u32[]{:S(2)}) collective-permute-start(bf16[8,264,128]{2,1,0:T(8,128)(2,1)S(1)} %get-tuple-element.21), channel_id=1, source_target_pairs={{0,1},{1,0},{2,3},{3,2},{4,5},{5,4},{6,7},{7,6},{8,9},{9,8},{10,11... | collective-permute-start | bytes 1622024 | tf_op jit(solution)/shard_map/ppermute | solution.py:326
  91.3 19.9 %all-to-all-start.1 = ((bf16[8,264,128]{2,1,0:T(8,128)(2,1)}), bf16[8,264,128]{2,1,0:T(8,128)(2,1)S(1)}, u32[]{:S(2)}, u32[]{:S(2)}) async-start(bf16[8,264,128]{2,1,0:T(8,128)(2,1)} %add_convert_fusion), calls=%async_computation.1 | async-start | bytes 1081344 | tf_op jit(solution)/shard_map/all_to_all | solution.py:24
  98.4 1.7 copy-start.5
  111.2 27.4 %copy-start.6 = (bf16[1024,1152]{1,0:T(8,128)(2,1)S(1)}, bf16[1024,1152]{1,0:T(8,128)(2,1)}, u32[]{:S(2)}) copy-start(bf16[1024,1152]{1,0:T(8,128)(2,1)} %copy-done.4) | copy-start | bytes 7077892
  134.8 3.8 %collective-permute-start.1 = (bf16[8,264,128]{2,1,0:T(8,128)(2,1)S(1)}, bf16[8,264,128]{2,1,0:T(8,128)(2,1)S(1)}, u32[]{:S(2)}, u32[]{:S(2)}) collective-permute-start(bf16[8,264,128]{2,1,0:T(8,128)(2,1)S(1)} %all_to_all.36.own_ref), channel_id=1, source_target_pairs={{0,1},{1,0},{2,3},{3,2},{4,5},{5,4},{6,7},{7,6},{8,9},{9,8},{10,11... | collective-permute-start | bytes 1622024 | tf_op jit(solution)/shard_map/ppermute | solution.py:331
  142.0 23.9 %copy-start.1 = (bf16[1,512,1024]{2,1,0:T(8,128)(2,1)S(1)}, bf16[1,512,1024]{2,1,0:T(8,128)(2,1)}, u32[]{:S(2)}) copy-start(bf16[1,512,1024]{2,1,0:T(8,128)(2,1)} %param.11) | copy-start | bytes 3145732
  142.1 24.2 %copy-start.3 = (bf16[512,1024]{1,0:T(8,128)(2,1)S(1)}, bf16[512,1024]{1,0:T(8,128)(2,1)}, u32[]{:S(2)}) copy-start(bf16[512,1024]{1,0:T(8,128)(2,1)} %get-tuple-element.22.centers_ref) | copy-start | bytes 3145732
  162.3 15.0 %all-to-all-start.4 = ((bf16[8,136,128]{2,1,0:T(8,128)(2,1)}), bf16[8,136,128]{2,1,0:T(8,128)(2,1)S(1)}, u32[]{:S(2)}, u32[]{:S(2)}) async-start(bf16[8,136,128]{2,1,0:T(8,128)(2,1)} %reduce_sum.31), calls=%async_computation.4 | async-start | bytes 557056 | tf_op jit(solution)/shard_map/all_to_all | solution.py:24
  166.2 1.7 copy-start.7

commit v6 on v5

--- a/solution.py
+++ b/solution.py
@@ -22,6 +22,23 @@
 
 def exchange(blocks, axes):
     return lax.all_to_all(blocks, axes, split_axis=0, concat_axis=0, tiled=True)
+
+
+def mirrored(blocks, axes, outer):
+    n = lax.axis_size(axes[0])
+    low = lax.axis_size(axes[1:]) // outer
+    groups = []
+    for index in range(outer):
+        base = index * low
+        groups.append([i * outer * low + base for i in range(n)])
+        groups.append([(n - 1 - i) * outer * low + base + 1 for i in range(n)])
+    return lax.all_to_all(
+        blocks, axes, split_axis=0, concat_axis=0, tiled=True, axis_index_groups=groups
+    )
+
+
+def mirror(index, count, core):
+    return index + core * (count - 1 - 2 * index)
 
 
 def iota(shape, dim):
@@ -56,10 +73,12 @@
     return mask.astype(F32).astype(BF16)
 
 
-def place_body(info_ref, emb_ref, out_ref, wide_ref):
+def place_body(keys_ref, one_ref, two_ref, emb_ref, out_ref, wide_ref):
     count, width = emb_ref.shape
     devices, slots, wide = out_ref.shape
-    info = info_ref[...]
+    info = jnp.concatenate(
+        [keys_ref[...], one_ref[...], two_ref[...], jnp.zeros((5, count), jnp.int32)], axis=0
+    )
     turned = jnp.transpose(info.astype(F32)).astype(jnp.int32)
     keys_row, keys_col = info[0:1, :], turned[:, 0:1]
     earlier = (keys_col == keys_row) & (iota((count, count), 0) < iota((count, count), 1))
@@ -79,7 +98,7 @@
         out_ref[piece * block : (piece + 1) * block] = moved.reshape(block, slots, wide)
 
 
-def place(info, embeddings, devices):
+def place(keys, one, two, embeddings, devices):
     count, width = embeddings.shape
     wide = width + LANES
     return kernel_call(
@@ -87,7 +106,7 @@
         "place",
         2 * devices * SLOTS * count * wide,
         [shaped((devices, SLOTS, wide))],
-        [info, embeddings],
+        [keys, one, two, embeddings],
         scratch=[pltpu.VMEM((count, wide), BF16)],
     )[0]
 
@@ -111,23 +130,30 @@
     return sums, matmul(jnp.ones((EXTRA, count), BF16), member, ((1,), (1,)))
 
 
-def first_body(core_ref, arrived_ref, rows_ref, keep_ref, send_ref):
-    total, wide = rows_ref.shape
-    width = wide - LANES
+def rows_of(arrived_ref):
+    devices, slots, wide = arrived_ref.shape
+    rows = arrived_ref[...].reshape(devices * slots, wide)
+    return rows[:, : wide - LANES], rows[:, wide - LANES :]
+
+
+def first_body(core_ref, arrived_ref, keep_ref, send_ref):
+    rows, tail = rows_of(arrived_ref)
+    width = rows.shape[1]
     parts, tall, _ = keep_ref.shape
     each = (tall - EXTRA) // (width // LANES)
     children = 2 * parts * each
-    rows = arrived_ref[...].reshape(total, wide)
-    rows_ref[...] = rows
-    sums, counts = sums_of(rows[:, :width], label_row(rows[:, width:], 1), children)
+    sums, counts = sums_of(rows, label_row(tail, 1), children)
     even = core_ref[0] == 0
     for j in range(width // LANES):
         at = slice(j * each, (j + 1) * each)
         piece = sums[:, j * LANES : (j + 1) * LANES].reshape(parts, 2, each, LANES)
-        keep_ref[:, at, :] = jnp.where(even, piece[:, 0], piece[:, 1]).astype(BF16)
-        send_ref[:, at, :] = jnp.where(even, piece[:, 1], piece[:, 0]).astype(BF16)
+        for y in range(parts):
+            zero, one = piece[y, 0], piece[parts - 1 - y, 1]
+            keep_ref[y, at, :] = jnp.where(even, zero, one).astype(BF16)
+            send_ref[y, at, :] = jnp.where(even, one, zero).astype(BF16)
     for y in range(parts):
-        chunks = [(2 * y + side) * each // LANES * LANES for side in range(2)]
+        blocks = (2 * y, 2 * (parts - 1 - y) + 1)
+        chunks = [block * each // LANES * LANES for block in blocks]
         zero, one = [counts[:, chunk : chunk + LANES] for chunk in chunks]
         keep_ref[y, tall - EXTRA :, :] = jnp.where(even, zero, one).astype(BF16)
         send_ref[y, tall - EXTRA :, :] = jnp.where(even, one, zero).astype(BF16)
@@ -142,15 +168,14 @@
         first_body,
         "first_sums",
         2 * total * children * width,
-        [shaped((total, wide)), shaped(half), shaped(half)],
+        [shaped(half), shaped(half)],
         [core, arrived],
         scalars=1,
     )
 
 
-def residual_of(rows_ref, centers_ref):
-    children, width = centers_ref.shape
-    rows, tail = rows_ref[:, :width], rows_ref[:, width:]
+def residual_of(rows, tail, centers_ref):
+    children = centers_ref.shape[0]
     picked = one_hot(iota((rows.shape[0], children), 1) == label_col(tail, 1))
     center = matmul(picked, centers_ref[...], ((1,), (0,)))
     return (rows.astype(F32) - center).astype(BF16)
@@ -173,26 +198,38 @@
     out_ref[...] = out.astype(BF16)
 
 
-def margins_one_body(rows_ref, cents_ref, squares_ref, out_ref):
-    width = cents_ref.shape[1]
-    label = label_col(rows_ref[:, width:], 1)
-    write_margins(rows_ref[:, :width], label, cents_ref, squares_ref, out_ref)
+def margins_one_body(arrived_ref, cents_ref, squares_ref, out_ref, rows_ref):
+    rows, tail = rows_of(arrived_ref)
+    rows_ref[:, : rows.shape[1]] = rows
+    rows_ref[:, rows.shape[1] :] = tail
+    write_margins(rows, label_col(tail, 1), cents_ref, squares_ref, out_ref)
 
 
 def margins_two_body(rows_ref, centers_ref, cents_ref, squares_ref, out_ref):
     width = cents_ref.shape[1]
-    label = label_col(rows_ref[:, width:], 3)
-    write_margins(residual_of(rows_ref, centers_ref), label, cents_ref, squares_ref, out_ref)
-
-
-def margins(body, rows, *others):
-    children, width = others[0].shape
-    return kernel_call(
-        body,
-        "margins",
-        2 * (len(others) - 1) * rows.shape[0] * children * width,
+    rows, tail = rows_ref[:, :width], rows_ref[:, width:]
+    residual = residual_of(rows, tail, centers_ref)
+    write_margins(residual, label_col(tail, 3), cents_ref, squares_ref, out_ref)
+
+
+def margins_one(arrived, centroids, squares):
+    devices, slots, wide = arrived.shape
+    return kernel_call(
+        margins_one_body,
+        "margins_one",
+        2 * devices * slots * centroids.size,
+        [shaped((EXTRA, LANES)), shaped((devices * slots, wide))],
+        [arrived, centroids, squares],
+    )
+
+
+def margins_two(rows, centers, centroids, squares):
+    return kernel_call(
+        margins_two_body,
+        "margins_two",
+        4 * rows.shape[0] * centroids.size,
         [shaped((EXTRA, LANES))],
-        [rows, *others],
+        [rows, centers, centroids, squares],
     )[0]
 
 
@@ -238,25 +275,28 @@
     core = core_ref[0]
     for ref, side in ((own_ref, core), (other_ref, 1 - core)):
         for y in range(parts):
-            at = pl.ds(pl.multiple_of((2 * y + side) * each, each), each)
+            block = 2 * mirror(y, parts, side) + side
+            at = pl.ds(pl.multiple_of(block * each, each), each)
             for j in range(width // LANES):
                 new_ref[at, j * LANES : (j + 1) * LANES] = ref[y, j * each : (j + 1) * each, :]
     chunks = children // LANES
     cost_ref[...] = cost_sum(own_ref[:, tall - EXTRA :, :], chunks) + cost_sum(
         other_ref[:, tall - EXTRA :, :], chunks
     )
-    label = label_row(rows_ref[:, width:], 3)
-    sums, counts = sums_of(residual_of(rows_ref, new_ref), label, children)
+    rows, tail = rows_ref[:, :width], rows_ref[:, width:]
+    sums, counts = sums_of(residual_of(rows, tail, new_ref), label_row(tail, 3), children)
     nx, nz, tall, _ = out_ref.shape
     each = children // (nx * nz)
     for j in range(width // LANES):
         piece = sums[:, j * LANES : (j + 1) * LANES].astype(BF16).reshape(nz, nx, each, LANES)
         for x in range(nx):
-            out_ref[x, :, j * each : (j + 1) * each, :] = piece[:, x]
+            out_ref[mirror(x, nx, core), :, j * each : (j + 1) * each, :] = piece[:, x]
     for z in range(nz):
         for x in range(nx):
             chunk = (z * nx + x) * each // LANES * LANES
-            out_ref[x, z, tall - EXTRA :, :] = counts[:, chunk : chunk + LANES].astype(BF16)
+            out_ref[mirror(x, nx, core), z, tall - EXTRA :, :] = counts[
+                :, chunk : chunk + LANES
+            ].astype(BF16)
 
 
 def second_sums(core, rows, own, other, children, nx, nz):
@@ -277,24 +317,29 @@
     )
 
 
-def last_body(full_ref, new_ref, cost_ref):
+def last_body(core_ref, full_ref, new_ref, cost_ref):
     nx, nz, tall, _ = full_ref.shape
     children, width = new_ref.shape
     each = children // (nx * nz)
-    for j in range(width // LANES):
-        piece = [full_ref[x, :, j * each : (j + 1) * each, :] for x in range(nx)]
-        new_ref[:, j * LANES : (j + 1) * LANES] = jnp.stack(piece, axis=1).reshape(children, LANES)
+    for x in range(nx):
+        for z in range(nz):
+            block = z * nx + mirror(x, nx, core_ref[0])
+            at = pl.ds(pl.multiple_of(block * each, each), each)
+            for j in range(width // LANES):
+                lanes = slice(j * LANES, (j + 1) * LANES)
+                new_ref[at, lanes] = full_ref[x, z, j * each : (j + 1) * each, :]
     chunks = children // LANES
     cost_ref[...] = sum(cost_sum(full_ref[x, :, tall - EXTRA :, :], chunks) for x in range(nx))
 
 
-def last(full, children, width):
+def last(core, full, children, width):
     return kernel_call(
         last_body,
         "last",
         full.size,
         [shaped((children, width)), shaped((children // LANES, LANES), F32)],
-        [full],
+        [core, full],
+        scalars=1,
     )
 
 
@@ -315,29 +360,33 @@
     group = lax.axis_index(GROUP).astype(jnp.int32)[None]
     shard = lax.axis_index(SHARD).astype(jnp.int32)[None]
 
-    info = jnp.stack(
-        [cluster_key[:, 0], child_first, child_second] + [jnp.zeros((rows_dev,), jnp.int32)] * 5
-    )
-    layout = place(info, embeddings, devices)
+    layout = place(
+        cluster_key.reshape(1, rows_dev),
+        child_first.reshape(1, rows_dev),
+        child_second.reshape(1, rows_dev),
+        embeddings,
+        devices,
+    )
     layout, core, group, shard = lax.optimization_barrier((layout, core, group, shard))
     arrived = exchange(layout, ALL)
 
-    rows, keep, send = first_sums(core, arrived, children, n_group)
+    keep, send = first_sums(core, arrived, children, n_group)
     taken = lax.ppermute(send, "core", SWAP)
-    parts_one = exchange((keep.astype(F32) + taken.astype(F32)).astype(BF16), "y")
-    costs_one = margins(margins_one_body, rows, coarse, squares_of(coarse))
+    parts_one = mirrored((keep.astype(F32) + taken.astype(F32)).astype(BF16), GROUP, 1)
+    costs_one, rows = margins_one(arrived, coarse, squares_of(coarse))
     copies_one = merge(group, parts_one, coarse, costs_one, lax.axis_size("y"))
-    own = exchange(copies_one, "y")
+    own = mirrored(copies_one, GROUP, 1)
     other = lax.ppermute(own, "core", SWAP)
 
     nx, nz = lax.axis_size("x"), lax.axis_size("z")
     coarse_new, coarse_cost, partial_two = second_sums(core, rows, own, other, children, nx, nz)
-    parts_two = jnp.sum(exchange(partial_two, "x").astype(F32), axis=0).astype(BF16)
+    parts_two = jnp.sum(mirrored(partial_two, ("x",) + GROUP, n_group // 2).astype(F32), axis=0).astype(BF16)
     parts_two = exchange(parts_two, "z")
-    costs_two = margins(margins_two_body, rows, coarse_new, fine, squares_of(fine))
+    costs_two = margins_two(rows, coarse_new, fine, squares_of(fine))
     copies_two = exchange(merge(shard, parts_two, fine, costs_two, nz), "z")
-    full_two = exchange(jnp.broadcast_to(copies_two[None], (nx,) + copies_two.shape), "x")
-    fine_new, fine_cost = last(full_two, children, width)
+    full_two = jnp.broadcast_to(copies_two[None], (nx,) + copies_two.shape)
+    full_two = mirrored(full_two, ("x",) + GROUP, n_group // 2)
+    fine_new, fine_cost = last(core, full_two, children, width)
     return (
         coarse_new[None],
         fine_new[None],

time: 210 us -> 209 us (level)
    all_to_all x5 -> x2, blocking collectives: 148 us -> 90 us  [exchange(): return lax.all_to_all(blocks, axes, split_axis=0, concat_axis=0, tiled=True)]
    all_to_all x0 -> x3, blocking collectives: none -> 56.3 us  [mirrored(): lax.all_to_all(blocks, axes, split_axis=0, concat_axis=0, tiled=True, axi...]
    all_to_all x0 -> x1, waiting for transfers between devices: none -> 10.2 us  [mirrored(): lax.all_to_all(blocks, axes, split_axis=0, concat_axis=0, tiled=True, axi...]
    all_to_all x2 -> x1, waiting for transfers between devices: 15.5 us -> 5.93 us  [exchange(): return lax.all_to_all(blocks, axes, split_axis=0, concat_axis=0, tiled=True)]
    all_to_all x0 -> x1, starting transfers between devices: none -> 7.44 us  [mirrored(): lax.all_to_all(blocks, axes, split_axis=0, concat_axis=0, tiled=True, axi...]
    all_to_all x2 -> x1, starting transfers between devices: 10.4 us -> 3.86 us  [exchange(): return lax.all_to_all(blocks, axes, split_axis=0, concat_axis=0, tiled=True)]
    unnamed x16 -> x20, local copies, waits for them, and re-layouts: 5.99 us -> 6.34 us
  transfers between devices with their start and end apart: 4 -> 4, of which waited for: 4 -> 4; matrix products, arithmetic and copies ran while one was open for 0% -> 0% of each run, Pallas kernels for 2% -> 3%
where the time goes in v6:
time: 209 us; the launch traced here: 208 us
  blocking collectives  146 us (70%)
  waiting for transfers between devices  19.3 us (9%)
  starting transfers between devices  17.3 us (8%)
  Pallas kernels  15.8 us (8%)
  local copies, waits for them, and re-layouts  6.48 us (3%)
  other arithmetic  2.42 us (1%)
    all_to_all x2, blocking collectives, exchange(): return lax.all_to_all(blocks, axes, split_axis=0, concat_axis=0, tiled=True)  90 us
    all_to_all x3, blocking collectives, mirrored(): lax.all_to_all(blocks, axes, split_axis=0, concat_axis=0, tiled=True, axi...  56.3 us
    pallas_call x8, Pallas kernels, kernel_call(): pl.pallas_call(body, name=name, in_specs=specs, out_specs=[pl.BlockSpec(m...  15.8 us
    all_to_all x1, waiting for transfers between devices, mirrored(): lax.all_to_all(blocks, axes, split_axis=0, concat_axis=0, tiled=True, axi...  10.2 us
    all_to_all x1, starting transfers between devices, mirrored(): lax.all_to_all(blocks, axes, split_axis=0, concat_axis=0, tiled=True, axi...  7.44 us
    unnamed x20, local copies, waits for them, and re-layouts  6.34 us
    all_to_all x1, waiting for transfers between devices, exchange(): return lax.all_to_all(blocks, axes, split_axis=0, concat_axis=0, tiled=True)  5.93 us
  transfers between devices with their start and end apart: 4, of which 4 were waited for; matrix products, arithmetic and copies ran while one was open for 0% of the time, Pallas kernels for 3%

profile of v6, /device:TPU:56, one launch (start us, length us, event | category | flops | bytes accessed | tf_op | source)
XLA Modules:
  0.0 208.4 jit_solution(7788666989006222386)
XLA Ops:
  0.7 1.2 copy-done.2
  1.9 0.7 copy-done.3
  2.6 0.7 copy-done.4
  3.2 0.7 copy-done.5
  3.9 2.1 place.1
  6.0 76.9 %all_to_all.35.arrived_ref = bf16[512,2,1152]{2,1,0:T(2,128)(2,1)S(1)} all-to-all(bf16[512,2,1152]{2,1,0:T(2,128)(2,1)S(1)} %place.1), channel_id=1, replica_groups=mesh['z'=8,'x'=4,'y'=8,'core'=2] {'z','x','y','core'}, dimensions={0} | all-to-all | bytes 4718592 | tf_op jit(solution)/shard_map/all_to_all | solution.py:24
  82.9 1.6 first_sums.1
  84.5 3.9 %collective-permute-start = (bf16[8,264,128]{2,1,0:T(8,128)(2,1)S(1)}, bf16[8,264,128]{2,1,0:T(8,128)(2,1)S(1)}, u32[]{:S(2)}, u32[]{:S(2)}) collective-permute-start(bf16[8,264,128]{2,1,0:T(8,128)(2,1)S(1)} %get-tuple-element.22), channel_id=1, source_target_pairs={{0,1},{1,0},{2,3},{3,2},{4,5},{5,4},{6,7},{7,6},{8,9},{9,8},{10,11... | collective-permute-start | bytes 1622024 | tf_op jit(solution)/shard_map/ppermute | solution.py:374
  88.4 1.5 collective-permute-done
  89.9 0.9 add_convert_fusion
  90.9 7.4 %all-to-all-start.1 = ((bf16[8,264,128]{2,1,0:T(8,128)(2,1)}), bf16[8,264,128]{2,1,0:T(8,128)(2,1)}, u32[]{:S(2)}, u32[]{:S(2)}) async-start(bf16[8,264,128]{2,1,0:T(8,128)(2,1)} %add_convert_fusion), calls=%async_computation.1 | async-start | bytes 1081344 | tf_op jit(solution)/shard_map/all_to_all | solution.py:35
  98.3 0.3 multiply_reduce_fusion.1
  98.6 2.6 %margins_one.1 = (bf16[8,128]{1,0:T(8,128)(2,1)S(1)}, bf16[1024,1152]{1,0:T(8,128)(2,1)S(1)}) custom-call(bf16[512,2,1152]{2,1,0:T(2,128)(2,1)S(1)} %all_to_all.35.arrived_ref, bf16[512,1024]{1,0:T(8,128)(2,1)S(1)} %bitcast.16, f32[1,512]{1,0:T(1,128)S(1)} %bitcast.20), custom_call_target="tpu_custom_call" | custom-call | flops 1073741824 | bytes 5771264 | tf_op jit(solution)/shard_map/margins_one/pallas_call | solution.py:56
  101.2 1.4 copy-done.7
  102.6 10.2 %all-to-all-done.1.arrived_ref = bf16[8,264,128]{2,1,0:T(8,128)(2,1)} async-done(((bf16[8,264,128]{2,1,0:T(8,128)(2,1)}), bf16[8,264,128]{2,1,0:T(8,128)(2,1)}, u32[]{:S(2)}, u32[]{:S(2)}) %all-to-all-start.1) | async-done | bytes 540704 | tf_op jit(solution)/shard_map/all_to_all | solution.py:35
  112.8 1.3 merge.2
  114.1 20.6 %all_to_all.36.own_ref = bf16[8,264,128]{2,1,0:T(8,128)(2,1)S(1)} all-to-all(bf16[8,264,128]{2,1,0:T(8,128)(2,1)S(1)} %merge.2), channel_id=1, replica_groups={{0,2,4,6,8,10,12,14},{15,13,11,9,7,5,3,1},{16,18,20,22,24,26,28,30},{31..., dimensions={0} | all-to-all | bytes 1081344 | tf_op jit(solution)/shard_map/all_to_all | solution.py:35
  134.8 2.1 %collective-permute-start.1 = (bf16[8,264,128]{2,1,0:T(8,128)(2,1)S(1)}, bf16[8,264,128]{2,1,0:T(8,128)(2,1)S(1)}, u32[]{:S(2)}, u32[]{:S(2)}) collective-permute-start(bf16[8,264,128]{2,1,0:T(8,128)(2,1)S(1)} %all_to_all.36.own_ref), channel_id=1, source_target_pairs={{0,1},{1,0},{2,3},{3,2},{4,5},{5,4},{6,7},{7,6},{8,9},{9,8},{10,11... | collective-permute-start | bytes 1622024 | tf_op jit(solution)/shard_map/ppermute | solution.py:379
  136.9 1.7 collective-permute-done.1.other_ref
  138.6 3.6 %second_sums.1 = (bf16[512,1024]{1,0:T(8,128)(2,1)}, f32[4,128]{1,0:T(4,128)}, bf16[4,8,136,128]{3,2,1,0:T(8,128)(2,1)S(1)}) custom-call(s32[1]{0:T(128)} %bitcast.3.core_ref, bf16[1024,1152]{1,0:T(8,128)(2,1)S(1)} %copy-done.8, bf16[8,264,128]{2,1,0:T(8,128)(2,1)S(1)} %all_to_all.36.own_ref, bf16[8,264,128]{2,1,0:T(8,128)(2,1)S(1)} %collective-permute-done.1.other_ref), custom_call_target="tpu_custom_call" | custom-call | flops 2147483648 | bytes 5605380 | tf_op jit(solution)/shard_map/second_sums/pallas_call | solution.py:56
  142.2 19.1 %all_to_all.37 = bf16[4,8,136,128]{3,2,1,0:T(8,128)(2,1)S(1)} all-to-all(bf16[4,8,136,128]{3,2,1,0:T(8,128)(2,1)S(1)} %get-tuple-element.26), channel_id=1, replica_groups={{0,16,32,48},{49,33,17,1},{2,18,34,50},{51,35,19,3},{4,20,36,52},{53,37..., dimensions={0} | all-to-all | bytes 2228224 | tf_op jit(solution)/shard_map/all_to_all | solution.py:35
  161.3 0.9 reduce_sum.31
  162.2 3.9 %all-to-all-start.4 = ((bf16[8,136,128]{2,1,0:T(8,128)(2,1)}), bf16[8,136,128]{2,1,0:T(8,128)(2,1)S(1)}, u32[]{:S(2)}, u32[]{:S(2)}) async-start(bf16[8,136,128]{2,1,0:T(8,128)(2,1)} %reduce_sum.31), calls=%async_computation.4 | async-start | bytes 557056 | tf_op jit(solution)/shard_map/all_to_all | solution.py:24
  166.1 0.3 multiply_reduce_fusion
  166.4 1.7 copy-done.9
  168.0 3.3 %margins_two.1.costs_ref = bf16[8,128]{1,0:T(8,128)(2,1)S(1)} custom-call(bf16[1024,1152]{1,0:T(8,128)(2,1)S(1)} %copy-done.9, bf16[512,1024]{1,0:T(8,128)(2,1)S(1)} %copy-done.6, bf16[512,1024]{1,0:T(8,128)(2,1)S(1)} %bitcast.18, f32[1,512]{1,0:T(1,128)S(1)} %bitcast.21), custom_call_target="tpu_custom_call" | custom-call | flops 2147483648 | bytes 4460544 | tf_op jit(solution)/shard_map/margins_two/pallas_call | solution.py:56
  171.3 5.9 %all-to-all-done.4.arrived_ref = bf16[8,136,128]{2,1,0:T(8,128)(2,1)S(1)} async-done(((bf16[8,136,128]{2,1,0:T(8,128)(2,1)}), bf16[8,136,128]{2,1,0:T(8,128)(2,1)S(1)}, u32[]{:S(2)}, u32[]{:S(2)}) %all-to-all-start.4) | async-done | bytes 278560 | tf_op jit(solution)/shard_map/all_to_all | solution.py:24
  177.3 0.1 merge.3
  177.4 13.1 %all_to_all.38 = bf16[8,136,128]{2,1,0:T(8,128)(2,1)S(1)} all-to-all(bf16[8,136,128]{2,1,0:T(8,128)(2,1)S(1)} %merge.3), channel_id=1, replica_groups=mesh['z'=8,'x'=4,'y'=8,'core'=2] {'z'}, dimensions={0} | all-to-all | bytes 557056 | tf_op jit(solution)/shard_map/all_to_all | solution.py:24
  190.5 0.1 broadcast_in_dim.33
  190.6 16.6 %all_to_all.39.full_ref = bf16[4,8,136,128]{3,2,1,0:T(8,128)(2,1)S(1)} all-to-all(bf16[4,8,136,128]{3,2,1,0:T(8,128)(2,1)S(1)} %broadcast_in_dim.33), channel_id=1, replica_groups={{0,16,32,48},{49,33,17,1},{2,18,34,50},{51,35,19,3},{4,20,36,52},{53,37..., dimensions={0} | all-to-all | bytes 2228224 | tf_op jit(solution)/shard_map/all_to_all | solution.py:35
  207.2 1.2 last.1
  (14 shorter events, 0.0 us)
Async XLA Ops:
  0.6 1.2 copy-start.2
  1.9 0.7 copy-start.3
  2.5 0.7 copy-start.4
  3.2 0.7 copy-start.5
  84.5 13.9 %copy-start = (bf16[1,512,1024]{2,1,0:T(8,128)(2,1)S(1)}, bf16[1,512,1024]{2,1,0:T(8,128)(2,1)}, u32[]{:S(2)}) copy-start(bf16[1,512,1024]{2,1,0:T(8,128)(2,1)} %param.10) | copy-start | bytes 3145732
  84.5 5.5 %collective-permute-start = (bf16[8,264,128]{2,1,0:T(8,128)(2,1)S(1)}, bf16[8,264,128]{2,1,0:T(8,128)(2,1)S(1)}, u32[]{:S(2)}, u32[]{:S(2)}) collective-permute-start(bf16[8,264,128]{2,1,0:T(8,128)(2,1)S(1)} %get-tuple-element.22), channel_id=1, source_target_pairs={{0,1},{1,0},{2,3},{3,2},{4,5},{5,4},{6,7},{7,6},{8,9},{9,8},{10,11... | collective-permute-start | bytes 1622024 | tf_op jit(solution)/shard_map/ppermute | solution.py:374
  90.9 21.9 %all-to-all-start.1 = ((bf16[8,264,128]{2,1,0:T(8,128)(2,1)}), bf16[8,264,128]{2,1,0:T(8,128)(2,1)}, u32[]{:S(2)}, u32[]{:S(2)}) async-start(bf16[8,264,128]{2,1,0:T(8,128)(2,1)} %add_convert_fusion), calls=%async_computation.1 | async-start | bytes 1081344 | tf_op jit(solution)/shard_map/all_to_all | solution.py:35
  101.2 1.4 copy-start.7
  112.8 25.8 %copy-start.8 = (bf16[1024,1152]{1,0:T(8,128)(2,1)S(1)}, bf16[1024,1152]{1,0:T(8,128)(2,1)}, u32[]{:S(2)}) copy-start(bf16[1024,1152]{1,0:T(8,128)(2,1)} %copy-done.7) | copy-start | bytes 7077892
  134.8 3.8 %collective-permute-start.1 = (bf16[8,264,128]{2,1,0:T(8,128)(2,1)S(1)}, bf16[8,264,128]{2,1,0:T(8,128)(2,1)S(1)}, u32[]{:S(2)}, u32[]{:S(2)}) collective-permute-start(bf16[8,264,128]{2,1,0:T(8,128)(2,1)S(1)} %all_to_all.36.own_ref), channel_id=1, source_target_pairs={{0,1},{1,0},{2,3},{3,2},{4,5},{5,4},{6,7},{7,6},{8,9},{9,8},{10,11... | collective-permute-start | bytes 1622024 | tf_op jit(solution)/shard_map/ppermute | solution.py:379
  142.2 23.9 %copy-start.1 = (bf16[1,512,1024]{2,1,0:T(8,128)(2,1)S(1)}, bf16[1,512,1024]{2,1,0:T(8,128)(2,1)}, u32[]{:S(2)}) copy-start(bf16[1,512,1024]{2,1,0:T(8,128)(2,1)} %param.11) | copy-start | bytes 3145732
  142.2 24.2 %copy-start.6 = (bf16[512,1024]{1,0:T(8,128)(2,1)S(1)}, bf16[512,1024]{1,0:T(8,128)(2,1)}, u32[]{:S(2)}) copy-start(bf16[512,1024]{1,0:T(8,128)(2,1)} %get-tuple-element.24.centers_ref) | copy-start | bytes 3145732
  162.2 15.1 %all-to-all-start.4 = ((bf16[8,136,128]{2,1,0:T(8,128)(2,1)}), bf16[8,136,128]{2,1,0:T(8,128)(2,1)S(1)}, u32[]{:S(2)}, u32[]{:S(2)}) async-start(bf16[8,136,128]{2,1,0:T(8,128)(2,1)} %reduce_sum.31), calls=%async_computation.4 | async-start | bytes 557056 | tf_op jit(solution)/shard_map/all_to_all | solution.py:24
  166.4 1.7 copy-start.9

commit v7 on v6

--- a/solution.py
+++ b/solution.py
@@ -24,16 +24,11 @@
     return lax.all_to_all(blocks, axes, split_axis=0, concat_axis=0, tiled=True)
 
 
-def mirrored(blocks, axes, outer):
-    n = lax.axis_size(axes[0])
-    low = lax.axis_size(axes[1:]) // outer
-    groups = []
-    for index in range(outer):
-        base = index * low
-        groups.append([i * outer * low + base for i in range(n)])
-        groups.append([(n - 1 - i) * outer * low + base + 1 for i in range(n)])
+def mirrored(blocks):
+    n = lax.axis_size("y")
+    groups = [[2 * i for i in range(n)], [2 * (n - 1 - i) + 1 for i in range(n)]]
     return lax.all_to_all(
-        blocks, axes, split_axis=0, concat_axis=0, tiled=True, axis_index_groups=groups
+        blocks, GROUP, split_axis=0, concat_axis=0, tiled=True, axis_index_groups=groups
     )
 
 
@@ -73,12 +68,10 @@
     return mask.astype(F32).astype(BF16)
 
 
-def place_body(keys_ref, one_ref, two_ref, emb_ref, out_ref, wide_ref):
+def place_body(info_ref, emb_ref, out_ref, wide_ref):
     count, width = emb_ref.shape
     devices, slots, wide = out_ref.shape
-    info = jnp.concatenate(
-        [keys_ref[...], one_ref[...], two_ref[...], jnp.zeros((5, count), jnp.int32)], axis=0
-    )
+    info = info_ref[...]
     turned = jnp.transpose(info.astype(F32)).astype(jnp.int32)
     keys_row, keys_col = info[0:1, :], turned[:, 0:1]
     earlier = (keys_col == keys_row) & (iota((count, count), 0) < iota((count, count), 1))
@@ -98,7 +91,7 @@
         out_ref[piece * block : (piece + 1) * block] = moved.reshape(block, slots, wide)
 
 
-def place(keys, one, two, embeddings, devices):
+def place(info, embeddings, devices):
     count, width = embeddings.shape
     wide = width + LANES
     return kernel_call(
@@ -106,7 +99,7 @@
         "place",
         2 * devices * SLOTS * count * wide,
         [shaped((devices, SLOTS, wide))],
-        [keys, one, two, embeddings],
+        [info, embeddings],
         scratch=[pltpu.VMEM((count, wide), BF16)],
     )[0]
 
@@ -290,13 +283,11 @@
     for j in range(width // LANES):
         piece = sums[:, j * LANES : (j + 1) * LANES].astype(BF16).reshape(nz, nx, each, LANES)
         for x in range(nx):
-            out_ref[mirror(x, nx, core), :, j * each : (j + 1) * each, :] = piece[:, x]
+            out_ref[x, :, j * each : (j + 1) * each, :] = piece[:, x]
     for z in range(nz):
         for x in range(nx):
             chunk = (z * nx + x) * each // LANES * LANES
-            out_ref[mirror(x, nx, core), z, tall - EXTRA :, :] = counts[
-                :, chunk : chunk + LANES
-            ].astype(BF16)
+            out_ref[x, z, tall - EXTRA :, :] = counts[:, chunk : chunk + LANES].astype(BF16)
 
 
 def second_sums(core, rows, own, other, children, nx, nz):
@@ -317,14 +308,13 @@
     )
 
 
-def last_body(core_ref, full_ref, new_ref, cost_ref):
+def last_body(full_ref, new_ref, cost_ref):
     nx, nz, tall, _ = full_ref.shape
     children, width = new_ref.shape
     each = children // (nx * nz)
     for x in range(nx):
         for z in range(nz):
-            block = z * nx + mirror(x, nx, core_ref[0])
-            at = pl.ds(pl.multiple_of(block * each, each), each)
+            at = slice((z * nx + x) * each, (z * nx + x + 1) * each)
             for j in range(width // LANES):
                 lanes = slice(j * LANES, (j + 1) * LANES)
                 new_ref[at, lanes] = full_ref[x, z, j * each : (j + 1) * each, :]
@@ -332,14 +322,13 @@
     cost_ref[...] = sum(cost_sum(full_ref[x, :, tall - EXTRA :, :], chunks) for x in range(nx))
 
 
-def last(core, full, children, width):
+def last(full, children, width):
     return kernel_call(
         last_body,
         "last",
         full.size,
         [shaped((children, width)), shaped((children // LANES, LANES), F32)],
-        [core, full],
-        scalars=1,
+        [full],
     )
 
 
@@ -360,33 +349,29 @@
     group = lax.axis_index(GROUP).astype(jnp.int32)[None]
     shard = lax.axis_index(SHARD).astype(jnp.int32)[None]
 
-    layout = place(
-        cluster_key.reshape(1, rows_dev),
-        child_first.reshape(1, rows_dev),
-        child_second.reshape(1, rows_dev),
-        embeddings,
-        devices,
-    )
+    info = jnp.stack(
+        [cluster_key[:, 0], child_first, child_second] + [jnp.zeros((rows_dev,), jnp.int32)] * 5
+    )
+    layout = place(info, embeddings, devices)
     layout, core, group, shard = lax.optimization_barrier((layout, core, group, shard))
     arrived = exchange(layout, ALL)
 
     keep, send = first_sums(core, arrived, children, n_group)
     taken = lax.ppermute(send, "core", SWAP)
-    parts_one = mirrored((keep.astype(F32) + taken.astype(F32)).astype(BF16), GROUP, 1)
+    parts_one = mirrored((keep.astype(F32) + taken.astype(F32)).astype(BF16))
     costs_one, rows = margins_one(arrived, coarse, squares_of(coarse))
     copies_one = merge(group, parts_one, coarse, costs_one, lax.axis_size("y"))
-    own = mirrored(copies_one, GROUP, 1)
+    own = mirrored(copies_one)
     other = lax.ppermute(own, "core", SWAP)
 
     nx, nz = lax.axis_size("x"), lax.axis_size("z")
     coarse_new, coarse_cost, partial_two = second_sums(core, rows, own, other, children, nx, nz)
-    parts_two = jnp.sum(mirrored(partial_two, ("x",) + GROUP, n_group // 2).astype(F32), axis=0).astype(BF16)
+    parts_two = jnp.sum(exchange(partial_two, "x").astype(F32), axis=0).astype(BF16)
     parts_two = exchange(parts_two, "z")
     costs_two = margins_two(rows, coarse_new, fine, squares_of(fine))
     copies_two = exchange(merge(shard, parts_two, fine, costs_two, nz), "z")
     full_two = jnp.broadcast_to(copies_two[None], (nx,) + copies_two.shape)
-    full_two = mirrored(full_two, ("x",) + GROUP, n_group // 2)
-    fine_new, fine_cost = last(core, full_two, children, width)
+    fine_new, fine_cost = last(exchange(full_two, "x"), children, width)
     return (
         coarse_new[None],
         fine_new[None],

time: 209 us -> 207 us (level)
    all_to_all x3 -> x1, blocking collectives: 56.3 us -> 20.6 us  [mirrored(): lax.all_to_all(blocks, GROUP, split_axis=0, concat_axis=0, tiled=True, ax...]
    all_to_all x2 -> x4, blocking collectives: 90 us -> 125 us  [exchange(): return lax.all_to_all(blocks, axes, split_axis=0, concat_axis=0, tiled=True)]
    unnamed x20 -> x14, local copies, waits for them, and re-layouts: 6.34 us -> 4.3 us
where the time goes in v7:
time: 207 us; the launch traced here: 206 us
  blocking collectives  145 us (70%)
  waiting for transfers between devices  19.5 us (9%)
  starting transfers between devices  17.3 us (8%)
  Pallas kernels  15.6 us (8%)
  local copies, waits for them, and re-layouts  5.19 us (3%)
  other arithmetic  2.42 us (1%)
    all_to_all x4, blocking collectives, exchange(): return lax.all_to_all(blocks, axes, split_axis=0, concat_axis=0, tiled=True)  125 us
    all_to_all x1, blocking collectives, mirrored(): lax.all_to_all(blocks, GROUP, split_axis=0, concat_axis=0, tiled=True, ax...  20.6 us
    pallas_call x8, Pallas kernels, kernel_call(): pl.pallas_call(body, name=name, in_specs=specs, out_specs=[pl.BlockSpec(m...  15.6 us
    all_to_all x1, waiting for transfers between devices, mirrored(): lax.all_to_all(blocks, GROUP, split_axis=0, concat_axis=0, tiled=True, ax...  10.1 us
    all_to_all x1, starting transfers between devices, mirrored(): lax.all_to_all(blocks, GROUP, split_axis=0, concat_axis=0, tiled=True, ax...  7.44 us
    all_to_all x1, waiting for transfers between devices, exchange(): return lax.all_to_all(blocks, axes, split_axis=0, concat_axis=0, tiled=True)  6.1 us
    unnamed x14, local copies, waits for them, and re-layouts  4.3 us
  transfers between devices with their start and end apart: 4, of which 4 were waited for; matrix products, arithmetic and copies ran while one was open for 0% of the time, Pallas kernels for 3%

profile of v7, /device:TPU:56, one launch (start us, length us, event | category | flops | bytes accessed | tf_op | source)
XLA Modules:
  0.0 206.2 jit_solution(395005203695697414)
XLA Ops:
  0.7 0.7 stack.15.info_ref
  1.4 0.0 copy-start.2
  1.4 1.2 copy-done.2
  2.6 2.0 place.1
  4.7 76.9 %all_to_all.35.arrived_ref = bf16[512,2,1152]{2,1,0:T(2,128)(2,1)S(1)} all-to-all(bf16[512,2,1152]{2,1,0:T(2,128)(2,1)S(1)} %place.1), channel_id=1, replica_groups=mesh['z'=8,'x'=4,'y'=8,'core'=2] {'z','x','y','core'}, dimensions={0} | all-to-all | bytes 4718592 | tf_op jit(solution)/shard_map/all_to_all | solution.py:24
  81.6 1.6 first_sums.1
  83.2 3.9 %collective-permute-start = (bf16[8,264,128]{2,1,0:T(8,128)(2,1)S(1)}, bf16[8,264,128]{2,1,0:T(8,128)(2,1)S(1)}, u32[]{:S(2)}, u32[]{:S(2)}) collective-permute-start(bf16[8,264,128]{2,1,0:T(8,128)(2,1)S(1)} %get-tuple-element.22), channel_id=1, source_target_pairs={{0,1},{1,0},{2,3},{3,2},{4,5},{5,4},{6,7},{7,6},{8,9},{9,8},{10,11... | collective-permute-start | bytes 1622024 | tf_op jit(solution)/shard_map/ppermute | solution.py:360
  87.1 1.5 collective-permute-done
  88.6 0.9 add_convert_fusion
  89.6 7.4 %all-to-all-start.1 = ((bf16[8,264,128]{2,1,0:T(8,128)(2,1)}), bf16[8,264,128]{2,1,0:T(8,128)(2,1)}, u32[]{:S(2)}, u32[]{:S(2)}) async-start(bf16[8,264,128]{2,1,0:T(8,128)(2,1)} %add_convert_fusion), calls=%async_computation.1 | async-start | bytes 1081344 | tf_op jit(solution)/shard_map/all_to_all | solution.py:30
  97.0 0.0 copy-done
  97.0 0.3 multiply_reduce_fusion.1
  97.3 2.6 %margins_one.1 = (bf16[8,128]{1,0:T(8,128)(2,1)S(1)}, bf16[1024,1152]{1,0:T(8,128)(2,1)S(1)}) custom-call(bf16[512,2,1152]{2,1,0:T(2,128)(2,1)S(1)} %all_to_all.35.arrived_ref, bf16[512,1024]{1,0:T(8,128)(2,1)S(1)} %bitcast.16, f32[1,512]{1,0:T(1,128)S(1)} %bitcast.20), custom_call_target="tpu_custom_call" | custom-call | flops 1073741824 | bytes 5771264 | tf_op jit(solution)/shard_map/margins_one/pallas_call | solution.py:51
  100.0 1.4 copy-done.4
  101.4 10.1 %all-to-all-done.1.arrived_ref = bf16[8,264,128]{2,1,0:T(8,128)(2,1)} async-done(((bf16[8,264,128]{2,1,0:T(8,128)(2,1)}), bf16[8,264,128]{2,1,0:T(8,128)(2,1)}, u32[]{:S(2)}, u32[]{:S(2)}) %all-to-all-start.1) | async-done | bytes 540704 | tf_op jit(solution)/shard_map/all_to_all | solution.py:30
  111.5 1.3 merge.2
  112.9 20.6 %all_to_all.36.own_ref = bf16[8,264,128]{2,1,0:T(8,128)(2,1)S(1)} all-to-all(bf16[8,264,128]{2,1,0:T(8,128)(2,1)S(1)} %merge.2), channel_id=1, replica_groups={{0,2,4,6,8,10,12,14},{15,13,11,9,7,5,3,1},{16,18,20,22,24,26,28,30},{31..., dimensions={0} | all-to-all | bytes 1081344 | tf_op jit(solution)/shard_map/all_to_all | solution.py:30
  133.5 2.1 %collective-permute-start.1 = (bf16[8,264,128]{2,1,0:T(8,128)(2,1)S(1)}, bf16[8,264,128]{2,1,0:T(8,128)(2,1)S(1)}, u32[]{:S(2)}, u32[]{:S(2)}) collective-permute-start(bf16[8,264,128]{2,1,0:T(8,128)(2,1)S(1)} %all_to_all.36.own_ref), channel_id=1, source_target_pairs={{0,1},{1,0},{2,3},{3,2},{4,5},{5,4},{6,7},{7,6},{8,9},{9,8},{10,11... | collective-permute-start | bytes 1622024 | tf_op jit(solution)/shard_map/ppermute | solution.py:365
  135.6 1.7 collective-permute-done.1.other_ref
  137.3 3.5 %second_sums.1 = (bf16[512,1024]{1,0:T(8,128)(2,1)}, f32[4,128]{1,0:T(4,128)}, bf16[4,8,136,128]{3,2,1,0:T(8,128)(2,1)S(1)}) custom-call(s32[1]{0:T(128)} %bitcast.3.core_ref, bf16[1024,1152]{1,0:T(8,128)(2,1)S(1)} %copy-done.5, bf16[8,264,128]{2,1,0:T(8,128)(2,1)S(1)} %all_to_all.36.own_ref, bf16[8,264,128]{2,1,0:T(8,128)(2,1)S(1)} %collective-permute-done.1.other_ref), custom_call_target="tpu_custom_call" | custom-call | flops 2147483648 | bytes 5605380 | tf_op jit(solution)/shard_map/second_sums/pallas_call | solution.py:51
  140.8 19.6 %all_to_all.37 = bf16[4,8,136,128]{3,2,1,0:T(8,128)(2,1)S(1)} all-to-all(bf16[4,8,136,128]{3,2,1,0:T(8,128)(2,1)S(1)} %get-tuple-element.26), channel_id=1, replica_groups=mesh['z'=8,'x'=4,'y'=8,'core'=2] {'x'}, dimensions={0} | all-to-all | bytes 2228224 | tf_op jit(solution)/shard_map/all_to_all | solution.py:24
  160.4 0.9 reduce_sum.31
  161.3 3.8 %all-to-all-start.4 = ((bf16[8,136,128]{2,1,0:T(8,128)(2,1)}), bf16[8,136,128]{2,1,0:T(8,128)(2,1)S(1)}, u32[]{:S(2)}, u32[]{:S(2)}) async-start(bf16[8,136,128]{2,1,0:T(8,128)(2,1)} %reduce_sum.31), calls=%async_computation.4 | async-start | bytes 557056 | tf_op jit(solution)/shard_map/all_to_all | solution.py:24
  165.2 0.3 multiply_reduce_fusion
  165.4 1.7 copy-done.6
  167.1 3.3 %margins_two.1.costs_ref = bf16[8,128]{1,0:T(8,128)(2,1)S(1)} custom-call(bf16[1024,1152]{1,0:T(8,128)(2,1)S(1)} %copy-done.6, bf16[512,1024]{1,0:T(8,128)(2,1)S(1)} %copy-done.3, bf16[512,1024]{1,0:T(8,128)(2,1)S(1)} %bitcast.18, f32[1,512]{1,0:T(1,128)S(1)} %bitcast.21), custom_call_target="tpu_custom_call" | custom-call | flops 2147483648 | bytes 4460544 | tf_op jit(solution)/shard_map/margins_two/pallas_call | solution.py:51
  170.4 6.1 %all-to-all-done.4.arrived_ref = bf16[8,136,128]{2,1,0:T(8,128)(2,1)S(1)} async-done(((bf16[8,136,128]{2,1,0:T(8,128)(2,1)}), bf16[8,136,128]{2,1,0:T(8,128)(2,1)S(1)}, u32[]{:S(2)}, u32[]{:S(2)}) %all-to-all-start.4) | async-done | bytes 278560 | tf_op jit(solution)/shard_map/all_to_all | solution.py:24
  176.5 0.1 merge.3
  176.6 13.1 %all_to_all.38 = bf16[8,136,128]{2,1,0:T(8,128)(2,1)S(1)} all-to-all(bf16[8,136,128]{2,1,0:T(8,128)(2,1)S(1)} %merge.3), channel_id=1, replica_groups=mesh['z'=8,'x'=4,'y'=8,'core'=2] {'z'}, dimensions={0} | all-to-all | bytes 557056 | tf_op jit(solution)/shard_map/all_to_all | solution.py:24
  189.7 0.1 broadcast_in_dim.33
  189.8 15.2 %all_to_all.39.full_ref = bf16[4,8,136,128]{3,2,1,0:T(8,128)(2,1)S(1)} all-to-all(bf16[4,8,136,128]{3,2,1,0:T(8,128)(2,1)S(1)} %broadcast_in_dim.33), channel_id=1, replica_groups=mesh['z'=8,'x'=4,'y'=8,'core'=2] {'x'}, dimensions={0} | all-to-all | bytes 2228224 | tf_op jit(solution)/shard_map/all_to_all | solution.py:24
  205.1 1.2 last.1
  (11 shorter events, 0.0 us)
Async XLA Ops:
  1.4 1.2 copy-start.2
  83.2 13.9 %copy-start = (bf16[1,512,1024]{2,1,0:T(8,128)(2,1)S(1)}, bf16[1,512,1024]{2,1,0:T(8,128)(2,1)}, u32[]{:S(2)}) copy-start(bf16[1,512,1024]{2,1,0:T(8,128)(2,1)} %param.10) | copy-start | bytes 3145732
  83.2 5.5 %collective-permute-start = (bf16[8,264,128]{2,1,0:T(8,128)(2,1)S(1)}, bf16[8,264,128]{2,1,0:T(8,128)(2,1)S(1)}, u32[]{:S(2)}, u32[]{:S(2)}) collective-permute-start(bf16[8,264,128]{2,1,0:T(8,128)(2,1)S(1)} %get-tuple-element.22), channel_id=1, source_target_pairs={{0,1},{1,0},{2,3},{3,2},{4,5},{5,4},{6,7},{7,6},{8,9},{9,8},{10,11... | collective-permute-start | bytes 1622024 | tf_op jit(solution)/shard_map/ppermute | solution.py:360
  89.6 21.9 %all-to-all-start.1 = ((bf16[8,264,128]{2,1,0:T(8,128)(2,1)}), bf16[8,264,128]{2,1,0:T(8,128)(2,1)}, u32[]{:S(2)}, u32[]{:S(2)}) async-start(bf16[8,264,128]{2,1,0:T(8,128)(2,1)} %add_convert_fusion), calls=%async_computation.1 | async-start | bytes 1081344 | tf_op jit(solution)/shard_map/all_to_all | solution.py:30
  99.9 1.4 copy-start.4
  111.5 25.8 %copy-start.5 = (bf16[1024,1152]{1,0:T(8,128)(2,1)S(1)}, bf16[1024,1152]{1,0:T(8,128)(2,1)}, u32[]{:S(2)}) copy-start(bf16[1024,1152]{1,0:T(8,128)(2,1)} %copy-done.4) | copy-start | bytes 7077892
  133.5 3.8 %collective-permute-start.1 = (bf16[8,264,128]{2,1,0:T(8,128)(2,1)S(1)}, bf16[8,264,128]{2,1,0:T(8,128)(2,1)S(1)}, u32[]{:S(2)}, u32[]{:S(2)}) collective-permute-start(bf16[8,264,128]{2,1,0:T(8,128)(2,1)S(1)} %all_to_all.36.own_ref), channel_id=1, source_target_pairs={{0,1},{1,0},{2,3},{3,2},{4,5},{5,4},{6,7},{7,6},{8,9},{9,8},{10,11... | collective-permute-start | bytes 1622024 | tf_op jit(solution)/shard_map/ppermute | solution.py:365
  140.8 24.3 %copy-start.1 = (bf16[1,512,1024]{2,1,0:T(8,128)(2,1)S(1)}, bf16[1,512,1024]{2,1,0:T(8,128)(2,1)}, u32[]{:S(2)}) copy-start(bf16[1,512,1024]{2,1,0:T(8,128)(2,1)} %param.11) | copy-start | bytes 3145732
  140.8 24.6 %copy-start.3 = (bf16[512,1024]{1,0:T(8,128)(2,1)S(1)}, bf16[512,1024]{1,0:T(8,128)(2,1)}, u32[]{:S(2)}) copy-start(bf16[512,1024]{1,0:T(8,128)(2,1)} %get-tuple-element.24.centers_ref) | copy-start | bytes 3145732
  161.3 15.2 %all-to-all-start.4 = ((bf16[8,136,128]{2,1,0:T(8,128)(2,1)}), bf16[8,136,128]{2,1,0:T(8,128)(2,1)S(1)}, u32[]{:S(2)}, u32[]{:S(2)}) async-start(bf16[8,136,128]{2,1,0:T(8,128)(2,1)} %reduce_sum.31), calls=%async_computation.4 | async-start | bytes 557056 | tf_op jit(solution)/shard_map/all_to_all | solution.py:24
  165.4 1.7 copy-start.6

commit v8 on v7

--- a/solution.py
+++ b/solution.py
@@ -366,9 +366,10 @@
 
     nx, nz = lax.axis_size("x"), lax.axis_size("z")
     coarse_new, coarse_cost, partial_two = second_sums(core, rows, own, other, children, nx, nz)
-    parts_two = jnp.sum(exchange(partial_two, "x").astype(F32), axis=0).astype(BF16)
-    parts_two = exchange(parts_two, "z")
+    parts_two = exchange(partial_two, "x")
     costs_two = margins_two(rows, coarse_new, fine, squares_of(fine))
+    parts_two, costs_two = lax.optimization_barrier((parts_two, costs_two))
+    parts_two = exchange(jnp.sum(parts_two.astype(F32), axis=0).astype(BF16), "z")
     copies_two = exchange(merge(shard, parts_two, fine, costs_two, nz), "z")
     full_two = jnp.broadcast_to(copies_two[None], (nx,) + copies_two.shape)
     fine_new, fine_cost = last(exchange(full_two, "x"), children, width)

time: 207 us -> 208 us (level)
  waiting for transfers between devices: 19.5 us -> 24.4 us
  blocking collectives: 145 us -> 142 us
    all_to_all x1, waiting for transfers between devices: 6.1 us -> 11 us  [exchange(): return lax.all_to_all(blocks, axes, split_axis=0, concat_axis=0, tiled=True)]
    all_to_all x4, blocking collectives: 125 us -> 122 us  [exchange(): return lax.all_to_all(blocks, axes, split_axis=0, concat_axis=0, tiled=True)]
where the time goes in v8:
time: 208 us
  blocking collectives  142 us (68%)
  waiting for transfers between devices  24.4 us (12%)
  starting transfers between devices  17.2 us (8%)
  Pallas kernels  16.2 us (8%)
  local copies, waits for them, and re-layouts  5.19 us (2%)
    all_to_all x4, blocking collectives, exchange(): return lax.all_to_all(blocks, axes, split_axis=0, concat_axis=0, tiled=True)  122 us
    all_to_all x1, blocking collectives, mirrored(): lax.all_to_all(blocks, GROUP, split_axis=0, concat_axis=0, tiled=True, ax...  20.6 us
    pallas_call x8, Pallas kernels, kernel_call(): pl.pallas_call(body, name=name, in_specs=specs, out_specs=[pl.BlockSpec(m...  16.2 us
    all_to_all x1, waiting for transfers between devices, exchange(): return lax.all_to_all(blocks, axes, split_axis=0, concat_axis=0, tiled=True)  11 us
    all_to_all x1, waiting for transfers between devices, mirrored(): lax.all_to_all(blocks, GROUP, split_axis=0, concat_axis=0, tiled=True, ax...  10.1 us
    all_to_all x1, starting transfers between devices, mirrored(): lax.all_to_all(blocks, GROUP, split_axis=0, concat_axis=0, tiled=True, ax...  7.44 us
    unnamed x14, local copies, waits for them, and re-layouts  4.3 us
  transfers between devices with their start and end apart: 4, of which 4 were waited for; matrix products, arithmetic and copies ran while one was open for 0% of the time, Pallas kernels for 3%

profile of v8, /device:TPU:56, one launch (start us, length us, event | category | flops | bytes accessed | tf_op | source)
XLA Modules:
  0.0 207.7 jit_solution(9786922370683092718)
XLA Ops:
  0.7 0.7 stack.15.info_ref
  1.4 0.0 copy-start.2
  1.4 1.2 copy-done.2
  2.6 2.0 place.1
  4.7 76.9 %all_to_all.35.arrived_ref = bf16[512,2,1152]{2,1,0:T(2,128)(2,1)S(1)} all-to-all(bf16[512,2,1152]{2,1,0:T(2,128)(2,1)S(1)} %place.1), channel_id=1, replica_groups=mesh['z'=8,'x'=4,'y'=8,'core'=2] {'z','x','y','core'}, dimensions={0} | all-to-all | bytes 4718592 | tf_op jit(solution)/shard_map/all_to_all | solution.py:24
  81.6 1.6 first_sums.1
  83.2 3.9 %collective-permute-start = (bf16[8,264,128]{2,1,0:T(8,128)(2,1)S(1)}, bf16[8,264,128]{2,1,0:T(8,128)(2,1)S(1)}, u32[]{:S(2)}, u32[]{:S(2)}) collective-permute-start(bf16[8,264,128]{2,1,0:T(8,128)(2,1)S(1)} %get-tuple-element.24), channel_id=1, source_target_pairs={{0,1},{1,0},{2,3},{3,2},{4,5},{5,4},{6,7},{7,6},{8,9},{9,8},{10,11... | collective-permute-start | bytes 1622024 | tf_op jit(solution)/shard_map/ppermute | solution.py:360
  87.1 1.5 collective-permute-done
  88.6 0.9 add_convert_fusion
  89.6 7.4 %all-to-all-start.1 = ((bf16[8,264,128]{2,1,0:T(8,128)(2,1)}), bf16[8,264,128]{2,1,0:T(8,128)(2,1)}, u32[]{:S(2)}, u32[]{:S(2)}) async-start(bf16[8,264,128]{2,1,0:T(8,128)(2,1)} %add_convert_fusion), calls=%async_computation.1 | async-start | bytes 1081344 | tf_op jit(solution)/shard_map/all_to_all | solution.py:30
  97.0 0.0 copy-done
  97.0 0.3 multiply_reduce_fusion.1
  97.3 2.6 %margins_one.1 = (bf16[8,128]{1,0:T(8,128)(2,1)S(1)}, bf16[1024,1152]{1,0:T(8,128)(2,1)S(1)}) custom-call(bf16[512,2,1152]{2,1,0:T(2,128)(2,1)S(1)} %all_to_all.35.arrived_ref, bf16[512,1024]{1,0:T(8,128)(2,1)S(1)} %bitcast.16, f32[1,512]{1,0:T(1,128)S(1)} %bitcast.20), custom_call_target="tpu_custom_call" | custom-call | flops 1073741824 | bytes 5771264 | tf_op jit(solution)/shard_map/margins_one/pallas_call | solution.py:51
  100.0 1.4 copy-done.4
  101.4 10.1 %all-to-all-done.1.arrived_ref = bf16[8,264,128]{2,1,0:T(8,128)(2,1)} async-done(((bf16[8,264,128]{2,1,0:T(8,128)(2,1)}), bf16[8,264,128]{2,1,0:T(8,128)(2,1)}, u32[]{:S(2)}, u32[]{:S(2)}) %all-to-all-start.1) | async-done | bytes 540704 | tf_op jit(solution)/shard_map/all_to_all | solution.py:30
  111.5 1.3 merge.2
  112.9 20.6 %all_to_all.36.own_ref = bf16[8,264,128]{2,1,0:T(8,128)(2,1)S(1)} all-to-all(bf16[8,264,128]{2,1,0:T(8,128)(2,1)S(1)} %merge.2), channel_id=1, replica_groups={{0,2,4,6,8,10,12,14},{15,13,11,9,7,5,3,1},{16,18,20,22,24,26,28,30},{31..., dimensions={0} | all-to-all | bytes 1081344 | tf_op jit(solution)/shard_map/all_to_all | solution.py:30
  133.5 2.1 %collective-permute-start.1 = (bf16[8,264,128]{2,1,0:T(8,128)(2,1)S(1)}, bf16[8,264,128]{2,1,0:T(8,128)(2,1)S(1)}, u32[]{:S(2)}, u32[]{:S(2)}) collective-permute-start(bf16[8,264,128]{2,1,0:T(8,128)(2,1)S(1)} %all_to_all.36.own_ref), channel_id=1, source_target_pairs={{0,1},{1,0},{2,3},{3,2},{4,5},{5,4},{6,7},{7,6},{8,9},{9,8},{10,11... | collective-permute-start | bytes 1622024 | tf_op jit(solution)/shard_map/ppermute | solution.py:365
  135.6 1.7 collective-permute-done.1.other_ref
  137.3 4.0 %second_sums.1 = (bf16[512,1024]{1,0:T(8,128)(2,1)}, f32[4,128]{1,0:T(4,128)}, bf16[4,8,136,128]{3,2,1,0:T(8,128)(2,1)}) custom-call(s32[1]{0:T(128)} %bitcast.3.core_ref, bf16[1024,1152]{1,0:T(8,128)(2,1)S(1)} %copy-done.5, bf16[8,264,128]{2,1,0:T(8,128)(2,1)S(1)} %all_to_all.36.own_ref, bf16[8,264,128]{2,1,0:T(8,128)(2,1)S(1)} %collective-permute-done.1.other_ref), custom_call_target="tpu_custom_call" | custom-call | flops 2147483648 | bytes 5605380 | tf_op jit(solution)/shard_map/second_sums/pallas_call | solution.py:51
  141.3 3.7 %all-to-all-start.3 = ((bf16[4,8,136,128]{3,2,1,0:T(8,128)(2,1)}), bf16[4,8,136,128]{3,2,1,0:T(8,128)(2,1)S(1)}, u32[]{:S(2)}, u32[]{:S(2)}) async-start(bf16[4,8,136,128]{3,2,1,0:T(8,128)(2,1)} %get-tuple-element.28), calls=%async_computation.3 | async-start | bytes 2228224 | tf_op jit(solution)/shard_map/all_to_all | solution.py:24
  145.0 0.3 multiply_reduce_fusion
  145.3 1.7 copy-done.6
  147.0 3.3 %margins_two.1.costs_ref = bf16[8,128]{1,0:T(8,128)(2,1)S(1)} custom-call(bf16[1024,1152]{1,0:T(8,128)(2,1)S(1)} %copy-done.6, bf16[512,1024]{1,0:T(8,128)(2,1)S(1)} %copy-done.3, bf16[512,1024]{1,0:T(8,128)(2,1)S(1)} %bitcast.18, f32[1,512]{1,0:T(1,128)S(1)} %bitcast.21), custom_call_target="tpu_custom_call" | custom-call | flops 2147483648 | bytes 4460544 | tf_op jit(solution)/shard_map/margins_two/pallas_call | solution.py:51
  150.3 11.0 %all-to-all-done.3 = bf16[4,8,136,128]{3,2,1,0:T(8,128)(2,1)S(1)} async-done(((bf16[4,8,136,128]{3,2,1,0:T(8,128)(2,1)}), bf16[4,8,136,128]{3,2,1,0:T(8,128)(2,1)S(1)}, u32[]{:S(2)}, u32[]{:S(2)}) %all-to-all-start.3) | async-done | bytes 1114144 | tf_op jit(solution)/shard_map/all_to_all | solution.py:24
  161.3 0.2 reduce_sum.32
  161.5 16.0 %all_to_all.37.arrived_ref = bf16[8,136,128]{2,1,0:T(8,128)(2,1)S(1)} all-to-all(bf16[8,136,128]{2,1,0:T(8,128)(2,1)S(1)} %reduce_sum.32), channel_id=1, replica_groups=mesh['z'=8,'x'=4,'y'=8,'core'=2] {'z'}, dimensions={0} | all-to-all | bytes 557056 | tf_op jit(solution)/shard_map/all_to_all | solution.py:24
  177.6 0.1 merge.3
  177.7 13.2 %all_to_all.38 = bf16[8,136,128]{2,1,0:T(8,128)(2,1)S(1)} all-to-all(bf16[8,136,128]{2,1,0:T(8,128)(2,1)S(1)} %merge.3), channel_id=1, replica_groups=mesh['z'=8,'x'=4,'y'=8,'core'=2] {'z'}, dimensions={0} | all-to-all | bytes 557056 | tf_op jit(solution)/shard_map/all_to_all | solution.py:24
  190.8 0.1 broadcast_in_dim.33
  191.0 15.5 %all_to_all.39.full_ref = bf16[4,8,136,128]{3,2,1,0:T(8,128)(2,1)S(1)} all-to-all(bf16[4,8,136,128]{3,2,1,0:T(8,128)(2,1)S(1)} %broadcast_in_dim.33), channel_id=1, replica_groups=mesh['z'=8,'x'=4,'y'=8,'core'=2] {'x'}, dimensions={0} | all-to-all | bytes 2228224 | tf_op jit(solution)/shard_map/all_to_all | solution.py:24
  206.5 1.2 last.1
  (11 shorter events, 0.0 us)
Async XLA Ops:
  1.4 1.2 copy-start.2
  83.2 13.9 %copy-start = (bf16[1,512,1024]{2,1,0:T(8,128)(2,1)S(1)}, bf16[1,512,1024]{2,1,0:T(8,128)(2,1)}, u32[]{:S(2)}) copy-start(bf16[1,512,1024]{2,1,0:T(8,128)(2,1)} %param.10) | copy-start | bytes 3145732
  83.2 5.5 %collective-permute-start = (bf16[8,264,128]{2,1,0:T(8,128)(2,1)S(1)}, bf16[8,264,128]{2,1,0:T(8,128)(2,1)S(1)}, u32[]{:S(2)}, u32[]{:S(2)}) collective-permute-start(bf16[8,264,128]{2,1,0:T(8,128)(2,1)S(1)} %get-tuple-element.24), channel_id=1, source_target_pairs={{0,1},{1,0},{2,3},{3,2},{4,5},{5,4},{6,7},{7,6},{8,9},{9,8},{10,11... | collective-permute-start | bytes 1622024 | tf_op jit(solution)/shard_map/ppermute | solution.py:360
  89.6 21.9 %all-to-all-start.1 = ((bf16[8,264,128]{2,1,0:T(8,128)(2,1)}), bf16[8,264,128]{2,1,0:T(8,128)(2,1)}, u32[]{:S(2)}, u32[]{:S(2)}) async-start(bf16[8,264,128]{2,1,0:T(8,128)(2,1)} %add_convert_fusion), calls=%async_computation.1 | async-start | bytes 1081344 | tf_op jit(solution)/shard_map/all_to_all | solution.py:30
  99.9 1.4 copy-start.4
  111.5 25.8 %copy-start.5 = (bf16[1024,1152]{1,0:T(8,128)(2,1)S(1)}, bf16[1024,1152]{1,0:T(8,128)(2,1)}, u32[]{:S(2)}) copy-start(bf16[1024,1152]{1,0:T(8,128)(2,1)} %copy-done.4) | copy-start | bytes 7077892
  133.5 3.8 %collective-permute-start.1 = (bf16[8,264,128]{2,1,0:T(8,128)(2,1)S(1)}, bf16[8,264,128]{2,1,0:T(8,128)(2,1)S(1)}, u32[]{:S(2)}, u32[]{:S(2)}) collective-permute-start(bf16[8,264,128]{2,1,0:T(8,128)(2,1)S(1)} %all_to_all.36.own_ref), channel_id=1, source_target_pairs={{0,1},{1,0},{2,3},{3,2},{4,5},{5,4},{6,7},{7,6},{8,9},{9,8},{10,11... | collective-permute-start | bytes 1622024 | tf_op jit(solution)/shard_map/ppermute | solution.py:365
  141.3 3.7 %copy-start.1 = (bf16[1,512,1024]{2,1,0:T(8,128)(2,1)S(1)}, bf16[1,512,1024]{2,1,0:T(8,128)(2,1)}, u32[]{:S(2)}) copy-start(bf16[1,512,1024]{2,1,0:T(8,128)(2,1)} %param.11) | copy-start | bytes 3145732
  141.3 4.0 %copy-start.3 = (bf16[512,1024]{1,0:T(8,128)(2,1)S(1)}, bf16[512,1024]{1,0:T(8,128)(2,1)}, u32[]{:S(2)}) copy-start(bf16[512,1024]{1,0:T(8,128)(2,1)} %get-tuple-element.26.centers_ref) | copy-start | bytes 3145732
  141.3 20.0 %all-to-all-start.3 = ((bf16[4,8,136,128]{3,2,1,0:T(8,128)(2,1)}), bf16[4,8,136,128]{3,2,1,0:T(8,128)(2,1)S(1)}, u32[]{:S(2)}, u32[]{:S(2)}) async-start(bf16[4,8,136,128]{3,2,1,0:T(8,128)(2,1)} %get-tuple-element.28), calls=%async_computation.3 | async-start | bytes 2228224 | tf_op jit(solution)/shard_map/all_to_all | solution.py:24
  145.3 1.7 copy-start.6

commit v9 on v7

--- a/solution.py
+++ b/solution.py
@@ -12,7 +12,7 @@
 SWAP = [(0, 1), (1, 0)]
 SLOTS = 2
 LANES = 128
-EXTRA = 8
+EXTRA = 16
 PIECES = 2
 VMEM_BYTES = 32 * 2**20
 DIGIT = 16

time: 207 us -> 210 us (1.014)
  blocking collectives: 145 us -> 148 us
where the time goes in v9:
time: 210 us; the launch traced here: 209 us
  blocking collectives  148 us (70%)
  waiting for transfers between devices  20.5 us (10%)
  starting transfers between devices  17.3 us (8%)
  Pallas kernels  15.6 us (7%)
  local copies, waits for them, and re-layouts  5.21 us (2%)
  other arithmetic  2.45 us (1%)
    all_to_all x4, blocking collectives, exchange(): return lax.all_to_all(blocks, axes, split_axis=0, concat_axis=0, tiled=True)  127 us
    all_to_all x1, blocking collectives, mirrored(): lax.all_to_all(blocks, GROUP, split_axis=0, concat_axis=0, tiled=True, ax...  20.9 us
    pallas_call x8, Pallas kernels, kernel_call(): pl.pallas_call(body, name=name, in_specs=specs, out_specs=[pl.BlockSpec(m...  15.6 us
    all_to_all x1, waiting for transfers between devices, mirrored(): lax.all_to_all(blocks, GROUP, split_axis=0, concat_axis=0, tiled=True, ax...  10.5 us
    all_to_all x1, starting transfers between devices, mirrored(): lax.all_to_all(blocks, GROUP, split_axis=0, concat_axis=0, tiled=True, ax...  7.45 us
    all_to_all x1, waiting for transfers between devices, exchange(): return lax.all_to_all(blocks, axes, split_axis=0, concat_axis=0, tiled=True)  6.77 us
    unnamed x14, local copies, waits for them, and re-layouts  4.32 us
  transfers between devices with their start and end apart: 4, of which 4 were waited for; matrix products, arithmetic and copies ran while one was open for 0% of the time, Pallas kernels for 3%

profile of v9, /device:TPU:56, one launch (start us, length us, event | category | flops | bytes accessed | tf_op | source)
XLA Modules:
  0.0 209.5 jit_solution(13873274448457822810)
XLA Ops:
  0.7 0.7 stack.15.info_ref
  1.4 0.0 copy-start.2
  1.4 1.2 copy-done.2
  2.6 2.0 place.1
  4.7 76.9 %all_to_all.35.arrived_ref = bf16[512,2,1152]{2,1,0:T(2,128)(2,1)S(1)} all-to-all(bf16[512,2,1152]{2,1,0:T(2,128)(2,1)S(1)} %place.1), channel_id=1, replica_groups=mesh['z'=8,'x'=4,'y'=8,'core'=2] {'z','x','y','core'}, dimensions={0} | all-to-all | bytes 4718592 | tf_op jit(solution)/shard_map/all_to_all | solution.py:24
  81.6 1.6 first_sums.1
  83.2 0.0 copy-start
  83.2 3.9 %collective-permute-start = (bf16[8,272,128]{2,1,0:T(8,128)(2,1)S(1)}, bf16[8,272,128]{2,1,0:T(8,128)(2,1)S(1)}, u32[]{:S(2)}, u32[]{:S(2)}) collective-permute-start(bf16[8,272,128]{2,1,0:T(8,128)(2,1)S(1)} %get-tuple-element.22), channel_id=1, source_target_pairs={{0,1},{1,0},{2,3},{3,2},{4,5},{5,4},{6,7},{7,6},{8,9},{9,8},{10,11... | collective-permute-start | bytes 1671176 | tf_op jit(solution)/shard_map/ppermute | solution.py:360
  87.1 1.6 collective-permute-done
  88.7 0.9 add_convert_fusion
  89.6 7.4 %all-to-all-start.1 = ((bf16[8,272,128]{2,1,0:T(8,128)(2,1)}), bf16[8,272,128]{2,1,0:T(8,128)(2,1)}, u32[]{:S(2)}, u32[]{:S(2)}) async-start(bf16[8,272,128]{2,1,0:T(8,128)(2,1)} %add_convert_fusion), calls=%async_computation.1 | async-start | bytes 1114112 | tf_op jit(solution)/shard_map/all_to_all | solution.py:30
  97.1 0.3 multiply_reduce_fusion.1
  97.3 2.6 %margins_one.1 = (bf16[16,128]{1,0:T(8,128)(2,1)S(1)}, bf16[1024,1152]{1,0:T(8,128)(2,1)S(1)}) custom-call(bf16[512,2,1152]{2,1,0:T(2,128)(2,1)S(1)} %all_to_all.35.arrived_ref, bf16[512,1024]{1,0:T(8,128)(2,1)S(1)} %bitcast.16, f32[1,512]{1,0:T(1,128)S(1)} %bitcast.20), custom_call_target="tpu_custom_call" | custom-call | flops 1073741824 | bytes 5773312 | tf_op jit(solution)/shard_map/margins_one/pallas_call | solution.py:51
  100.0 1.4 copy-done.4
  101.4 10.5 %all-to-all-done.1.arrived_ref = bf16[8,272,128]{2,1,0:T(8,128)(2,1)} async-done(((bf16[8,272,128]{2,1,0:T(8,128)(2,1)}), bf16[8,272,128]{2,1,0:T(8,128)(2,1)}, u32[]{:S(2)}, u32[]{:S(2)}) %all-to-all-start.1) | async-done | bytes 557088 | tf_op jit(solution)/shard_map/all_to_all | solution.py:30
  111.9 1.3 merge.2
  113.2 20.9 %all_to_all.36.own_ref = bf16[8,272,128]{2,1,0:T(8,128)(2,1)S(1)} all-to-all(bf16[8,272,128]{2,1,0:T(8,128)(2,1)S(1)} %merge.2), channel_id=1, replica_groups={{0,2,4,6,8,10,12,14},{15,13,11,9,7,5,3,1},{16,18,20,22,24,26,28,30},{31..., dimensions={0} | all-to-all | bytes 1114112 | tf_op jit(solution)/shard_map/all_to_all | solution.py:30
  134.1 2.1 collective-permute-start.1
  136.2 1.7 collective-permute-done.1.other_ref
  138.0 3.5 %second_sums.1 = (bf16[512,1024]{1,0:T(8,128)(2,1)}, f32[4,128]{1,0:T(4,128)}, bf16[4,8,144,128]{3,2,1,0:T(8,128)(2,1)S(1)}) custom-call(s32[1]{0:T(128)} %bitcast.3.core_ref, bf16[1024,1152]{1,0:T(8,128)(2,1)S(1)} %copy-done.5, bf16[8,272,128]{2,1,0:T(8,128)(2,1)S(1)} %all_to_all.36.own_ref, bf16[8,272,128]{2,1,0:T(8,128)(2,1)S(1)} %collective-permute-done.1.other_ref), custom_call_target="tpu_custom_call" | custom-call | flops 2147483648 | bytes 5703684 | tf_op jit(solution)/shard_map/second_sums/pallas_call | solution.py:51
  141.5 20.4 %all_to_all.37 = bf16[4,8,144,128]{3,2,1,0:T(8,128)(2,1)S(1)} all-to-all(bf16[4,8,144,128]{3,2,1,0:T(8,128)(2,1)S(1)} %get-tuple-element.26), channel_id=1, replica_groups=mesh['z'=8,'x'=4,'y'=8,'core'=2] {'x'}, dimensions={0} | all-to-all | bytes 2359296 | tf_op jit(solution)/shard_map/all_to_all | solution.py:24
  161.8 0.9 reduce_sum.31
  162.8 3.9 %all-to-all-start.4 = ((bf16[8,144,128]{2,1,0:T(8,128)(2,1)}), bf16[8,144,128]{2,1,0:T(8,128)(2,1)S(1)}, u32[]{:S(2)}, u32[]{:S(2)}) async-start(bf16[8,144,128]{2,1,0:T(8,128)(2,1)} %reduce_sum.31), calls=%async_computation.4 | async-start | bytes 589824 | tf_op jit(solution)/shard_map/all_to_all | solution.py:24
  166.6 0.3 multiply_reduce_fusion
  166.9 1.7 copy-done.6
  168.6 3.3 %margins_two.1.costs_ref = bf16[16,128]{1,0:T(8,128)(2,1)S(1)} custom-call(bf16[1024,1152]{1,0:T(8,128)(2,1)S(1)} %copy-done.6, bf16[512,1024]{1,0:T(8,128)(2,1)S(1)} %copy-done.3, bf16[512,1024]{1,0:T(8,128)(2,1)S(1)} %bitcast.18, f32[1,512]{1,0:T(1,128)S(1)} %bitcast.21), custom_call_target="tpu_custom_call" | custom-call | flops 2147483648 | bytes 4462592 | tf_op jit(solution)/shard_map/margins_two/pallas_call | solution.py:51
  171.9 6.8 %all-to-all-done.4.arrived_ref = bf16[8,144,128]{2,1,0:T(8,128)(2,1)S(1)} async-done(((bf16[8,144,128]{2,1,0:T(8,128)(2,1)}), bf16[8,144,128]{2,1,0:T(8,128)(2,1)S(1)}, u32[]{:S(2)}, u32[]{:S(2)}) %all-to-all-start.4) | async-done | bytes 294944 | tf_op jit(solution)/shard_map/all_to_all | solution.py:24
  178.6 0.1 merge.3
  178.8 13.3 %all_to_all.38 = bf16[8,144,128]{2,1,0:T(8,128)(2,1)S(1)} all-to-all(bf16[8,144,128]{2,1,0:T(8,128)(2,1)S(1)} %merge.3), channel_id=1, replica_groups=mesh['z'=8,'x'=4,'y'=8,'core'=2] {'z'}, dimensions={0} | all-to-all | bytes 589824 | tf_op jit(solution)/shard_map/all_to_all | solution.py:24
  192.1 0.2 broadcast_in_dim.33
  192.2 16.1 %all_to_all.39.full_ref = bf16[4,8,144,128]{3,2,1,0:T(8,128)(2,1)S(1)} all-to-all(bf16[4,8,144,128]{3,2,1,0:T(8,128)(2,1)S(1)} %broadcast_in_dim.33), channel_id=1, replica_groups=mesh['z'=8,'x'=4,'y'=8,'core'=2] {'x'}, dimensions={0} | all-to-all | bytes 2359296 | tf_op jit(solution)/shard_map/all_to_all | solution.py:24
  208.3 1.2 last.1
  (11 shorter events, 0.0 us)
Async XLA Ops:
  1.4 1.2 copy-start.2
  83.2 13.9 %copy-start = (bf16[1,512,1024]{2,1,0:T(8,128)(2,1)S(1)}, bf16[1,512,1024]{2,1,0:T(8,128)(2,1)}, u32[]{:S(2)}) copy-start(bf16[1,512,1024]{2,1,0:T(8,128)(2,1)} %param.10) | copy-start | bytes 3145732
  83.2 5.5 %collective-permute-start = (bf16[8,272,128]{2,1,0:T(8,128)(2,1)S(1)}, bf16[8,272,128]{2,1,0:T(8,128)(2,1)S(1)}, u32[]{:S(2)}, u32[]{:S(2)}) collective-permute-start(bf16[8,272,128]{2,1,0:T(8,128)(2,1)S(1)} %get-tuple-element.22), channel_id=1, source_target_pairs={{0,1},{1,0},{2,3},{3,2},{4,5},{5,4},{6,7},{7,6},{8,9},{9,8},{10,11... | collective-permute-start | bytes 1671176 | tf_op jit(solution)/shard_map/ppermute | solution.py:360
  89.6 22.2 %all-to-all-start.1 = ((bf16[8,272,128]{2,1,0:T(8,128)(2,1)}), bf16[8,272,128]{2,1,0:T(8,128)(2,1)}, u32[]{:S(2)}, u32[]{:S(2)}) async-start(bf16[8,272,128]{2,1,0:T(8,128)(2,1)} %add_convert_fusion), calls=%async_computation.1 | async-start | bytes 1114112 | tf_op jit(solution)/shard_map/all_to_all | solution.py:30
  100.0 1.4 copy-start.4
  111.9 26.1 %copy-start.5 = (bf16[1024,1152]{1,0:T(8,128)(2,1)S(1)}, bf16[1024,1152]{1,0:T(8,128)(2,1)}, u32[]{:S(2)}) copy-start(bf16[1024,1152]{1,0:T(8,128)(2,1)} %copy-done.4) | copy-start | bytes 7077892
  134.1 3.8 %collective-permute-start.1 = (bf16[8,272,128]{2,1,0:T(8,128)(2,1)S(1)}, bf16[8,272,128]{2,1,0:T(8,128)(2,1)S(1)}, u32[]{:S(2)}, u32[]{:S(2)}) collective-permute-start(bf16[8,272,128]{2,1,0:T(8,128)(2,1)S(1)} %all_to_all.36.own_ref), channel_id=1, source_target_pairs={{0,1},{1,0},{2,3},{3,2},{4,5},{5,4},{6,7},{7,6},{8,9},{9,8},{10,11... | collective-permute-start | bytes 1671176 | tf_op jit(solution)/shard_map/ppermute | solution.py:365
  141.5 25.2 %copy-start.1 = (bf16[1,512,1024]{2,1,0:T(8,128)(2,1)S(1)}, bf16[1,512,1024]{2,1,0:T(8,128)(2,1)}, u32[]{:S(2)}) copy-start(bf16[1,512,1024]{2,1,0:T(8,128)(2,1)} %param.11) | copy-start | bytes 3145732
  161.8 5.1 %copy-start.3 = (bf16[512,1024]{1,0:T(8,128)(2,1)S(1)}, bf16[512,1024]{1,0:T(8,128)(2,1)}, u32[]{:S(2)}) copy-start(bf16[512,1024]{1,0:T(8,128)(2,1)} %get-tuple-element.24.centers_ref) | copy-start | bytes 3145732
  162.8 15.9 %all-to-all-start.4 = ((bf16[8,144,128]{2,1,0:T(8,128)(2,1)}), bf16[8,144,128]{2,1,0:T(8,128)(2,1)S(1)}, u32[]{:S(2)}, u32[]{:S(2)}) async-start(bf16[8,144,128]{2,1,0:T(8,128)(2,1)} %reduce_sum.31), calls=%async_computation.4 | async-start | bytes 589824 | tf_op jit(solution)/shard_map/all_to_all | solution.py:24
  166.9 1.7 copy-start.6

commit v10 on v7

--- a/solution.py
+++ b/solution.py
@@ -366,8 +366,7 @@
 
     nx, nz = lax.axis_size("x"), lax.axis_size("z")
     coarse_new, coarse_cost, partial_two = second_sums(core, rows, own, other, children, nx, nz)
-    parts_two = jnp.sum(exchange(partial_two, "x").astype(F32), axis=0).astype(BF16)
-    parts_two = exchange(parts_two, "z")
+    parts_two = exchange(partial_two.reshape((n_shard,) + partial_two.shape[2:]), ("x", "z"))
     costs_two = margins_two(rows, coarse_new, fine, squares_of(fine))
     copies_two = exchange(merge(shard, parts_two, fine, costs_two, nz), "z")
     full_two = jnp.broadcast_to(copies_two[None], (nx,) + copies_two.shape)

time: 207 us -> 211 us (1.019)
  waiting for transfers between devices: 19.5 us -> 38.4 us
  blocking collectives: 145 us -> 129 us
    all_to_all x1, waiting for transfers between devices: 6.1 us -> 25 us  [exchange(): return lax.all_to_all(blocks, axes, split_axis=0, concat_axis=0, tiled=True)]
    all_to_all x4 -> x3, blocking collectives: 125 us -> 108 us  [exchange(): return lax.all_to_all(blocks, axes, split_axis=0, concat_axis=0, tiled=True)]
where the time goes in v10:
time: 211 us
  blocking collectives  129 us (61%)
  waiting for transfers between devices  38.4 us (18%)
  starting transfers between devices  19.4 us (9%)
  Pallas kernels  16.3 us (8%)
  local copies, waits for them, and re-layouts  5.18 us (2%)
    all_to_all x3, blocking collectives, exchange(): return lax.all_to_all(blocks, axes, split_axis=0, concat_axis=0, tiled=True)  108 us
    all_to_all x1, waiting for transfers between devices, exchange(): return lax.all_to_all(blocks, axes, split_axis=0, concat_axis=0, tiled=True)  25 us
    all_to_all x1, blocking collectives, mirrored(): lax.all_to_all(blocks, GROUP, split_axis=0, concat_axis=0, tiled=True, ax...  20.6 us
    pallas_call x8, Pallas kernels, kernel_call(): pl.pallas_call(body, name=name, in_specs=specs, out_specs=[pl.BlockSpec(m...  16.3 us
    all_to_all x1, waiting for transfers between devices, mirrored(): lax.all_to_all(blocks, GROUP, split_axis=0, concat_axis=0, tiled=True, ax...  10.2 us
    all_to_all x1, starting transfers between devices, mirrored(): lax.all_to_all(blocks, GROUP, split_axis=0, concat_axis=0, tiled=True, ax...  7.44 us
    all_to_all x1, starting transfers between devices, exchange(): return lax.all_to_all(blocks, axes, split_axis=0, concat_axis=0, tiled=True)  5.91 us
    unnamed x14, local copies, waits for them, and re-layouts  4.29 us
  transfers between devices with their start and end apart: 4, of which 4 were waited for; matrix products, arithmetic and copies ran while one was open for 0% of the time, Pallas kernels for 3%

profile of v10, /device:TPU:56, one launch (start us, length us, event | category | flops | bytes accessed | tf_op | source)
XLA Modules:
  0.0 210.6 jit_solution(7185859675382527891)
XLA Ops:
  0.7 0.7 stack.15.info_ref
  1.4 0.0 copy-start.2
  1.4 1.2 copy-done.2
  2.6 2.0 place.1
  4.7 76.9 %all_to_all.30.arrived_ref = bf16[512,2,1152]{2,1,0:T(2,128)(2,1)S(1)} all-to-all(bf16[512,2,1152]{2,1,0:T(2,128)(2,1)S(1)} %place.1), channel_id=1, replica_groups=mesh['z'=8,'x'=4,'y'=8,'core'=2] {'z','x','y','core'}, dimensions={0} | all-to-all | bytes 4718592 | tf_op jit(solution)/shard_map/all_to_all | solution.py:24
  81.6 1.6 first_sums.1
  83.2 3.9 %collective-permute-start = (bf16[8,264,128]{2,1,0:T(8,128)(2,1)S(1)}, bf16[8,264,128]{2,1,0:T(8,128)(2,1)S(1)}, u32[]{:S(2)}, u32[]{:S(2)}) collective-permute-start(bf16[8,264,128]{2,1,0:T(8,128)(2,1)S(1)} %get-tuple-element.22), channel_id=1, source_target_pairs={{0,1},{1,0},{2,3},{3,2},{4,5},{5,4},{6,7},{7,6},{8,9},{9,8},{10,11... | collective-permute-start | bytes 1622024 | tf_op jit(solution)/shard_map/ppermute | solution.py:360
  87.1 1.5 collective-permute-done
  88.6 0.9 add_convert_fusion
  89.6 7.4 %all-to-all-start.1 = ((bf16[8,264,128]{2,1,0:T(8,128)(2,1)}), bf16[8,264,128]{2,1,0:T(8,128)(2,1)}, u32[]{:S(2)}, u32[]{:S(2)}) async-start(bf16[8,264,128]{2,1,0:T(8,128)(2,1)} %add_convert_fusion), calls=%async_computation.1 | async-start | bytes 1081344 | tf_op jit(solution)/shard_map/all_to_all | solution.py:30
  97.0 0.0 copy-done
  97.0 0.3 multiply_reduce_fusion.1
  97.3 2.6 %margins_one.1 = (bf16[8,128]{1,0:T(8,128)(2,1)S(1)}, bf16[1024,1152]{1,0:T(8,128)(2,1)S(1)}) custom-call(bf16[512,2,1152]{2,1,0:T(2,128)(2,1)S(1)} %all_to_all.30.arrived_ref, bf16[512,1024]{1,0:T(8,128)(2,1)S(1)} %bitcast.17, f32[1,512]{1,0:T(1,128)S(1)} %bitcast.21), custom_call_target="tpu_custom_call" | custom-call | flops 1073741824 | bytes 5771264 | tf_op jit(solution)/shard_map/margins_one/pallas_call | solution.py:51
  99.9 0.0 copy-start.4
  99.9 1.4 copy-done.4
  101.3 10.2 %all-to-all-done.1.arrived_ref = bf16[8,264,128]{2,1,0:T(8,128)(2,1)} async-done(((bf16[8,264,128]{2,1,0:T(8,128)(2,1)}), bf16[8,264,128]{2,1,0:T(8,128)(2,1)}, u32[]{:S(2)}, u32[]{:S(2)}) %all-to-all-start.1) | async-done | bytes 540704 | tf_op jit(solution)/shard_map/all_to_all | solution.py:30
  111.5 1.3 merge.2
  112.8 20.6 %all_to_all.31.own_ref = bf16[8,264,128]{2,1,0:T(8,128)(2,1)S(1)} all-to-all(bf16[8,264,128]{2,1,0:T(8,128)(2,1)S(1)} %merge.2), channel_id=1, replica_groups={{0,2,4,6,8,10,12,14},{15,13,11,9,7,5,3,1},{16,18,20,22,24,26,28,30},{31..., dimensions={0} | all-to-all | bytes 1081344 | tf_op jit(solution)/shard_map/all_to_all | solution.py:30
  133.5 2.1 collective-permute-start.1
  135.6 1.7 collective-permute-done.1.other_ref
  137.3 0.0 copy-done.5
  137.3 4.0 %second_sums.1 = (bf16[512,1024]{1,0:T(8,128)(2,1)}, f32[4,128]{1,0:T(4,128)}, bf16[4,8,136,128]{3,2,1,0:T(8,128)(2,1)}) custom-call(s32[1]{0:T(128)} %bitcast.3.core_ref, bf16[1024,1152]{1,0:T(8,128)(2,1)S(1)} %copy-done.5, bf16[8,264,128]{2,1,0:T(8,128)(2,1)S(1)} %all_to_all.31.own_ref, bf16[8,264,128]{2,1,0:T(8,128)(2,1)S(1)} %collective-permute-done.1.other_ref), custom_call_target="tpu_custom_call" | custom-call | flops 2147483648 | bytes 5605380 | tf_op jit(solution)/shard_map/second_sums/pallas_call | solution.py:51
  141.4 5.9 %all-to-all-start.3 = ((bf16[32,136,128]{2,1,0:T(8,128)(2,1)}), bf16[32,136,128]{2,1,0:T(8,128)(2,1)S(1)}, u32[]{:S(2)}, u32[]{:S(2)}) async-start(bf16[32,136,128]{2,1,0:T(8,128)(2,1)} %bitcast.9), calls=%async_computation.3 | async-start | bytes 2228224 | tf_op jit(solution)/shard_map/all_to_all | solution.py:24
  147.3 0.3 multiply_reduce_fusion
  147.6 1.7 copy-done.6
  149.2 3.3 %margins_two.1.costs_ref = bf16[8,128]{1,0:T(8,128)(2,1)S(1)} custom-call(bf16[1024,1152]{1,0:T(8,128)(2,1)S(1)} %copy-done.6, bf16[512,1024]{1,0:T(8,128)(2,1)S(1)} %copy-done.3, bf16[512,1024]{1,0:T(8,128)(2,1)S(1)} %bitcast.19, f32[1,512]{1,0:T(1,128)S(1)} %bitcast.22), custom_call_target="tpu_custom_call" | custom-call | flops 2147483648 | bytes 4460544 | tf_op jit(solution)/shard_map/margins_two/pallas_call | solution.py:51
  152.6 25.0 %all-to-all-done.3.arrived_ref = bf16[32,136,128]{2,1,0:T(8,128)(2,1)S(1)} async-done(((bf16[32,136,128]{2,1,0:T(8,128)(2,1)}), bf16[32,136,128]{2,1,0:T(8,128)(2,1)S(1)}, u32[]{:S(2)}, u32[]{:S(2)}) %all-to-all-start.3) | async-done | bytes 1114144 | tf_op jit(solution)/shard_map/all_to_all | solution.py:24
  177.5 0.2 merge.3
  177.8 14.2 %all_to_all.32 = bf16[8,136,128]{2,1,0:T(8,128)(2,1)S(1)} all-to-all(bf16[8,136,128]{2,1,0:T(8,128)(2,1)S(1)} %merge.3), channel_id=1, replica_groups=mesh['z'=8,'x'=4,'y'=8,'core'=2] {'z'}, dimensions={0} | all-to-all | bytes 557056 | tf_op jit(solution)/shard_map/all_to_all | solution.py:24
  192.0 0.1 broadcast_in_dim.33
  192.1 17.3 %all_to_all.33.full_ref = bf16[4,8,136,128]{3,2,1,0:T(8,128)(2,1)S(1)} all-to-all(bf16[4,8,136,128]{3,2,1,0:T(8,128)(2,1)S(1)} %broadcast_in_dim.33), channel_id=1, replica_groups=mesh['z'=8,'x'=4,'y'=8,'core'=2] {'x'}, dimensions={0} | all-to-all | bytes 2228224 | tf_op jit(solution)/shard_map/all_to_all | solution.py:24
  209.4 1.2 last.1
  (9 shorter events, 0.0 us)
Async XLA Ops:
  1.4 1.2 copy-start.2
  83.2 13.9 %copy-start = (bf16[1,512,1024]{2,1,0:T(8,128)(2,1)S(1)}, bf16[1,512,1024]{2,1,0:T(8,128)(2,1)}, u32[]{:S(2)}) copy-start(bf16[1,512,1024]{2,1,0:T(8,128)(2,1)} %param.10) | copy-start | bytes 3145732
  83.2 5.5 %collective-permute-start = (bf16[8,264,128]{2,1,0:T(8,128)(2,1)S(1)}, bf16[8,264,128]{2,1,0:T(8,128)(2,1)S(1)}, u32[]{:S(2)}, u32[]{:S(2)}) collective-permute-start(bf16[8,264,128]{2,1,0:T(8,128)(2,1)S(1)} %get-tuple-element.22), channel_id=1, source_target_pairs={{0,1},{1,0},{2,3},{3,2},{4,5},{5,4},{6,7},{7,6},{8,9},{9,8},{10,11... | collective-permute-start | bytes 1622024 | tf_op jit(solution)/shard_map/ppermute | solution.py:360
  89.6 21.9 %all-to-all-start.1 = ((bf16[8,264,128]{2,1,0:T(8,128)(2,1)}), bf16[8,264,128]{2,1,0:T(8,128)(2,1)}, u32[]{:S(2)}, u32[]{:S(2)}) async-start(bf16[8,264,128]{2,1,0:T(8,128)(2,1)} %add_convert_fusion), calls=%async_computation.1 | async-start | bytes 1081344 | tf_op jit(solution)/shard_map/all_to_all | solution.py:30
  99.9 1.4 copy-start.4
  111.5 25.8 %copy-start.5 = (bf16[1024,1152]{1,0:T(8,128)(2,1)S(1)}, bf16[1024,1152]{1,0:T(8,128)(2,1)}, u32[]{:S(2)}) copy-start(bf16[1024,1152]{1,0:T(8,128)(2,1)} %copy-done.4) | copy-start | bytes 7077892
  133.5 3.8 %collective-permute-start.1 = (bf16[8,264,128]{2,1,0:T(8,128)(2,1)S(1)}, bf16[8,264,128]{2,1,0:T(8,128)(2,1)S(1)}, u32[]{:S(2)}, u32[]{:S(2)}) collective-permute-start(bf16[8,264,128]{2,1,0:T(8,128)(2,1)S(1)} %all_to_all.31.own_ref), channel_id=1, source_target_pairs={{0,1},{1,0},{2,3},{3,2},{4,5},{5,4},{6,7},{7,6},{8,9},{9,8},{10,11... | collective-permute-start | bytes 1622024 | tf_op jit(solution)/shard_map/ppermute | solution.py:365
  141.3 5.9 %copy-start.1 = (bf16[1,512,1024]{2,1,0:T(8,128)(2,1)S(1)}, bf16[1,512,1024]{2,1,0:T(8,128)(2,1)}, u32[]{:S(2)}) copy-start(bf16[1,512,1024]{2,1,0:T(8,128)(2,1)} %param.11) | copy-start | bytes 3145732
  141.3 6.2 %copy-start.3 = (bf16[512,1024]{1,0:T(8,128)(2,1)S(1)}, bf16[512,1024]{1,0:T(8,128)(2,1)}, u32[]{:S(2)}) copy-start(bf16[512,1024]{1,0:T(8,128)(2,1)} %get-tuple-element.24.centers_ref) | copy-start | bytes 3145732
  141.4 36.2 %all-to-all-start.3 = ((bf16[32,136,128]{2,1,0:T(8,128)(2,1)}), bf16[32,136,128]{2,1,0:T(8,128)(2,1)S(1)}, u32[]{:S(2)}, u32[]{:S(2)}) async-start(bf16[32,136,128]{2,1,0:T(8,128)(2,1)} %bitcast.9), calls=%async_computation.3 | async-start | bytes 2228224 | tf_op jit(solution)/shard_map/all_to_all | solution.py:24
  147.6 1.7 copy-start.6
